TPU v7x, 512 devices: a whole 4x8x8 slice. The times are simulated.
512 devices in a mesh: prompt: 8 (over y), dp: 4 (over x), expert: 16 (over z, core).
Axes of the slice: x: 4, y: 8, z: 8, core: 2. Of those that a mesh axis runs over, the one named last changes fastest.
Arguments:
- ssm_input: bfloat16 [65536, 4096], P(('prompt', 'dp', 'expert')), may hold values from -6 to 6
- b_inputs: bfloat16 [65536, 128], P(('prompt', 'dp', 'expert')), may hold values from -1.5 to 1.5
- c_readout: bfloat16 [65536, 128], P(('prompt', 'dp', 'expert')), may hold values from -1.5 to 1.5
- step_raw: float32 [65536, 64], P(('prompt', 'dp', 'expert')), may hold values from -4 to 4
- decay_rate: float32 [64], replicated, may hold values from 0.00234375 to 0.05
- skip_gain: float32 [64], replicated, may hold values from 0.25 to 1.75
- conv_weight: float32 [4, 4096], replicated, may hold values from -3 to 3
- prompt_state: bfloat16 [32, 64, 64, 128], P('expert', ('prompt', 'dp')), may hold values from -6 to 6
- prompt_taps: bfloat16 [32, 64, 192], P('expert', ('prompt', 'dp')), may hold values from -6 to 6
- group_index: int32 [512], P(('prompt', 'dp', 'expert')), may hold values from 0 to 1
- lengths: int32 [512], P(('prompt', 'dp', 'expert')), may hold values from 1 to 128
- mixed_grad: bfloat16 [65536, 4096], P(('prompt', 'dp', 'expert')), may hold values from -6 to 6
- expert_index: int32 [65536, 1], P(('prompt', 'dp', 'expert')), may hold values from 0 to 15; in each aligned block of 128 rows (0 to 127, 128 to 255, ...) at most 12 rows name the same one
- route_gain: float32 [65536, 1], P(('prompt', 'dp', 'expert')), may hold values from 0.1 to 1
- gate_weight: bfloat16 [16, 768, 4096], P('expert', ('prompt', 'dp')), may hold values from -0.09375 to 0.09375
- up_weight: bfloat16 [16, 768, 4096], P('expert', ('prompt', 'dp')), may hold values from -0.09375 to 0.09375
- down_weight: bfloat16 [16, 768, 4096], P('expert', ('prompt', 'dp')), may hold values from -0.21875 to 0.21875
Outputs:
- moe_out: bfloat16 [65536, 4096], P(('prompt', 'dp', 'expert'))
- state_grad: float32 [32, 64, 64, 128], P('expert', ('prompt', 'dp'))
- taps_grad: float32 [32, 64, 192], P('expert', ('prompt', 'dp'))
Inputs may be any that keep to these rules, and one draw needn't show every extreme that they name: `expert_index`: within each response's 128 tokens no expert is named more than 12 times, a bound that some block reaches.
All inputs are finite; a program needn't handle non-finite values.
Results may differ from a plain program's by a relative error of at most 0.019.
Values may be sent and summed in bfloat16 or wider, within the bound.
No kernel may reach another device: no remote copies, remote signals or barrier semaphores. Data moves between devices by JAX's collectives and lax.ppermute only.
A program may use at most 128 MiB of HBM per device.

v0:
```python
import jax
import jax.numpy as jnp
from jax import lax
from jax.sharding import PartitionSpec as P


def mixer(
    x_rows,
    b_rows,
    c_rows,
    step_raw,
    decay_rate,
    skip_gain,
    conv_weight,
    state_zero,
    taps_zero,
    length,
):
    steps_n, row_width = x_rows.shape
    head_count, head_size, state_n = state_zero.shape
    taps_n = taps_zero.shape[1] // head_size
    prior = jnp.transpose(taps_zero.reshape(head_count, taps_n, head_size), (1, 0, 2)).reshape(
        taps_n, row_width
    )
    series = jnp.concatenate([prior, x_rows.astype(jnp.float32)], 0)
    summed = conv_weight[taps_n] * series[taps_n:]
    for offset in range(taps_n):
        summed = summed + conv_weight[offset] * series[offset : offset + steps_n]
    conv_out = jax.nn.silu(summed).reshape(steps_n, head_count, head_size)
    step_size = jax.nn.softplus(step_raw)
    decay_sum = jnp.cumsum(-step_size * decay_rate[None, :], axis=0)
    scores = jnp.dot(c_rows, b_rows.T, preferred_element_type=jnp.float32)
    positions = lax.iota(jnp.int32, steps_n)
    causal = positions[:, None] >= positions[None, :]
    gaps = decay_sum.T[:, :, None] - decay_sum.T[:, None, :]
    factor = jnp.where(causal[None], jnp.exp(jnp.where(causal[None], gaps, -60.0)), 0.0)
    factor = factor * scores[None] * step_size.T[:, None, :]
    inner = jnp.einsum("hts,shp->thp", factor, conv_out, precision=lax.Precision.HIGHEST)
    carried = jnp.dot(
        c_rows.astype(jnp.float32),
        state_zero.reshape(head_count * head_size, state_n).T,
        precision=lax.Precision.HIGHEST,
    ).reshape(steps_n, head_count, head_size)
    output = inner + jnp.exp(decay_sum)[:, :, None] * carried + skip_gain[None, :, None] * conv_out
    live = (positions < length)[:, None, None]
    return jnp.where(live, output, 0.0).reshape(steps_n, row_width)


def expert_apply(rows, gate_w, up_w, down_w):
    dims = (((1,), (1,)), ((), ()))
    gate = lax.dot_general(rows, gate_w, dims, preferred_element_type=jnp.float32)
    upper = lax.dot_general(rows, up_w, dims, preferred_element_type=jnp.float32)
    hidden = (jax.nn.silu(gate) * upper).astype(jnp.bfloat16)
    return jnp.dot(hidden, down_w, preferred_element_type=jnp.float32)


def shards(
    ssm_input,
    b_inputs,
    c_readout,
    step_raw,
    decay_rate,
    skip_gain,
    conv_weight,
    prompt_state,
    prompt_taps,
    group_index,
    lengths,
    mixed_grad,
    expert_index,
    route_gain,
    gate_weight,
    up_weight,
    down_weight,
):
    steps_n, row_width = ssm_input.shape
    owned = prompt_state.shape[0]
    member = group_index[0]
    pieces = (
        lax.all_gather(prompt_state, ("prompt", "dp"), axis=1, tiled=True),
        lax.all_gather(prompt_taps, ("prompt", "dp"), axis=1, tiled=True),
    )
    state_piece = lax.dynamic_index_in_dim(pieces[0], member, 0, keepdims=False)
    taps_piece = lax.dynamic_index_in_dim(pieces[1], member, 0, keepdims=False)

    def forward(state_in, taps_in):
        return mixer(
            ssm_input,
            b_inputs,
            c_readout,
            step_raw,
            decay_rate,
            skip_gain,
            conv_weight,
            state_in,
            taps_in,
            lengths[0],
        )

    mixed, pull = jax.vjp(forward, state_piece.astype(jnp.float32), taps_piece.astype(jnp.float32))
    grad_s, grad_t = pull(mixed_grad.astype(jnp.float32))
    grad_s = lax.optimization_barrier(grad_s.astype(jnp.bfloat16)).astype(jnp.float32)
    grad_t = lax.optimization_barrier(grad_t.astype(jnp.bfloat16)).astype(jnp.float32)
    selected = lax.iota(jnp.int32, owned) == member
    term_state = jnp.where(selected[:, None, None, None], grad_s[None], 0.0)
    term_taps = jnp.where(selected[:, None, None], grad_t[None], 0.0)
    state_grad, taps_grad = (
        lax.psum_scatter(
            term_state.astype(jnp.bfloat16), ("prompt", "dp"), scatter_dimension=1, tiled=True
        ).astype(jnp.float32),
        lax.psum_scatter(
            term_taps.astype(jnp.bfloat16), ("prompt", "dp"), scatter_dimension=1, tiled=True
        ).astype(jnp.float32),
    )
    rows_in = mixed.astype(jnp.bfloat16)
    expert_count = lax.axis_size("expert")
    capacity = 3 * steps_n // (2 * expert_count)
    chosen = expert_index[:, 0]
    onehot = (chosen[:, None] == lax.iota(jnp.int32, expert_count)[None, :]).astype(jnp.int32)
    slot = jnp.sum((jnp.cumsum(onehot, axis=0) - onehot) * onehot, axis=1)
    target = chosen * capacity + slot
    placing = (lax.iota(jnp.int32, expert_count * capacity)[:, None] == target[None, :]).astype(
        jnp.bfloat16
    )
    outgoing = jnp.dot(placing, rows_in, preferred_element_type=jnp.float32).astype(jnp.bfloat16)
    arrived = lax.all_to_all(
        outgoing.reshape(expert_count, capacity, row_width),
        "expert",
        split_axis=0,
        concat_axis=0,
        tiled=True,
    )
    slot_rows = arrived.reshape(expert_count * capacity, row_width)
    pieces = (
        lax.all_gather(gate_weight, ("prompt", "dp"), axis=1, tiled=True),
        lax.all_gather(up_weight, ("prompt", "dp"), axis=1, tiled=True),
        lax.all_gather(down_weight, ("prompt", "dp"), axis=1, tiled=True),
    )
    produced = expert_apply(slot_rows, pieces[0][0], pieces[1][0], pieces[2][0])
    returned = lax.all_to_all(
        produced.astype(jnp.bfloat16).reshape(expert_count, capacity, row_width),
        "expert",
        split_axis=0,
        concat_axis=0,
        tiled=True,
    )
    flat_back = returned.reshape(expert_count * capacity, row_width)
    per_token = lax.dot_general(
        placing, flat_back, (((0,), (0,)), ((), ())), preferred_element_type=jnp.float32
    )
    moe_out = (route_gain * per_token).astype(jnp.bfloat16)
    return (moe_out, state_grad, taps_grad)


def solution(mesh):
    placed = (
        P(("prompt", "dp", "expert"), None),
        P(("prompt", "dp", "expert"), None),
        P(("prompt", "dp", "expert"), None),
        P(("prompt", "dp", "expert"), None),
        P(),
        P(),
        P(),
        P("expert", ("prompt", "dp"), None, None),
        P("expert", ("prompt", "dp"), None),
        P(("prompt", "dp", "expert")),
        P(("prompt", "dp", "expert")),
        P(("prompt", "dp", "expert"), None),
        P(("prompt", "dp", "expert"), None),
        P(("prompt", "dp", "expert"), None),
        P("expert", ("prompt", "dp"), None),
        P("expert", ("prompt", "dp"), None),
        P("expert", ("prompt", "dp"), None),
    )
    return jax.shard_map(
        shards,
        mesh=mesh,
        in_specs=placed,
        out_specs=(
            P(("prompt", "dp", "expert"), None),
            P("expert", ("prompt", "dp"), None, None),
            P("expert", ("prompt", "dp"), None),
        ),
        check_vma=False,
    )
```

profile of v0, /device:TPU:56, one launch (start us, length us, event | category | flops | bytes accessed | tf_op | source)
XLA Modules:
  0.0 580.2 jit_solution(7677808252604385388)
XLA Ops:
  7.2 0.0 all-gather.5.cloned.1.call-start
  7.2 0.7 all-gather.5.cloned.1.call-update
  7.9 0.0 all-gather.7.cloned.1.call-start
  8.0 0.7 all-gather.7.cloned.1.call-update
  8.7 0.0 all-gather.11.cloned.1.call-start
  8.7 0.7 all-gather.11.cloned.1.call-update
  9.4 0.0 all-gather.9.cloned.1.call-start
  9.5 0.5 all-gather.9.cloned.1.call-update
  10.0 0.8 negate_multiply_fusion
  10.8 0.1 copy.72
  10.9 0.2 reduce_window_sum.23
  11.1 0.1 copy.73
  11.9 1.6 copy.76
  13.6 0.1 fusion.73
  13.7 0.0 copy-done.13
  13.7 6.1 %bitcast_add_fusion = f32[128,64,64]{0,2,1:T(8,128)} fusion(f32[64,128]{1,0:T(8,128)S(1)} %get-tuple-element.14, f32[128,128]{1,0:T(8,128)S(1)} %fusion.73, f32[64,128]{1,0:T(8,128)S(1)} %copy.73, pred[128,128]{1,0:T(8,128)(4,1)S(1)} %iota_compare_fusion.3, f32[64]{0:T(128)S(1)} %copy-done.13, pred[128]{0:T(512)(128)(4,1)S(1)} %iota_compare_fusion.6, ...), kind=kOutput, calls=%fused_computation.30 | convolution fusion | flops 813694976 | bytes 3293568 | tf_op jit(solution)/shard_map/transpose(jvp(hts,shp->thp))/dot_general | solution.py:38
  19.8 1.9 copy.77
  22.5 50.8 %all_gather.15 = bf16[2,64,192]{2,0,1:T(2,128)(2,1)S(1)} all-gather(bf16[2,2,192]{2,0,1:T(2,128)(2,1)S(1)} %copy.68), channel_id=1, replica_groups=mesh['prompt'=8,'dp'=4,'expert'=16] {'prompt','dp'}, dimensions={1}, use_global_device_ids=true | all-gather | bytes 50688 | tf_op jit(solution)/shard_map/all_gather | solution.py:81
  73.3 0.1 constant_dynamic-slice_fusion
  73.4 0.1 copy.85
  73.5 0.1 copy.70
  73.6 0.1 reshape.109
  73.7 1.4 convert_element_type.67
  75.2 2.7 broadcast_multiply_fusion
  78.0 3.1 broadcast_multiply_fusion.1
  81.0 1.8 copy.71
  82.9 0.1 copy.75
  82.9 0.0 copy-done.8
  83.0 0.1 fusion.59
  83.0 0.2 reduce_window_sum.22
  83.2 0.2 select_reduce_fusion
  83.4 13.9 %all-gather.5.cloned.1.call-done = bf16[2,64,64,128]{3,2,1,0:T(8,128)(2,1)} async-done(((bf16[2,2,64,128]{3,2,1,0:T(8,128)(2,1)}), bf16[2,64,64,128]{3,2,1,0:T(8,128)(2,1)}) %all-gather.5.cloned.1.call-update) | async-done | bytes 2097168 | tf_op jit(solution)/shard_map/all_gather | solution.py:80
  97.3 1.3 constant_dynamic-slice_fusion.1
  98.6 0.4 fusion.74
  99.0 1.1 copy-done.1
  100.2 8.5 %fusion.25 = bf16[128,64,64]{0,2,1:T(8,128)(2,1)S(1)} fusion(f32[128,64,64]{0,2,1:T(8,128)S(1)} %bitcast.96, f32[128,64,64]{0,2,1:T(8,128)S(1)} %bitcast.95, f32[64,128]{1,0:T(8,128)S(1)} %get-tuple-element.14, f32[128,128]{1,0:T(8,128)S(1)} %copy-done.4, f32[64,128]{1,0:T(8,128)S(1)} %copy-done.6, pred[128,128]{1,0:T(8,128)(4,1)S(1)} %iota_compare_fusion.3, ...), kind=kOutput, calls=%fused_computation.36 | convolution fusion | flops 813694976 | bytes 5423488 | tf_op jit(solution)/shard_map/jvp(hts,shp->thp)/dot_general | solution.py:38
  108.7 1.7 convolution_convert_fusion
  110.4 2.3 reshape.102
  112.7 57.1 %all_to_all.10 = bf16[16,12,4096]{2,1,0:T(8,128)(2,1)} all-to-all(bf16[16,12,4096]{2,1,0:T(8,128)(2,1)S(1)} %reshape.102), channel_id=1, replica_groups=mesh['prompt'=8,'dp'=4,'expert'=16] {'expert'}, dimensions={0} | all-to-all | bytes 3145728 | tf_op jit(solution)/shard_map/all_to_all | solution.py:126
  169.8 2.5 reshape.103
  172.3 19.6 %all-gather.7.cloned.1.call-done = bf16[1,768,4096]{2,1,0:T(8,128)(2,1)} async-done(((bf16[1,24,4096]{2,1,0:T(8,128)(2,1)}), bf16[1,768,4096]{2,1,0:T(8,128)(2,1)}) %all-gather.7.cloned.1.call-update) | async-done | bytes 6291472 | tf_op jit(solution)/shard_map/all_gather | solution.py:135
  191.9 5.8 %fusion.4 = f32[192,768]{1,0:T(8,128)} fusion(bf16[192,4096]{1,0:T(8,128)(2,1)S(1)} %reshape.103, bf16[1,768,4096]{2,1,0:T(8,128)(2,1)} %all-gather.7.cloned.1.call-done), kind=kOutput, calls=%fused_computation.4 | convolution fusion | flops 1207959552 | bytes 8454144 | tf_op jit(solution)/shard_map/dot_general | solution.py:51
  197.7 88.7 %all-gather.11.cloned.1.call-done = bf16[1,768,4096]{2,1,0:T(8,128)(2,1)} async-done(((bf16[1,24,4096]{2,1,0:T(8,128)(2,1)}), bf16[1,768,4096]{2,1,0:T(8,128)(2,1)}) %all-gather.11.cloned.1.call-update) | async-done | bytes 6291472 | tf_op jit(solution)/shard_map/all_gather | solution.py:137
  286.4 94.3 %all-gather.9.cloned.1.call-done = bf16[1,768,4096]{2,1,0:T(8,128)(2,1)} async-done(((bf16[1,24,4096]{2,1,0:T(8,128)(2,1)}), bf16[1,768,4096]{2,1,0:T(8,128)(2,1)}) %all-gather.9.cloned.1.call-update) | async-done | bytes 6291472 | tf_op jit(solution)/shard_map/all_gather | solution.py:136
  380.7 10.4 %fusion.6 = bf16[192,4096]{1,0:T(8,128)(2,1)} fusion(bf16[1,768,4096]{2,1,0:T(8,128)(2,1)} %all-gather.11.cloned.1.call-done, bf16[192,4096]{1,0:T(8,128)(2,1)S(1)} %reshape.103, bf16[1,768,4096]{2,1,0:T(8,128)(2,1)} %all-gather.9.cloned.1.call-done, f32[192,768]{1,0:T(8,128)} %fusion.4), kind=kOutput, calls=%fused_computation.6 | convolution fusion | flops 2417590272 | bytes 16318464 | tf_op jit(solution)/shard_map/dot_general | solution.py:54
  391.1 3.4 reshape.104
  394.6 7.5 %all-to-all-start.1 = ((bf16[16,12,4096]{2,1,0:T(8,128)(2,1)}), bf16[16,12,4096]{2,1,0:T(8,128)(2,1)S(1)}, u32[]{:S(2)}, u32[]{:S(2)}) async-start(bf16[16,12,4096]{2,1,0:T(8,128)(2,1)} %reshape.104), calls=%async_computation.1 | async-start | bytes 4194304 | tf_op jit(solution)/shard_map/all_to_all | solution.py:140
  402.0 0.0 all-reduce.8.cloned.1.call-start
  402.1 0.2 bitcast_multiply_fusion
  402.3 1.1 convolution_convert_fusion.1
  403.4 2.0 select_convert_fusion
  405.4 0.0 all-reduce.8.cloned.1.call-update
  405.4 1.1 fusion.58
  406.5 0.1 convert_element_type.80
  406.6 0.1 copy.79
  406.7 0.1 copy.80
  406.8 1.3 dynamic-slice
  408.8 0.1 select_convert_fusion.1
  408.8 133.7 %all-reduce.5 = bf16[2,64,192]{2,1,0:T(8,128)(2,1)S(1)} all-reduce(bf16[2,64,192]{2,1,0:T(8,128)(2,1)S(1)} %select_convert_fusion.1), channel_id=3, replica_groups=mesh['prompt'=8,'dp'=4,'expert'=16] {'prompt','dp'}, use_global_device_ids=true, to_apply=%region_4.5.clone | all-reduce | flops 24576 | bytes 98304
  542.5 0.6 dynamic-slice_convert_fusion.1
  543.1 24.9 %all-reduce.8.cloned.1.call-done = bf16[2,64,64,128]{3,2,1,0:T(8,128)(2,1)} async-done(((bf16[2,64,64,128]{3,2,1,0:T(8,128)(2,1)}), bf16[2,64,64,128]{3,2,1,0:T(8,128)(2,1)}) %all-reduce.8.cloned.1.call-update) | async-done | bytes 2097168
  568.0 1.5 dynamic-slice_convert_fusion
  569.5 1.3 reshape.105
  570.8 2.9 fusion.9
  (36 shorter events, 0.2 us)
Async XLA Ops:
  7.2 6.4 %copy-start = (bf16[128,128]{1,0:T(8,128)(2,1)S(1)}, bf16[128,128]{1,0:T(8,128)(2,1)}, u32[]{:S(2)}) copy-start(bf16[128,128]{1,0:T(8,128)(2,1)} %param.19) | copy-start | bytes 98308
  7.2 6.4 %copy-start.7 = (bf16[128,128]{1,0:T(8,128)(2,1)S(1)}, bf16[128,128]{1,0:T(8,128)(2,1)}, u32[]{:S(2)}) copy-start(bf16[128,128]{1,0:T(8,128)(2,1)} %param.18) | copy-start | bytes 98308
  7.2 6.5 %copy-start.13 = (f32[64]{0:T(128)S(1)}, f32[64]{0:T(128)}, u32[]{:S(2)}) copy-start(f32[64]{0:T(128)} %param.22) | copy-start | bytes 772
  7.2 90.1 %all-gather.5.cloned.1.call-start = ((), (), s32[]{:S(2)}) async-start(), calls=%async_computation.2 | async-start | bytes 2162688 | tf_op jit(solution)/shard_map/all_gather | solution.py:80
  7.9 183.9 %all-gather.7.cloned.1.call-start = ((), (), s32[]{:S(2)}) async-start(), calls=%async_computation.3 | async-start | bytes 6488064 | tf_op jit(solution)/shard_map/all_gather | solution.py:135
  8.7 277.7 %all-gather.11.cloned.1.call-start = ((), (), s32[]{:S(2)}) async-start(), calls=%async_computation.5 | async-start | bytes 6488064 | tf_op jit(solution)/shard_map/all_gather | solution.py:137
  9.4 371.3 %all-gather.9.cloned.1.call-start = ((), (), s32[]{:S(2)}) async-start(), calls=%async_computation.4 | async-start | bytes 6488064 | tf_op jit(solution)/shard_map/all_gather | solution.py:136
  11.2 8.6 %copy-start.5 = (f32[64,128]{1,0:T(8,128)}, f32[64,128]{1,0:T(8,128)S(1)}, u32[]{:S(2)}) copy-start(f32[64,128]{1,0:T(8,128)S(1)} %copy.73) | copy-start | bytes 98308
  13.5 6.3 %copy-start.11 = (pred[128]{0:T(512)(128)(4,1)}, pred[128]{0:T(512)(128)(4,1)S(1)}, u32[]{:S(2)}) copy-start(pred[128]{0:T(512)(128)(4,1)S(1)} %iota_compare_fusion.6) | copy-start | bytes 388
  13.7 6.1 %copy-start.3 = (f32[128,128]{1,0:T(8,128)}, f32[128,128]{1,0:T(8,128)S(1)}, u32[]{:S(2)}) copy-start(f32[128,128]{1,0:T(8,128)S(1)} %fusion.73) | copy-start | bytes 196612
  19.8 2.6 copy-start.9
  21.8 53.4 %copy-start.2 = (f32[4,4096]{1,0:T(4,128)S(1)}, f32[4,4096]{1,0:T(4,128)}, u32[]{:S(2)}) copy-start(f32[4,4096]{1,0:T(4,128)} %param.23) | copy-start | bytes 196612
  81.0 1.9 copy-start.8
  98.6 1.6 copy-start.1
  98.6 1.6 copy-start.4
  98.6 1.6 copy-start.6
  98.6 1.6 copy-start.12
  98.6 1.6 copy-start.14
  394.6 174.9 %all-to-all-start.1 = ((bf16[16,12,4096]{2,1,0:T(8,128)(2,1)}), bf16[16,12,4096]{2,1,0:T(8,128)(2,1)S(1)}, u32[]{:S(2)}, u32[]{:S(2)}) async-start(bf16[16,12,4096]{2,1,0:T(8,128)(2,1)} %reshape.104), calls=%async_computation.1 | async-start | bytes 4194304 | tf_op jit(solution)/shard_map/all_to_all | solution.py:140
  402.0 165.9 %all-reduce.8.cloned.1.call-start = ((), (), s32[]{:S(2)}) async-start(), calls=%async_computation.6 | async-start | bytes 4194304
  406.7 164.1 %copy-start.10 = (f32[128,1]{0,1:T(1,128)S(1)}, f32[128,1]{0,1:T(1,128)}, u32[]{:S(2)}) copy-start(f32[128,1]{0,1:T(1,128)} %param.30) | copy-start | bytes 1540
Sparse Core Ops, SparseCore 0:
  11.2 86.0 all-gather.4
  100.4 91.4 all-gather.6
  195.0 91.2 all-gather.10
  289.4 91.2 all-gather.8
  406.1 161.8 all-reduce.7
where the time goes:
time: 583 us; the launch traced here: 580 us
  waiting for transfers between devices  244 us (42%)
  blocking collectives  242 us (42%)
  matrix products  37.1 us (6%)
  local copies, waits for them, and re-layouts  19.7 us (3%)
  between operations  16.2 us (3%)
  other arithmetic  14.2 us (2%)
  starting transfers between devices  7.67 us (1%)
    unnamed x1, blocking collectives  134 us
    all_gather x1, waiting for transfers between devices, shards(): lax.all_gather(up_weight, ('prompt', 'dp'), axis=1, tiled=True)  94.3 us
    all_gather x1, waiting for transfers between devices, shards(): lax.all_gather(down_weight, ('prompt', 'dp'), axis=1, tiled=True)  88.7 us
    all_to_all x1, blocking collectives, shards(): lax.all_to_all(outgoing.reshape(expert_count, capacity, row_width), 'expe...  57.1 us
    all_gather x1, blocking collectives, shards(): lax.all_gather(prompt_taps, ('prompt', 'dp'), axis=1, tiled=True)  50.8 us
    unnamed x6, waiting for transfers between devices  27.5 us
    all_gather x1, waiting for transfers between devices, shards(): lax.all_gather(gate_weight, ('prompt', 'dp'), axis=1, tiled=True)  19.6 us
    dot_general x2, matrix products, mixer(): jnp.einsum('hts,shp->thp', factor, conv_out, precision=lax.Precision.HIGH...  14.6 us
  transfers between devices with their start and end apart: 6, of which 5 were waited for; matrix products, arithmetic and copies ran while one was open for 9% of the time, Pallas kernels for 0%

commit v1 on v0

v1 whole, which is shorter than its diff:
```python
import functools

import jax
import jax.numpy as jnp
from jax import lax
from jax.experimental import pallas as pl
from jax.experimental.pallas import tpu as pltpu
from jax.sharding import Mesh
from jax.sharding import PartitionSpec as P

AXES = ("y", "xh", "xl", "z", "c")
PLANE = ("y", "xh", "xl")
LINE = ("xh", "z")
GROUPS = 4


def mixer(
    x_rows,
    b_rows,
    c_rows,
    step_raw,
    decay_rate,
    skip_gain,
    conv_weight,
    state_zero,
    taps_zero,
    length,
):
    steps_n, row_width = x_rows.shape
    head_count, head_size, state_n = state_zero.shape
    taps_n = taps_zero.shape[1] // head_size
    prior = jnp.transpose(taps_zero.reshape(head_count, taps_n, head_size), (1, 0, 2)).reshape(
        taps_n, row_width
    )
    series = jnp.concatenate([prior, x_rows.astype(jnp.float32)], 0)
    summed = conv_weight[taps_n] * series[taps_n:]
    for offset in range(taps_n):
        summed = summed + conv_weight[offset] * series[offset : offset + steps_n]
    conv_out = jax.nn.silu(summed).reshape(steps_n, head_count, head_size)
    step_size = jax.nn.softplus(step_raw)
    decay_sum = jnp.cumsum(-step_size * decay_rate[None, :], axis=0)
    scores = jnp.dot(c_rows, b_rows.T, preferred_element_type=jnp.float32)
    positions = lax.iota(jnp.int32, steps_n)
    causal = positions[:, None] >= positions[None, :]
    gaps = decay_sum.T[:, :, None] - decay_sum.T[:, None, :]
    factor = jnp.where(causal[None], jnp.exp(jnp.where(causal[None], gaps, -60.0)), 0.0)
    factor = factor * scores[None] * step_size.T[:, None, :]
    inner = jnp.einsum("hts,shp->thp", factor, conv_out, precision=lax.Precision.HIGHEST)
    carried = jnp.dot(
        c_rows.astype(jnp.float32),
        state_zero.reshape(head_count * head_size, state_n).T,
        precision=lax.Precision.HIGHEST,
    ).reshape(steps_n, head_count, head_size)
    output = inner + jnp.exp(decay_sum)[:, :, None] * carried + skip_gain[None, :, None] * conv_out
    live = (positions < length)[:, None, None]
    return jnp.where(live, output, 0.0).reshape(steps_n, row_width)


def unpack_rows(slots, sources, group):
    count, total = sources * slots, sources * GROUPS * slots
    row = lax.broadcasted_iota(jnp.int32, (count, total), 0)
    col = lax.broadcasted_iota(jnp.int32, (count, total), 1)
    wanted = (row // slots) * (GROUPS * slots) + group * slots + row % slots
    return (col == wanted).astype(jnp.bfloat16)


def expert_kernel(slots, sources, arrived_ref, weight_ref, out_ref, rows_ref, total_ref):
    step = pl.program_id(0)
    width = arrived_ref.shape[1]

    @pl.when(step == 0)
    def _():
        for group in range(GROUPS):
            pick = unpack_rows(slots, sources, group)
            rows_ref[:, group * width : (group + 1) * width] = jnp.dot(
                pick, arrived_ref[...], preferred_element_type=jnp.float32
            ).astype(jnp.bfloat16)
        total_ref[...] = jnp.zeros_like(total_ref)

    dims = (((1,), (1,)), ((), ()))
    rows = rows_ref[...]
    gate = lax.dot_general(rows, weight_ref[0], dims, preferred_element_type=jnp.float32)
    upper = lax.dot_general(rows, weight_ref[1], dims, preferred_element_type=jnp.float32)
    hidden = (jax.nn.silu(gate) * upper).astype(jnp.bfloat16)
    total_ref[...] += jnp.dot(hidden, weight_ref[2], preferred_element_type=jnp.float32)

    @pl.when(step == pl.num_programs(0) - 1)
    def _():
        packed = None
        for group in range(GROUPS):
            part = total_ref[:, group * width : (group + 1) * width].astype(jnp.bfloat16)
            pick = unpack_rows(slots, sources, group)
            term = lax.dot_general(
                pick, part, (((0,), (0,)), ((), ())), preferred_element_type=jnp.float32
            )
            packed = term if packed is None else packed + term
        out_ref[...] = packed.astype(jnp.bfloat16)


def expert_apply(arrived, weights, slots, sources, chunk=256):
    packed_rows, width = arrived.shape
    units, channels = weights.shape[1:]
    count = slots * sources
    return pl.pallas_call(
        functools.partial(expert_kernel, slots, sources),
        grid=(units // chunk,),
        in_specs=[
            pl.BlockSpec((packed_rows, width), lambda i: (0, 0)),
            pl.BlockSpec((3, chunk, channels), lambda i: (0, i, 0)),
        ],
        out_specs=pl.BlockSpec((packed_rows, width), lambda i: (0, 0)),
        out_shape=jax.ShapeDtypeStruct((packed_rows, width), jnp.bfloat16),
        scratch_shapes=[
            pltpu.VMEM((count, channels), jnp.bfloat16),
            pltpu.VMEM((count, channels), jnp.float32),
        ],
        compiler_params=pltpu.CompilerParams(vmem_limit_bytes=48 * 1024 * 1024),
        cost_estimate=pl.CostEstimate(
            flops=6 * count * units * channels,
            bytes_accessed=6 * units * channels + 4 * packed_rows * width,
            transcendentals=count * units,
        ),
    )(arrived, weights)


def shards(
    ssm_input,
    b_inputs,
    c_readout,
    step_raw,
    decay_rate,
    skip_gain,
    conv_weight,
    prompt_state,
    prompt_taps,
    group_index,
    lengths,
    mixed_grad,
    expert_index,
    route_gain,
    gate_weight,
    up_weight,
    down_weight,
):
    steps_n, row_width = ssm_input.shape
    prompts, own_heads, head_size, state_n = prompt_state.shape
    taps_width = prompt_taps.shape[2]
    owners = lax.axis_size(PLANE)
    lines, expert_count = lax.axis_size(LINE), lax.axis_size(("z", "c"))
    heads = owners * own_heads
    state_rows = own_heads * head_size
    taps_rows = own_heads * taps_width // state_n

    stacked = jnp.concatenate([gate_weight, up_weight, down_weight], 0)
    swapped = lax.ppermute(
        stacked, ("xh", "c"), [(a * 2 + b, b * 2 + a) for a in range(2) for b in range(2)]
    )
    weights = lax.all_gather(swapped, ("y", "xl", "c"), axis=1, tiled=True)

    members = lax.all_gather(group_index, PLANE, axis=0, tiled=True)
    held = jnp.concatenate(
        [
            prompt_state.reshape(prompts, state_rows, state_n),
            prompt_taps.reshape(prompts, taps_rows, state_n),
        ],
        1,
    )
    outgoing_state = jnp.where((members == 0)[:, None, None], held[0][None], held[1][None])
    arrived_state = lax.all_to_all(outgoing_state, PLANE, 0, 0, tiled=True)
    state_piece = arrived_state[:, :state_rows].reshape(heads, head_size, state_n)
    taps_piece = arrived_state[:, state_rows:].reshape(heads, taps_width)

    def forward(state_in, taps_in):
        return mixer(
            ssm_input,
            b_inputs,
            c_readout,
            step_raw,
            decay_rate,
            skip_gain,
            conv_weight,
            state_in,
            taps_in,
            lengths[0],
        )

    mixed, pull = jax.vjp(forward, state_piece.astype(jnp.float32), taps_piece.astype(jnp.float32))
    grad_s, grad_t = pull(mixed_grad.astype(jnp.float32))
    outgoing_grad = jnp.concatenate(
        [
            grad_s.astype(jnp.bfloat16).reshape(owners, state_rows, state_n),
            grad_t.astype(jnp.bfloat16).reshape(owners, taps_rows, state_n),
        ],
        1,
    )
    arrived_grad = lax.all_to_all(outgoing_grad, PLANE, 0, 0, tiled=True)
    belongs = (lax.iota(jnp.int32, prompts)[:, None] == members[None, :]).astype(jnp.bfloat16)
    summed = lax.dot_general(
        belongs, arrived_grad, (((1,), (0,)), ((), ())), preferred_element_type=jnp.float32
    )
    state_grad = summed[:, :state_rows].reshape(prompts, own_heads, head_size, state_n)
    taps_grad = summed[:, state_rows:].reshape(prompts, own_heads, taps_width)

    slots = 3 * steps_n // (2 * expert_count)
    width = row_width // GROUPS
    rows = mixed.astype(jnp.bfloat16)
    chosen = expert_index[:, 0]
    onehot = (chosen[:, None] == lax.iota(jnp.int32, expert_count)[None, :]).astype(jnp.int32)
    slot = jnp.sum((jnp.cumsum(onehot, axis=0) - onehot) * onehot, axis=1)
    place = (chosen % 2) * (lines // 2) + chosen // 2
    base = place * (GROUPS * slots) + slot
    packed_rows = lines * GROUPS * slots
    spots = lax.iota(jnp.int32, packed_rows)
    placing = [
        (spots[:, None] == (base + group * slots)[None, :]).astype(jnp.bfloat16)
        for group in range(GROUPS)
    ]
    outgoing = None
    for group in range(GROUPS):
        term = jnp.dot(
            placing[group],
            rows[:, group * width : (group + 1) * width],
            preferred_element_type=jnp.float32,
        )
        outgoing = term if outgoing is None else outgoing + term
    arrived = lax.all_to_all(
        outgoing.astype(jnp.bfloat16).reshape(lines, GROUPS * slots, width), LINE, 0, 0, tiled=True
    )
    produced = expert_apply(arrived.reshape(packed_rows, width), weights, slots, lines)
    returned = lax.all_to_all(
        produced.reshape(lines, GROUPS * slots, width), LINE, 0, 0, tiled=True
    ).reshape(packed_rows, width)
    per_token = jnp.concatenate(
        [
            lax.dot_general(
                placing[group], returned, (((0,), (0,)), ((), ())), preferred_element_type=jnp.float32
            )
            for group in range(GROUPS)
        ],
        1,
    )
    moe_out = (route_gain * per_token).astype(jnp.bfloat16)
    return (moe_out, state_grad, taps_grad)


def solution(mesh):
    prompt, dp, expert = (mesh.shape[name] for name in ("prompt", "dp", "expert"))
    fine = Mesh(mesh.devices.reshape(prompt, 2, dp // 2, expert // 2, 2), AXES)
    tokens = P(AXES, None)
    single = P(AXES)
    experts, plane = ("z", "c"), PLANE
    return jax.shard_map(
        shards,
        mesh=fine,
        in_specs=(
            tokens,
            tokens,
            tokens,
            tokens,
            P(),
            P(),
            P(),
            P(experts, plane, None, None),
            P(experts, plane, None),
            single,
            single,
            tokens,
            tokens,
            tokens,
            P(experts, plane, None),
            P(experts, plane, None),
            P(experts, plane, None),
        ),
        out_specs=(
            tokens,
            P(experts, plane, None, None),
            P(experts, plane, None),
        ),
        check_vma=False,
    )
```

time: 583 us -> 271 us (0.46)
  the two profiles are of different devices: /device:TPU:56 before, /device:TPU:48 now
where the time goes in v1:
time: 271 us; the launch traced here: 270 us
  waiting for transfers between devices  116 us (43%)
  starting transfers between devices  39.3 us (15%)
  blocking collectives  29.5 us (11%)
  matrix products  21.7 us (8%)
  other arithmetic  19.2 us (7%)
  between operations  16 us (6%)
  local copies, waits for them, and re-layouts  14.2 us (5%)
  Pallas kernels  14.2 us (5%)
    all_to_all x1, waiting for transfers between devices, shards(): lax.all_to_all(produced.reshape(lines, GROUPS * slots, width), LINE, 0, 0...  38.3 us
    all_to_all x1, waiting for transfers between devices, shards(): lax.all_to_all(outgoing.astype(jnp.bfloat16).reshape(lines, GROUPS * slot...  32.1 us
    unnamed x1, blocking collectives  29.5 us
    all_gather x1, waiting for transfers between devices, shards(): weights = lax.all_gather(swapped, ('y', 'xl', 'c'), axis=1, tiled=True)  23.7 us
    all_to_all x1, waiting for transfers between devices, shards(): arrived_state = lax.all_to_all(outgoing_state, PLANE, 0, 0, tiled=True)  21.5 us
    dot_general x2, matrix products, mixer(): jnp.einsum('hts,shp->thp', factor, conv_out, precision=lax.Precision.HIGH...  14.6 us
    pallas_call x1, Pallas kernels, expert_apply(): pl.pallas_call(functools.partial(expert_kernel, slots, sources), grid=(un...  14.2 us
    all_to_all x1, starting transfers between devices, shards(): lax.all_to_all(outgoing.astype(jnp.bfloat16).reshape(lines, GROUPS * slot...  12.7 us
  transfers between devices with their start and end apart: 6, of which 4 were waited for; matrix products, arithmetic and copies ran while one was open for 17% of the time, Pallas kernels for 5%

profile of v1, /device:TPU:48, one launch (start us, length us, event | category | flops | bytes accessed | tf_op | source)
XLA Modules:
  0.0 269.7 jit_solution(14354011119867994341)
XLA Ops:
  7.2 1.2 pad_maximum_fusion.2
  8.4 0.7 collective-permute-start
  9.2 0.8 copy-done.8
  10.0 0.9 reshape.209
  11.6 1.3 dynamic-slice
  12.8 0.8 dynamic-update-slice
  13.6 29.5 %all-reduce.4 = s32[32]{0:T(128)S(1)} all-reduce(s32[32]{0:T(128)S(1)} %dynamic-update-slice), channel_id=1, replica_groups=mesh['y'=8,'xh'=2,'xl'=2,'z'=8,'c'=2] {'y','xh','xl'}, use_global_device_ids=true, to_apply=%add.4 | all-reduce | flops 32 | bytes 256
  43.1 0.8 fusion.61
  43.9 1.2 broadcast_select_fusion
  45.1 8.0 %all-to-all-start = ((bf16[32,131,128]{2,1,0:T(8,128)(2,1)}), bf16[32,131,128]{2,1,0:T(8,128)(2,1)S(1)}, u32[]{:S(2)}, u32[]{:S(2)}) async-start(bf16[32,131,128]{2,1,0:T(8,128)(2,1)} %broadcast_select_fusion), calls=%async_computation | async-start | bytes 2228224 | tf_op jit(solution)/shard_map/all_to_all | solution.py:169
  53.1 0.1 negate_multiply_fusion
  53.2 0.1 copy.61
  53.3 0.2 reduce_window_sum.23
  53.5 0.1 copy.62
  54.2 0.7 copy.65
  55.0 0.1 fusion.79
  55.2 6.1 %bitcast_add_fusion = f32[128,64,64]{0,2,1:T(8,128)} fusion(f32[64,128]{1,0:T(8,128)S(1)} %get-tuple-element.30, f32[128,128]{1,0:T(8,128)S(1)} %fusion.79, f32[64,128]{1,0:T(8,128)S(1)} %copy.62, pred[128,128]{1,0:T(8,128)(4,1)S(1)} %iota_compare_fusion.12, f32[64]{0:T(128)S(1)} %copy-done.32, pred[128]{0:T(512)(128)(4,1)S(1)} %iota_compare_fusion.14, ...), kind=kOutput, calls=%fused_computation.22 | convolution fusion | flops 813694976 | bytes 3293568 | tf_op jit(solution)/shard_map/transpose(jvp(hts,shp->thp))/dot_general | solution.py:48
  61.3 1.9 copy.66
  63.3 2.8 %convert_element_type.48 = f32[128,4096]{1,0:T(8,128)} convert(bf16[128,4096]{1,0:T(8,128)(2,1)} %param.17) | non-fusion elementwise | flops 524288 | bytes 3145728 | tf_op jit(solution)/shard_map/jvp()/convert_element_type | solution.py:35
  66.1 0.1 copy.64
  66.2 0.1 fusion.59
  66.3 0.2 reduce_window_sum.22
  66.5 0.2 select_reduce_fusion
  66.7 0.6 broadcast_add_fusion
  67.3 0.6 broadcast_add_fusion.2
  67.8 0.6 fusion.77
  68.5 21.5 %all-to-all-done = bf16[32,131,128]{2,1,0:T(8,128)(2,1)S(1)} async-done(((bf16[32,131,128]{2,1,0:T(8,128)(2,1)}), bf16[32,131,128]{2,1,0:T(8,128)(2,1)S(1)}, u32[]{:S(2)}, u32[]{:S(2)}) %all-to-all-start) | async-done | bytes 1073184 | tf_op jit(solution)/shard_map/all_to_all | solution.py:169
  90.0 0.1 reshape.228
  90.2 0.1 reshape.225
  90.3 5.9 %broadcast_multiply_fusion = (f32[128,4096]{1,0:T(8,128)}, f32[128,4096]{1,0:T(8,128)S(1)}, f32[128,4096]{1,0:T(8,128)S(1)}) fusion(f32[4096]{0:T(1024)} %bitcast.100, f32[128,4096]{1,0:T(8,128)S(1)} %copy.66, f32[128,4096]{1,0:T(8,128)} %convert_element_type.48, f32[3,4096]{1,0:T(4,128)S(1)} %reshape.225, f32[4096]{0:T(1024)S(1)} %bitcast.98, ...), kind=kLoop, calls=%fused_computation.52 | loop fusion | flops 10485760 | bytes 10600448 | tf_op jit(solution)/shard_map/transpose(jvp())/mul | solution.py:38
  96.2 3.0 %broadcast_multiply_fusion.1 = (f32[128,4096]{1,0:T(8,128)}, f32[128,4096]{1,0:T(8,128)}, f32[128,4096]{1,0:T(8,128)}, f32[128,4096]{1,0:T(8,128)S(1)}) fusion(f32[128,4096]{1,0:T(8,128)S(1)} %get-tuple-element.16, f32[4096]{0:T(1024)S(1)} %bitcast.99, f32[4096]{0:T(1024)S(1)} %bitcast.97, f32[4096]{0:T(1024)S(1)} %bitcast.95, ...), kind=kLoop, calls=%fused_computation.53 | loop fusion | flops 3670016 | bytes 12632064 | tf_op jit(solution)/shard_map/transpose(jvp())/mul | solution.py:38
  99.2 1.9 copy.60
  101.0 0.1 slice.75
  101.2 0.4 fusion.80
  101.7 1.1 copy-done.6
  102.8 8.5 %fusion.16 = bf16[128,64,64]{0,2,1:T(8,128)(2,1)S(1)} fusion(f32[128,64,64]{0,2,1:T(8,128)S(1)} %bitcast.84, f32[128,64,64]{0,2,1:T(8,128)S(1)} %bitcast.83, f32[64,128]{1,0:T(8,128)S(1)} %copy-done.14, f32[128,128]{1,0:T(8,128)S(1)} %copy-done.11, f32[64,128]{1,0:T(8,128)S(1)} %copy-done.16, pred[128,128]{1,0:T(8,128)(4,1)S(1)} %copy-done.19, ...), kind=kOutput, calls=%fused_computation.28 | convolution fusion | flops 813694976 | bytes 5423488 | tf_op jit(solution)/shard_map/jvp(hts,shp->thp)/dot_general | solution.py:48
  111.4 0.6 fusion.45
  112.0 0.6 fusion.41
  112.6 0.6 fusion.43
  113.2 0.1 copy-done.21
  113.3 1.8 add_convert_fusion
  115.1 12.7 %all-to-all-start.1 = ((bf16[16,48,1024]{2,1,0:T(8,128)(2,1)}), bf16[16,48,1024]{2,1,0:T(8,128)(2,1)S(1)}, u32[]{:S(2)}, u32[]{:S(2)}) async-start(bf16[16,48,1024]{2,1,0:T(8,128)(2,1)} %bitcast.20), calls=%async_computation.1 | async-start | bytes 3145728 | tf_op jit(solution)/shard_map/all_to_all | solution.py:226
  127.9 0.2 bitcast_multiply_fusion
  128.1 1.1 convolution_convert_fusion
  129.2 0.3 copy-done.2
  129.5 0.7 copy-done.3
  130.1 0.7 copy-done.1
  130.9 0.1 convert_element_type.56
  131.1 0.1 convert_element_type.58
  131.2 1.1 pad_maximum_fusion.1
  132.3 32.1 %all-to-all-done.1 = bf16[16,48,1024]{2,1,0:T(8,128)(2,1)S(1)} async-done(((bf16[16,48,1024]{2,1,0:T(8,128)(2,1)}), bf16[16,48,1024]{2,1,0:T(8,128)(2,1)S(1)}, u32[]{:S(2)}, u32[]{:S(2)}) %all-to-all-start.1) | async-done | bytes 1572896 | tf_op jit(solution)/shard_map/all_to_all | solution.py:226
  164.3 7.2 %all-to-all-start.3 = ((bf16[32,131,128]{2,1,0:T(8,128)(2,1)}), bf16[32,131,128]{2,1,0:T(8,128)(2,1)S(1)}, u32[]{:S(2)}, u32[]{:S(2)}) async-start(bf16[32,131,128]{2,1,0:T(8,128)(2,1)} %pad_maximum_fusion.1), calls=%async_computation.3 | async-start | bytes 2228224 | tf_op jit(solution)/shard_map/all_to_all | solution.py:196
  171.5 23.7 %all-gather.2.cloned.1.call-done.weight_ref = bf16[3,768,4096]{2,1,0:T(8,128)(2,1)} async-done(((bf16[3,24,4096]{2,1,0:T(8,128)(2,1)}), bf16[3,768,4096]{2,1,0:T(8,128)(2,1)}) %all-gather.2.cloned.1.call-update) | async-done | bytes 18874384 | tf_op jit(solution)/shard_map/all_gather | solution.py:158
  195.2 14.2 %shard_map.184 = bf16[768,1024]{1,0:T(8,128)(2,1)} custom-call(bf16[768,1024]{1,0:T(8,128)(2,1)S(1)} %bitcast.74, bf16[3,768,4096]{2,1,0:T(8,128)(2,1)} %all-gather.2.cloned.1.call-done.weight_ref), custom_call_target="tpu_custom_call" | custom-call | flops 3623878656 | bytes 22020096 | tf_op jit(solution)/shard_map/pallas_call | solution.py:104
  209.3 10.7 %all-to-all-start.2 = ((bf16[16,48,1024]{2,1,0:T(8,128)(2,1)}), bf16[16,48,1024]{2,1,0:T(8,128)(2,1)S(1)}, u32[]{:S(2)}, u32[]{:S(2)}) async-start(bf16[16,48,1024]{2,1,0:T(8,128)(2,1)} %bitcast.22), calls=%async_computation.2 | async-start | bytes 3145728 | tf_op jit(solution)/shard_map/all_to_all | solution.py:230
  220.0 0.3 fusion.35
  220.3 0.7 copy.71
  221.0 0.7 reshape.223
  221.7 38.3 %all-to-all-done.2 = bf16[16,48,1024]{2,1,0:T(8,128)(2,1)S(1)} async-done(((bf16[16,48,1024]{2,1,0:T(8,128)(2,1)}), bf16[16,48,1024]{2,1,0:T(8,128)(2,1)S(1)}, u32[]{:S(2)}, u32[]{:S(2)}) %all-to-all-start.2) | async-done | bytes 1572896 | tf_op jit(solution)/shard_map/all_to_all | solution.py:230
  260.0 0.4 fusion.40
  260.4 0.4 fusion.42
  260.8 0.4 fusion.44
  261.2 0.4 fusion.39
  261.7 1.2 fusion.12
  (78 shorter events, 0.5 us)
Async XLA Ops:
  7.2 47.8 %copy-start = (bf16[128,128]{1,0:T(8,128)(2,1)S(1)}, bf16[128,128]{1,0:T(8,128)(2,1)}, u32[]{:S(2)}) copy-start(bf16[128,128]{1,0:T(8,128)(2,1)} %param.19) | copy-start | bytes 98308
  7.2 188.0 %all-gather.2.cloned.1.call-start = ((), (), s32[]{:S(2)}) async-start(), calls=%async_computation.4 | async-start | bytes 19464192 | tf_op jit(solution)/shard_map/all_gather | solution.py:158
  8.4 44.7 %copy-start.12 = (f32[128,64]{0,1:T(8,128)S(1)}, f32[128,64]{0,1:T(8,128)}, u32[]{:S(2)}) copy-start(f32[128,64]{0,1:T(8,128)} %param.20) | copy-start | bytes 98308
  8.4 44.7 %copy-start.28 = (f32[64]{0:T(128)S(1)}, f32[64]{0:T(128)}, u32[]{:S(2)}) copy-start(f32[64]{0:T(128)} %param.21) | copy-start | bytes 772
  8.4 0.7 collective-permute-start
  9.2 0.8 copy-start.8
  10.0 44.2 %copy-start.7 = (bf16[128,4096]{1,0:T(8,128)(2,1)S(1)}, bf16[128,4096]{1,0:T(8,128)(2,1)}, u32[]{:S(2)}) copy-start(bf16[128,4096]{1,0:T(8,128)(2,1)} %param.28) | copy-start | bytes 3145732
  43.1 10.1 %copy-start.26 = (s32[32]{0:T(128)}, s32[32]{0:T(128)S(1)}, u32[]{:S(2)}) copy-start(s32[32]{0:T(128)S(1)} %all-reduce.4) | copy-start | bytes 388
  45.1 9.9 %copy-start.17 = (bf16[128,128]{1,0:T(8,128)(2,1)S(1)}, bf16[128,128]{1,0:T(8,128)(2,1)}, u32[]{:S(2)}) copy-start(bf16[128,128]{1,0:T(8,128)(2,1)} %param.18) | copy-start | bytes 98308
  45.1 10.1 %copy-start.32 = (f32[64]{0:T(128)S(1)}, f32[64]{0:T(128)}, u32[]{:S(2)}) copy-start(f32[64]{0:T(128)} %param.22) | copy-start | bytes 772
  45.1 45.0 %all-to-all-start = ((bf16[32,131,128]{2,1,0:T(8,128)(2,1)}), bf16[32,131,128]{2,1,0:T(8,128)(2,1)S(1)}, u32[]{:S(2)}, u32[]{:S(2)}) async-start(bf16[32,131,128]{2,1,0:T(8,128)(2,1)} %broadcast_select_fusion), calls=%async_computation | async-start | bytes 2228224 | tf_op jit(solution)/shard_map/all_to_all | solution.py:169
  53.2 8.1 %copy-start.13 = (f32[64,128]{1,0:T(8,128)}, f32[64,128]{1,0:T(8,128)S(1)}, u32[]{:S(2)}) copy-start(f32[64,128]{1,0:T(8,128)S(1)} %get-tuple-element.30) | copy-start | bytes 98308
  53.5 7.7 %copy-start.15 = (f32[64,128]{1,0:T(8,128)}, f32[64,128]{1,0:T(8,128)S(1)}, u32[]{:S(2)}) copy-start(f32[64,128]{1,0:T(8,128)S(1)} %copy.62) | copy-start | bytes 98308
  54.9 6.4 %copy-start.4 = (bf16[128,4096]{0,1:T(8,128)(2,1)}, bf16[128,4096]{0,1:T(8,128)(2,1)S(1)}, u32[]{:S(2)}) copy-start(bf16[128,4096]{0,1:T(8,128)(2,1)S(1)} %copy.65) | copy-start | bytes 3145732
  54.9 6.4 %copy-start.30 = (pred[128]{0:T(512)(128)(4,1)}, pred[128]{0:T(512)(128)(4,1)S(1)}, u32[]{:S(2)}) copy-start(pred[128]{0:T(512)(128)(4,1)S(1)} %iota_compare_fusion.14) | copy-start | bytes 388
  55.0 6.3 %copy-start.18 = (pred[128,128]{1,0:T(8,128)(4,1)}, pred[128,128]{1,0:T(8,128)(4,1)S(1)}, u32[]{:S(2)}) copy-start(pred[128,128]{1,0:T(8,128)(4,1)S(1)} %iota_compare_fusion.12) | copy-start | bytes 49156
  55.1 6.2 %copy-start.10 = (f32[128,128]{1,0:T(8,128)}, f32[128,128]{1,0:T(8,128)S(1)}, u32[]{:S(2)}) copy-start(f32[128,128]{1,0:T(8,128)S(1)} %fusion.79) | copy-start | bytes 196612
  63.3 2.9 %copy-start.20 = (s32[128,1]{0,1:T(1,128)S(1)}, s32[128,1]{0,1:T(1,128)}, u32[]{:S(2)}) copy-start(s32[128,1]{0,1:T(1,128)} %param.29) | copy-start | bytes 1540
  63.3 4.6 %copy-start.9 = (f32[4,4096]{1,0:T(4,128)S(1)}, f32[4,4096]{1,0:T(4,128)}, u32[]{:S(2)}) copy-start(f32[4,4096]{1,0:T(4,128)} %param.23) | copy-start | bytes 196612
  67.3 22.9 %copy-start.22 = (s32[128]{0:T(128)}, s32[128]{0:T(128)S(1)}, u32[]{:S(2)}) copy-start(s32[128]{0:T(128)S(1)} %get-tuple-element.19) | copy-start | bytes 1540
  101.2 1.6 copy-start.6
  101.2 1.6 copy-start.11
  101.2 1.6 copy-start.14
  101.2 1.6 copy-start.16
  101.2 1.6 copy-start.19
  101.2 1.6 copy-start.31
  101.2 1.6 copy-start.33
  102.8 8.5 %copy-start.23 = (s32[128]{0:T(128)S(1)}, s32[128]{0:T(128)}, u32[]{:S(2)}) copy-start(s32[128]{0:T(128)} %copy-done.22) | copy-start | bytes 1540
  111.4 0.7 copy-start.25
  112.0 0.7 copy-start.24
  112.6 0.7 copy-start.21
  115.1 12.7 %copy-start.5 = (bf16[128,4096]{0,1:T(8,128)(2,1)S(1)}, bf16[128,4096]{0,1:T(8,128)(2,1)}, u32[]{:S(2)}) copy-start(bf16[128,4096]{0,1:T(8,128)(2,1)} %copy-done.4) | copy-start | bytes 3145732
  115.1 49.2 %all-to-all-start.1 = ((bf16[16,48,1024]{2,1,0:T(8,128)(2,1)}), bf16[16,48,1024]{2,1,0:T(8,128)(2,1)S(1)}, u32[]{:S(2)}, u32[]{:S(2)}) async-start(bf16[16,48,1024]{2,1,0:T(8,128)(2,1)} %bitcast.20), calls=%async_computation.1 | async-start | bytes 3145728 | tf_op jit(solution)/shard_map/all_to_all | solution.py:226
  127.8 1.6 copy-start.2
  127.8 2.3 copy-start.3
  128.1 2.8 %copy-start.1 = (f32[128,4096]{1,0:T(8,128)S(1)}, f32[128,4096]{1,0:T(8,128)}, u32[]{:S(2)}) copy-start(f32[128,4096]{1,0:T(8,128)} %get-tuple-element.15) | copy-start | bytes 6291460
  164.3 45.0 %all-to-all-start.3 = ((bf16[32,131,128]{2,1,0:T(8,128)(2,1)}), bf16[32,131,128]{2,1,0:T(8,128)(2,1)S(1)}, u32[]{:S(2)}, u32[]{:S(2)}) async-start(bf16[32,131,128]{2,1,0:T(8,128)(2,1)} %pad_maximum_fusion.1), calls=%async_computation.3 | async-start | bytes 2228224 | tf_op jit(solution)/shard_map/all_to_all | solution.py:196
  209.3 10.7 %copy-start.27 = (s32[32]{0:T(128)S(1)}, s32[32]{0:T(128)}, u32[]{:S(2)}) copy-start(s32[32]{0:T(128)} %copy-done.26) | copy-start | bytes 388
  209.3 50.6 %all-to-all-start.2 = ((bf16[16,48,1024]{2,1,0:T(8,128)(2,1)}), bf16[16,48,1024]{2,1,0:T(8,128)(2,1)S(1)}, u32[]{:S(2)}, u32[]{:S(2)}) async-start(bf16[16,48,1024]{2,1,0:T(8,128)(2,1)} %bitcast.22), calls=%async_computation.2 | async-start | bytes 3145728 | tf_op jit(solution)/shard_map/all_to_all | solution.py:230
  260.8 0.9 copy-start.29
Sparse Core Ops, SparseCore 0:
  10.1 184.9 all-gather.1

commit v2 on v1

v2 whole, which is shorter than its diff:
```python
import functools

import jax
import jax.numpy as jnp
from jax import lax
from jax.experimental import pallas as pl
from jax.experimental.pallas import tpu as pltpu
from jax.sharding import Mesh
from jax.sharding import PartitionSpec as P

AXES = ("y", "xh", "xl", "z", "c")
PLANE = ("y", "xh", "xl")
LINE = ("xh", "z")
GROUPS = 4


def spread(values, first, width, head_size):
    heads = values.shape[1]
    head = lax.broadcasted_iota(jnp.int32, (heads, width), 0)
    channel = lax.broadcasted_iota(jnp.int32, (heads, width), 1) + first
    pick = (channel // head_size == head).astype(jnp.float32)
    return jnp.dot(values, pick, precision=lax.Precision.HIGHEST, preferred_element_type=jnp.float32)


def mixer_kernel(
    head_size,
    length_ref,
    x_ref,
    prior_ref,
    conv_ref,
    skip_ref,
    grad_ref,
    b_ref,
    c_ref,
    step_ref,
    rate_ref,
    base_ref,
    state_grad_ref,
    taps_grad_ref,
    grow_ref,
    series_ref,
    scores_ref,
    first_ref,
    decay_ref,
):
    step = pl.program_id(0)
    steps_n, width = x_ref.shape
    exact = dict(precision=lax.Precision.HIGHEST, preferred_element_type=jnp.float32)
    across = (((1,), (1,)), ((), ()))
    down = (((0,), (0,)), ((), ()))

    @pl.when(step == 0)
    def _():
        row = lax.broadcasted_iota(jnp.int32, (steps_n, steps_n), 0)
        col = lax.broadcasted_iota(jnp.int32, (steps_n, steps_n), 1)
        scores = lax.dot_general(
            c_ref[...], b_ref[...], across, preferred_element_type=jnp.float32
        )
        scores_ref[...] = jnp.where(row >= col, scores, 0.0)
        turned = lax.dot_general(
            b_ref[...], c_ref[...], across, preferred_element_type=jnp.float32
        )
        first_ref[...] = jnp.where(col >= row, turned, 0.0)[: first_ref.shape[0]]
        lower = (row >= col).astype(jnp.float32)
        decay_sum = jnp.dot(lower, -step_ref[...] * rate_ref[...], **exact)
        grow_ref[...] = jnp.exp(decay_sum)
        decay_ref[...] = step_ref[...] * jnp.exp(-decay_sum)

    grow = spread(grow_ref[...], step * width, width, head_size)
    shrink = spread(decay_ref[...], step * width, width, head_size)
    series_ref[0:8] = prior_ref[...]
    series_ref[8 : 8 + steps_n] = x_ref[...].astype(jnp.float32)
    taps = [conv_ref[k : k + 1] for k in range(4)]
    summed = taps[3] * series_ref[8 : 8 + steps_n]
    for k in range(3):
        summed = summed + taps[k] * series_ref[5 + k : 5 + k + steps_n]
    conv_out = summed * jax.nn.sigmoid(summed)
    skip = skip_ref[...]
    inner = jnp.dot(scores_ref[...], conv_out * shrink, **exact)
    base_ref[...] = grow * inner + skip * conv_out

    live = lax.broadcasted_iota(jnp.int32, (steps_n, width), 0) < length_ref[0]
    given = jnp.where(live, grad_ref[...].astype(jnp.float32), 0.0)
    scaled = grow * given
    high = scaled.astype(jnp.bfloat16)
    low = (scaled - high.astype(jnp.float32)).astype(jnp.bfloat16)
    c_rows = c_ref[...]
    state_grad_ref[...] = (
        lax.dot_general(high, c_rows, down, preferred_element_type=jnp.float32)
        + lax.dot_general(low, c_rows, down, preferred_element_type=jnp.float32)
    ).astype(jnp.bfloat16)
    early = first_ref.shape[0]
    conv_grad = shrink[:early] * jnp.dot(first_ref[...], scaled, **exact) + skip * given[:early]
    gate = jax.nn.sigmoid(summed[:early])
    series_grad = conv_grad * gate * (1.0 + summed[:early] * (1.0 - gate))
    one, two, three = (series_grad[k : k + 1] for k in range(3))
    taps_grad_ref[...] = jnp.zeros_like(taps_grad_ref)
    taps_grad_ref[0:1] = taps[0] * one
    taps_grad_ref[1:2] = taps[1] * one + taps[0] * two
    taps_grad_ref[2:3] = taps[2] * one + taps[1] * two + taps[0] * three


def mixer_base(
    length, x_rows, prior, conv_weight, skip, grads, b_rows, c_rows, step_size, rate, head_size, block=512
):
    steps_n, channels = x_rows.shape
    heads, state_n = step_size.shape[1], c_rows.shape[1]
    whole = lambda *shape: pl.BlockSpec(shape, lambda i: (0,) * len(shape))
    part = lambda rows: pl.BlockSpec((rows, block), lambda i: (0, i))
    return pl.pallas_call(
        functools.partial(mixer_kernel, head_size),
        grid=(channels // block,),
        in_specs=[
            pl.BlockSpec(memory_space=pltpu.SMEM),
            part(steps_n),
            part(8),
            part(4),
            part(1),
            part(steps_n),
            whole(steps_n, state_n),
            whole(steps_n, state_n),
            whole(steps_n, heads),
            whole(1, heads),
        ],
        out_specs=[
            part(steps_n),
            pl.BlockSpec((block, state_n), lambda i: (i, 0)),
            part(8),
            whole(steps_n, heads),
        ],
        out_shape=[
            jax.ShapeDtypeStruct((steps_n, channels), jnp.float32),
            jax.ShapeDtypeStruct((channels, state_n), jnp.bfloat16),
            jax.ShapeDtypeStruct((8, channels), jnp.float32),
            jax.ShapeDtypeStruct((steps_n, heads), jnp.float32),
        ],
        scratch_shapes=[
            pltpu.VMEM((8 + steps_n, block), jnp.float32),
            pltpu.VMEM((steps_n, steps_n), jnp.float32),
            pltpu.VMEM((8, steps_n), jnp.float32),
            pltpu.VMEM((steps_n, heads), jnp.float32),
        ],
        compiler_params=pltpu.CompilerParams(vmem_limit_bytes=32 * 1024 * 1024),
        cost_estimate=pl.CostEstimate(
            flops=20 * steps_n * channels * state_n,
            bytes_accessed=10 * steps_n * channels,
            transcendentals=steps_n * channels,
        ),
    )(length, x_rows, prior, conv_weight, skip, grads, b_rows, c_rows, step_size, rate)


def dispatch_kernel(
    head_size, slots, length_ref, base_ref, state_ref, c_ref, grow_ref, spot_ref, out_ref, total_ref
):
    group = pl.program_id(0)
    steps_n, width = base_ref.shape
    carried = lax.dot_general(
        c_ref[...], state_ref[...], (((1,), (1,)), ((), ())), preferred_element_type=jnp.float32
    )
    grow = spread(grow_ref[...], group * width, width, head_size)
    live = lax.broadcasted_iota(jnp.int32, (steps_n, width), 0) < length_ref[0]
    rows = jnp.where(live, base_ref[...] + grow * carried, 0.0).astype(jnp.bfloat16)
    packed = out_ref.shape[0]
    spots = lax.broadcasted_iota(jnp.int32, (packed, steps_n), 0)
    placing = (spots == spot_ref[...] + group * slots).astype(jnp.bfloat16)
    term = jnp.dot(placing, rows, preferred_element_type=jnp.float32)

    @pl.when(group == 0)
    def _():
        total_ref[...] = term

    @pl.when(group > 0)
    def _():
        total_ref[...] += term

    @pl.when(group == GROUPS - 1)
    def _():
        out_ref[...] = total_ref[...].astype(jnp.bfloat16)


def dispatch(length, base, state, c_rows, grow, spot, head_size, slots, packed):
    steps_n, channels = base.shape
    state_n, heads, width = state.shape[1], grow.shape[1], channels // GROUPS
    return pl.pallas_call(
        functools.partial(dispatch_kernel, head_size, slots),
        grid=(GROUPS,),
        in_specs=[
            pl.BlockSpec(memory_space=pltpu.SMEM),
            pl.BlockSpec((steps_n, width), lambda g: (0, g)),
            pl.BlockSpec((width, state_n), lambda g: (g, 0)),
            pl.BlockSpec((steps_n, state_n), lambda g: (0, 0)),
            pl.BlockSpec((steps_n, heads), lambda g: (0, 0)),
            pl.BlockSpec((1, steps_n), lambda g: (0, 0)),
        ],
        out_specs=pl.BlockSpec((packed, width), lambda g: (0, 0)),
        out_shape=jax.ShapeDtypeStruct((packed, width), jnp.bfloat16),
        scratch_shapes=[pltpu.VMEM((packed, width), jnp.float32)],
        compiler_params=pltpu.CompilerParams(vmem_limit_bytes=32 * 1024 * 1024),
        cost_estimate=pl.CostEstimate(
            flops=2 * channels * steps_n * (packed + state_n),
            bytes_accessed=6 * channels * steps_n + 2 * packed * width,
            transcendentals=0,
        ),
    )(length, base, state, c_rows, grow, spot)


def unpack_rows(slots, sources, group):
    count, total = sources * slots, sources * GROUPS * slots
    row = lax.broadcasted_iota(jnp.int32, (count, total), 0)
    col = lax.broadcasted_iota(jnp.int32, (count, total), 1)
    wanted = (row // slots) * (GROUPS * slots) + group * slots + row % slots
    return (col == wanted).astype(jnp.bfloat16)


def unpack_kernel(slots, sources, arrived_ref, rows_ref):
    pick = unpack_rows(slots, sources, pl.program_id(0))
    rows_ref[...] = jnp.dot(
        pick, arrived_ref[...], preferred_element_type=jnp.float32
    ).astype(jnp.bfloat16)


def unpack(arrived, slots, sources):
    packed, width = arrived.shape
    count = slots * sources
    return pl.pallas_call(
        functools.partial(unpack_kernel, slots, sources),
        grid=(GROUPS,),
        in_specs=[pl.BlockSpec((packed, width), lambda g: (0, 0))],
        out_specs=pl.BlockSpec((count, width), lambda g: (0, g)),
        out_shape=jax.ShapeDtypeStruct((count, GROUPS * width), jnp.bfloat16),
        compiler_params=pltpu.CompilerParams(vmem_limit_bytes=24 * 1024 * 1024),
        cost_estimate=pl.CostEstimate(
            flops=2 * GROUPS * count * packed * width,
            bytes_accessed=4 * packed * width,
            transcendentals=0,
        ),
    )(arrived)


def expert_kernel(slots, sources, rows_ref, weight_ref, out_ref, total_ref):
    step = pl.program_id(0)
    width = out_ref.shape[1]
    dims = (((1,), (1,)), ((), ()))
    rows = rows_ref[...]
    gate = lax.dot_general(rows, weight_ref[0], dims, preferred_element_type=jnp.float32)
    upper = lax.dot_general(rows, weight_ref[1], dims, preferred_element_type=jnp.float32)
    hidden = (jax.nn.silu(gate) * upper).astype(jnp.bfloat16)
    part = jnp.dot(hidden, weight_ref[2], preferred_element_type=jnp.float32)

    @pl.when(step == 0)
    def _():
        total_ref[...] = part

    @pl.when(step > 0)
    def _():
        total_ref[...] += part

    @pl.when(step == pl.num_programs(0) - 1)
    def _():
        packed = None
        for group in range(GROUPS):
            block = total_ref[:, group * width : (group + 1) * width].astype(jnp.bfloat16)
            pick = unpack_rows(slots, sources, group)
            term = lax.dot_general(
                pick, block, (((0,), (0,)), ((), ())), preferred_element_type=jnp.float32
            )
            packed = term if packed is None else packed + term
        out_ref[...] = packed.astype(jnp.bfloat16)


def expert_apply(rows, weights, slots, sources, chunk=256):
    count, channels = rows.shape
    units = weights.shape[1]
    packed, width = count * GROUPS, channels // GROUPS
    return pl.pallas_call(
        functools.partial(expert_kernel, slots, sources),
        grid=(units // chunk,),
        in_specs=[
            pl.BlockSpec((count, channels), lambda i: (0, 0)),
            pl.BlockSpec((3, chunk, channels), lambda i: (0, i, 0)),
        ],
        out_specs=pl.BlockSpec((packed, width), lambda i: (0, 0)),
        out_shape=jax.ShapeDtypeStruct((packed, width), jnp.bfloat16),
        scratch_shapes=[pltpu.VMEM((count, channels), jnp.float32)],
        compiler_params=pltpu.CompilerParams(vmem_limit_bytes=48 * 1024 * 1024),
        cost_estimate=pl.CostEstimate(
            flops=6 * count * units * channels,
            bytes_accessed=6 * units * channels + 4 * packed * width,
            transcendentals=count * units,
        ),
    )(rows, weights)


def deliver(parts, members):
    y, x = lax.axis_index("y"), lax.axis_index(("xh", "xl"))
    size_y, size_x = parts.shape[:2]
    column = []
    for step in range(size_x):
        piece = lax.dynamic_index_in_dim(parts, (x + step) % size_x, 1, keepdims=False)
        if step:
            piece = lax.ppermute(
                piece, ("xh", "xl"), [(i, (i + step) % size_x) for i in range(size_x)]
            )
        column.append(piece)
    total = None
    for step in range(size_y):
        there = (y + step) % size_y
        piece = jnp.stack(
            [lax.dynamic_index_in_dim(block, there, 0, keepdims=False) for block in column], 0
        )
        if step:
            piece = lax.ppermute(piece, "y", [(i, (i + step) % size_y) for i in range(size_y)])
        for k in range(size_x):
            second = lax.dynamic_index_in_dim(
                members, (y - step) % size_y * size_x + (x - k) % size_x, 0, keepdims=False
            )
            value = piece[k].astype(jnp.float32)
            both = jnp.stack([jnp.where(second, 0.0, value), jnp.where(second, value, 0.0)])
            total = both if total is None else total + both
    return total


def shards(
    ssm_input,
    b_inputs,
    c_readout,
    step_raw,
    decay_rate,
    skip_gain,
    conv_weight,
    prompt_state,
    prompt_taps,
    group_index,
    lengths,
    mixed_grad,
    expert_index,
    route_gain,
    gate_weight,
    up_weight,
    down_weight,
):
    steps_n, row_width = ssm_input.shape
    prompts, own_heads, head_size, state_n = prompt_state.shape
    taps_n, lanes = prompt_taps.shape[2] // head_size, own_heads * head_size
    owners = lax.axis_size(PLANE)
    lines, expert_count = lax.axis_size(LINE), lax.axis_size(("z", "c"))
    state_rows = own_heads * head_size

    stacked = jnp.concatenate([gate_weight, up_weight, down_weight], 0)
    swapped = lax.ppermute(
        stacked, ("xh", "c"), [(a * 2 + b, b * 2 + a) for a in range(2) for b in range(2)]
    )
    weights = lax.all_gather(swapped, ("y", "xl", "c"), axis=1, tiled=True)

    own_taps = jnp.transpose(
        prompt_taps.reshape(prompts, own_heads, taps_n, head_size), (0, 2, 1, 3)
    ).reshape(prompts * taps_n, lanes)
    own_member = jnp.broadcast_to(group_index.astype(jnp.bfloat16)[:, None], (1, lanes))
    notice = jnp.concatenate(
        [own_taps, own_member, jnp.zeros((7 - prompts * taps_n, lanes), jnp.bfloat16)], 0
    )
    notices = lax.all_to_all(
        jnp.broadcast_to(notice[None], (owners,) + notice.shape), PLANE, 0, 0, tiled=True
    )
    members = notices[:, prompts * taps_n, 0] > 0.5
    mine = group_index[0] == 1
    prior = jnp.where(mine, notices[:, taps_n : 2 * taps_n], notices[:, :taps_n])
    prior = jnp.transpose(prior, (1, 0, 2)).reshape(taps_n, row_width).astype(jnp.float32)
    prior = jnp.concatenate([jnp.zeros((8 - taps_n, row_width), jnp.float32), prior], 0)

    held = prompt_state.reshape(prompts, state_rows, state_n)
    outgoing_state = jnp.where(members[:, None, None], held[1][None], held[0][None])
    state = lax.all_to_all(outgoing_state, PLANE, 0, 0, tiled=True).reshape(row_width, state_n)

    step_size = jax.nn.softplus(step_raw)
    base, grad_s, grad_t, grow = mixer_base(
        lengths,
        ssm_input,
        prior,
        conv_weight,
        jnp.repeat(skip_gain, head_size)[None, :],
        mixed_grad,
        b_inputs,
        c_readout,
        step_size,
        decay_rate[None, :],
        head_size,
    )
    outgoing_grad = jnp.concatenate(
        [
            grad_s.reshape(owners, state_rows, state_n),
            jnp.transpose(grad_t[:taps_n].astype(jnp.bfloat16).reshape(taps_n, owners, lanes), (1, 0, 2)),
        ],
        1,
    )
    slots = 3 * steps_n // (2 * expert_count)
    width = row_width // GROUPS
    chosen = expert_index[:, 0]
    order = lax.iota(jnp.int32, steps_n)
    before = (chosen[:, None] == chosen[None, :]) & (order[:, None] < order[None, :])
    slot = jnp.sum(before.astype(jnp.int32), axis=0)
    place = (chosen % 2) * (lines // 2) + chosen // 2
    spot = (place * (GROUPS * slots) + slot)[None, :]
    packed_rows = lines * GROUPS * slots
    outgoing = dispatch(lengths, base, state, c_readout, grow, spot, head_size, slots, packed_rows)
    arrived = lax.all_to_all(
        outgoing.reshape(lines, GROUPS * slots, width), LINE, 0, 0, tiled=True
    )
    expert_rows = unpack(arrived.reshape(packed_rows, width), slots, lines)
    weights, outgoing_grad = lax.optimization_barrier((weights, outgoing_grad))
    produced = expert_apply(expert_rows, weights, slots, lines)
    returned = lax.all_to_all(
        produced.reshape(lines, GROUPS * slots, width), LINE, 0, 0, tiled=True
    ).reshape(packed_rows, width)
    spots = lax.iota(jnp.int32, packed_rows)
    placing = [
        (spots[:, None] == spot + group * slots).astype(jnp.bfloat16) for group in range(GROUPS)
    ]
    per_token = jnp.concatenate(
        [
            lax.dot_general(
                placing[group], returned, (((0,), (0,)), ((), ())), preferred_element_type=jnp.float32
            )
            for group in range(GROUPS)
        ],
        1,
    )
    summed = deliver(
        outgoing_grad.reshape(lax.axis_size("y"), -1, state_rows + taps_n, lanes), members
    )
    state_grad = summed[:, :state_rows].reshape(prompts, own_heads, head_size, state_n)
    taps_grad = jnp.transpose(
        summed[:, state_rows:].reshape(prompts, taps_n, own_heads, head_size), (0, 2, 1, 3)
    ).reshape(prompts, own_heads, taps_n * head_size)
    moe_out = (route_gain * per_token).astype(jnp.bfloat16)
    return (moe_out, state_grad, taps_grad)


def solution(mesh):
    prompt, dp, expert = (mesh.shape[name] for name in ("prompt", "dp", "expert"))
    fine = Mesh(mesh.devices.reshape(prompt, 2, dp // 2, expert // 2, 2), AXES)
    tokens = P(AXES, None)
    single = P(AXES)
    experts, plane = ("z", "c"), PLANE
    return jax.shard_map(
        shards,
        mesh=fine,
        in_specs=(
            tokens,
            tokens,
            tokens,
            tokens,
            P(),
            P(),
            P(),
            P(experts, plane, None, None),
            P(experts, plane, None),
            single,
            single,
            tokens,
            tokens,
            tokens,
            P(experts, plane, None),
            P(experts, plane, None),
            P(experts, plane, None),
        ),
        out_specs=(
            tokens,
            P(experts, plane, None, None),
            P(experts, plane, None),
        ),
        check_vma=False,
    )
```

time: 271 us -> 304 us (1.12)
  the two profiles are of different devices: /device:TPU:48 before, /device:TPU:56 now
where the time goes in v2:
time: 304 us; the launch traced here: 300 us
  waiting for transfers between devices  104 us (34%)
  starting transfers between devices  84.8 us (28%)
  other arithmetic  39.8 us (13%)
  Pallas kernels  31.8 us (10%)
  local copies, waits for them, and re-layouts  20.8 us (7%)
  between operations  16.7 us (5%)
    all_gather x1, waiting for transfers between devices, shards(): weights = lax.all_gather(swapped, ('y', 'xl', 'c'), axis=1, tiled=True)  34 us
    all_to_all x1, waiting for transfers between devices, shards(): lax.all_to_all(outgoing.reshape(lines, GROUPS * slots, width), LINE, 0, 0...  30.5 us
    select_n x11, other arithmetic, deliver(): jnp.where(second, 0.0, value)  24.9 us
    ppermute x7, starting transfers between devices, deliver(): lax.ppermute(piece, 'y', [(i, (i + step) % size_y) for i in range(size_y)])  24.8 us
    all_to_all x1, waiting for transfers between devices, shards(): lax.all_to_all(outgoing_state, PLANE, 0, 0, tiled=True)  22.6 us
    all_to_all x1, starting transfers between devices, shards(): lax.all_to_all(jnp.broadcast_to(notice[None], (owners,) + notice.shape),...  21.5 us
    pallas_call x1, Pallas kernels, expert_apply(): pl.pallas_call(functools.partial(expert_kernel, slots, sources), grid=(un...  13.2 us
    all_to_all x1, starting transfers between devices, shards(): lax.all_to_all(outgoing.reshape(lines, GROUPS * slots, width), LINE, 0, 0...  13 us
  transfers between devices with their start and end apart: 16, of which 5 were waited for; matrix products, arithmetic and copies ran while one was open for 16% of the time, Pallas kernels for 11%

profile of v2, /device:TPU:56, one launch (start us, length us, event | category | flops | bytes accessed | tf_op | source)
XLA Modules:
  0.0 299.9 jit_solution(17294966140970764)
XLA Ops:
  7.3 1.2 pad_maximum_fusion.1
  8.4 0.7 collective-permute-start
  9.2 0.8 copy-done.9
  11.1 0.6 broadcast_in_dim.135
  11.7 21.5 %all-to-all-start = ((bf16[32,8,128]{2,1,0:T(8,128)(2,1)}), bf16[32,8,128]{2,1,0:T(8,128)(2,1)S(1)}, u32[]{:S(2)}, u32[]{:S(2)}) async-start(bf16[32,8,128]{2,1,0:T(8,128)(2,1)} %broadcast_in_dim.135), calls=%async_computation | async-start | bytes 131072 | tf_op jit(solution)/shard_map/all_to_all | solution.py:362
  34.2 6.8 %all-to-all-done = bf16[32,8,128]{2,1,0:T(8,128)(2,1)S(1)} async-done(((bf16[32,8,128]{2,1,0:T(8,128)(2,1)}), bf16[32,8,128]{2,1,0:T(8,128)(2,1)S(1)}, u32[]{:S(2)}, u32[]{:S(2)}) %all-to-all-start) | async-done | bytes 65568 | tf_op jit(solution)/shard_map/all_to_all | solution.py:362
  41.0 0.7 fusion.43
  41.7 1.1 broadcast_select_fusion
  42.8 6.2 %all-to-all-start.1 = ((bf16[32,128,128]{2,1,0:T(8,128)(2,1)}), bf16[32,128,128]{2,1,0:T(8,128)(2,1)S(1)}, u32[]{:S(2)}, u32[]{:S(2)}) async-start(bf16[32,128,128]{2,1,0:T(8,128)(2,1)} %broadcast_select_fusion), calls=%async_computation.1 | async-start | bytes 2097152 | tf_op jit(solution)/shard_map/all_to_all | solution.py:373
  49.3 1.2 copy-done.3
  50.6 1.2 copy-done.4
  51.8 9.9 %shard_map.184 = (f32[128,4096]{1,0:T(8,128)S(1)}, bf16[4096,128]{1,0:T(8,128)(2,1)S(1)}, f32[8,4096]{1,0:T(8,128)S(1)}, f32[128,64]{1,0:T(8,128)S(1)}) custom-call(s32[1]{0:T(128)S(6)} %copy.112.length_ref, bf16[128,4096]{1,0:T(8,128)(2,1)S(1)} %copy-done.3, f32[8,4096]{1,0:T(8,128)S(1)} %pad_convert_fusion.prior_ref, f32[4,4096]{1,0:T(4,128)S(1)} %copy-done.5, ...), custom_call_target="tpu_custom_call" | custom-call | flops 1342177280 | bytes 5242880 | tf_op jit(solution)/shard_map/pallas_call | solution.py:110
  61.7 1.0 copy-done
  62.7 22.6 %all-to-all-done.1 = bf16[32,128,128]{2,1,0:T(8,128)(2,1)S(1)} async-done(((bf16[32,128,128]{2,1,0:T(8,128)(2,1)}), bf16[32,128,128]{2,1,0:T(8,128)(2,1)S(1)}, u32[]{:S(2)}, u32[]{:S(2)}) %all-to-all-start.1) | async-done | bytes 1048608 | tf_op jit(solution)/shard_map/all_to_all | solution.py:373
  85.3 6.7 %shard_map.185 = bf16[768,1024]{1,0:T(8,128)(2,1)} custom-call(s32[1]{0:T(128)S(6)} %copy.112.length_ref, f32[128,4096]{1,0:T(8,128)S(1)} %get-tuple-element.9.base_ref, bf16[4096,128]{1,0:T(8,128)(2,1)S(1)} %bitcast.122, bf16[128,128]{1,0:T(8,128)(2,1)S(1)} %copy-done.2, f32[128,64]{1,0:T(8,128)S(1)} %get-tuple-element.10.grow_ref, ...), custom_call_target="tpu_custom_call" | custom-call | flops 939524096 | bytes 4718592 | tf_op jit(solution)/shard_map/pallas_call | solution.py:184
  92.0 13.0 %all-to-all-start.2 = ((bf16[16,48,1024]{2,1,0:T(8,128)(2,1)}), bf16[16,48,1024]{2,1,0:T(8,128)(2,1)S(1)}, u32[]{:S(2)}, u32[]{:S(2)}) async-start(bf16[16,48,1024]{2,1,0:T(8,128)(2,1)} %bitcast.13), calls=%async_computation.2 | async-start | bytes 3145728 | tf_op jit(solution)/shard_map/all_to_all | solution.py:406
  105.6 0.5 broadcast_add_fusion.2
  106.2 0.5 broadcast_add_fusion.1
  106.8 0.7 copy.93
  107.5 0.7 constant_dynamic-slice_fusion.54
  108.1 0.7 constant_dynamic-slice_fusion.55
  108.8 1.1 pad_maximum_fusion
  109.9 30.5 %all-to-all-done.2 = bf16[16,48,1024]{2,1,0:T(8,128)(2,1)S(1)} async-done(((bf16[16,48,1024]{2,1,0:T(8,128)(2,1)}), bf16[16,48,1024]{2,1,0:T(8,128)(2,1)S(1)}, u32[]{:S(2)}, u32[]{:S(2)}) %all-to-all-start.2) | async-done | bytes 1572896 | tf_op jit(solution)/shard_map/all_to_all | solution.py:406
  140.4 2.1 shard_map.186.rows_ref
  142.5 34.0 %all-gather.2.cloned.1.call-done.weight_ref = bf16[3,768,4096]{2,1,0:T(8,128)(2,1)} async-done(((bf16[3,24,4096]{2,1,0:T(8,128)(2,1)}), bf16[3,768,4096]{2,1,0:T(8,128)(2,1)}) %all-gather.2.cloned.1.call-update) | async-done | bytes 18874384 | tf_op jit(solution)/shard_map/all_gather | solution.py:353
  176.5 4.6 %constant_dynamic-slice_fusion.53 = (bf16[8,1,131,128]{3,1,0,2:T(2,128)(2,1)}, bf16[8,1,131,128]{3,1,0,2:T(2,128)(2,1)S(1)}, bf16[8,1,131,128]{3,1,0,2:T(2,128)(2,1)S(1)}) fusion(bf16[8,4,131,128]{3,1,0,2:T(4,128)(2,1)} %bitcast.130, s32[]{:T(128)S(6)} %select_n.871, s32[]{:T(128)S(6)} %select_n.885, s32[]{:T(128)S(6)} %select_n.878), kind=kLoop, calls=%fused_computation.222 | loop fusion | bytes 1609740 | tf_op jit(solution)/shard_map/jit(dynamic_index_in_dim)/dynamic_slice | solution.py:299
  181.1 0.8 copy.107
  181.9 3.9 %collective-permute-start.3 = (bf16[8,131,128]{2,0,1:T(8,128)(2,1)}, bf16[8,131,128]{2,0,1:T(8,128)(2,1)S(1)}, u32[]{:S(2)}, u32[]{:S(2)}) collective-permute-start(bf16[8,131,128]{2,0,1:T(8,128)(2,1)} %bitcast.117), channel_id=1, source_target_pairs={{0,48},{16,0},{32,16},{48,32},{1,49},{17,1},{33,17},{49,33},{2,50}... | collective-permute-start | bytes 804872 | tf_op jit(solution)/shard_map/ppermute | solution.py:301
  185.8 0.7 copy.108
  186.5 2.8 collective-permute-start.2
  189.3 13.2 %shard_map.187 = bf16[768,1024]{1,0:T(8,128)(2,1)} custom-call(bf16[192,4096]{1,0:T(8,128)(2,1)S(1)} %shard_map.186.rows_ref, bf16[3,768,4096]{2,1,0:T(8,128)(2,1)} %all-gather.2.cloned.1.call-done.weight_ref), custom_call_target="tpu_custom_call" | custom-call | flops 3623878656 | bytes 22020096 | tf_op jit(solution)/shard_map/pallas_call | solution.py:275
  202.5 1.6 fusion.35
  204.1 1.6 fusion.34
  205.7 9.9 %all-to-all-start.3 = ((bf16[16,48,1024]{2,1,0:T(8,128)(2,1)}), bf16[16,48,1024]{2,1,0:T(8,128)(2,1)S(1)}, u32[]{:S(2)}, u32[]{:S(2)}) async-start(bf16[16,48,1024]{2,1,0:T(8,128)(2,1)} %bitcast.17), calls=%async_computation.3 | async-start | bytes 3145728 | tf_op jit(solution)/shard_map/all_to_all | solution.py:412
  215.7 1.9 collective-permute-start.1
  217.7 1.8 dynamic-slice_bitcast_fusion.6
  219.5 0.5 constant_dynamic-slice_fusion.45
  220.0 2.4 constant_dynamic-slice_fusion.46
  222.4 10.4 %collective-permute-done.1 = bf16[8,131,128]{2,0,1:T(8,128)(2,1)S(1)} collective-permute-done((bf16[8,131,128]{2,0,1:T(8,128)(2,1)S(1)}, bf16[8,131,128]{2,0,1:T(8,128)(2,1)S(1)}, u32[]{:S(2)}, u32[]{:S(2)}) %collective-permute-start.1) | collective-permute-done | bytes 268320 | tf_op jit(solution)/shard_map/ppermute | solution.py:301
  232.8 0.5 constant_dynamic-slice_fusion.47
  233.6 1.9 collective-permute-start.10
  235.9 1.9 collective-permute-start.9
  238.1 3.5 %collective-permute-start.8 = (bf16[4,131,128]{2,0,1:T(4,128)(2,1)S(1)}, bf16[4,131,128]{2,0,1:T(4,128)(2,1)S(1)}, u32[]{:S(2)}, u32[]{:S(2)}) collective-permute-start(bf16[4,131,128]{2,0,1:T(4,128)(2,1)S(1)} %pad_maximum_fusion.6), channel_id=1, source_target_pairs={{0,320},{64,384},{128,448},{192,0},{256,64},{320,128},{384,192},{4... | collective-permute-start | bytes 402440 | tf_op jit(solution)/shard_map/ppermute | solution.py:312
  242.0 6.8 %collective-permute-start.7 = (bf16[4,131,128]{2,0,1:T(4,128)(2,1)S(1)}, bf16[4,131,128]{2,0,1:T(4,128)(2,1)S(1)}, u32[]{:S(2)}, u32[]{:S(2)}) collective-permute-start(bf16[4,131,128]{2,0,1:T(4,128)(2,1)S(1)} %pad_maximum_fusion.5), channel_id=1, source_target_pairs={{0,256},{64,320},{128,384},{192,448},{256,0},{320,64},{384,128},{4... | collective-permute-start | bytes 402440 | tf_op jit(solution)/shard_map/ppermute | solution.py:312
  249.1 4.8 %collective-permute-start.6 = (bf16[4,131,128]{2,0,1:T(4,128)(2,1)S(1)}, bf16[4,131,128]{2,0,1:T(4,128)(2,1)S(1)}, u32[]{:S(2)}, u32[]{:S(2)}) collective-permute-start(bf16[4,131,128]{2,0,1:T(4,128)(2,1)S(1)} %pad_maximum_fusion.4), channel_id=1, source_target_pairs={{0,192},{64,256},{128,320},{192,384},{256,448},{320,0},{384,64},{4... | collective-permute-start | bytes 402440 | tf_op jit(solution)/shard_map/ppermute | solution.py:312
  254.6 0.8 broadcast_select_fusion.58
  255.4 1.7 broadcast_select_fusion.60
  257.0 0.7 broadcast_select_fusion.62
  257.8 3.1 %collective-permute-start.5 = (bf16[4,131,128]{2,0,1:T(4,128)(2,1)S(1)}, bf16[4,131,128]{2,0,1:T(4,128)(2,1)S(1)}, u32[]{:S(2)}, u32[]{:S(2)}) collective-permute-start(bf16[4,131,128]{2,0,1:T(4,128)(2,1)S(1)} %pad_maximum_fusion.3), channel_id=1, source_target_pairs={{0,128},{64,192},{128,256},{192,320},{256,384},{320,448},{384,0},{... | collective-permute-start | bytes 402440 | tf_op jit(solution)/shard_map/ppermute | solution.py:312
  260.9 2.8 broadcast_select_fusion.8
  263.7 2.7 collective-permute-start.4
  266.4 2.9 broadcast_select_fusion.16
  269.4 2.9 broadcast_select_fusion.24
  272.2 2.9 broadcast_select_fusion.32
  275.2 2.8 broadcast_select_fusion.40
  278.0 2.8 broadcast_select_fusion.48
  280.8 3.0 %broadcast_select_fusion.56 = (f32[1,131,128]{2,0,1:T(1,128)S(1)}, f32[1,131,128]{2,0,1:T(1,128)S(1)}, f32[1,131,128]{2,0,1:T(1,128)S(1)}, f32[1,131,128]{2,0,1:...) fusion(pred[]{:T(512)} %bitcast.29, ...), kind=kLoop, calls=%fused_computation.115 | loop fusion | flops 201216 | bytes 670724 | tf_op jit(solution)/shard_map/jit(_where)/select_n | solution.py:318
  283.9 4.4 %maximum_add_fusion.5 = f32[2,131,128]{2,0,1:T(2,128)S(1)} fusion(f32[1,131,128]{2,0,1:T(1,128)S(1)} %get-tuple-element.120, f32[1,131,128]{2,0,1:T(1,128)S(1)} %get-tuple-element.123, f32[1,131,128]{2,0,1:T(1,128)S(1)} %get-tuple-element.121, f32[1,131,128]{2,0,1:T(1,128)S(1)} %get-tuple-element.124, f32[1,131,128]{2,0,1:T(1,128)S(1)} %get-tuple-element.122, ...), kind=kLoop, calls=%fused_computation.59 | loop fusion | flops 2112768 | bytes 4426752 | tf_op jit(solution)/shard_map/add | solution.py:319
  288.3 0.7 copy.98
  289.0 0.7 reshape.349
  290.1 0.4 fusion.4
  290.7 0.4 fusion.3
  291.2 0.4 fusion.2
  291.8 1.2 fusion
  (81 shorter events, 4.2 us)
Async XLA Ops:
  7.2 2.8 copy-start.15
  7.2 26.8 %copy-start.16 = (f32[64]{0:T(128)S(1)}, f32[64]{0:T(128)}, u32[]{:S(2)}) copy-start(f32[64]{0:T(128)} %param.22) | copy-start | bytes 772
  7.2 26.9 %copy-start.11 = (f32[128,64]{0,1:T(8,128)S(1)}, f32[128,64]{0,1:T(8,128)}, u32[]{:S(2)}) copy-start(f32[128,64]{0,1:T(8,128)} %param.20) | copy-start | bytes 98308
  7.2 27.0 %copy-start.10 = (bf16[2,2,64,128]{3,2,1,0:T(8,128)(2,1)S(1)}, bf16[2,2,64,128]{3,2,1,0:T(8,128)(2,1)}, u32[]{:S(2)}) copy-start(bf16[2,2,64,128]{3,2,1,0:T(8,128)(2,1)} %param.24) | copy-start | bytes 196612
  7.2 169.3 %all-gather.2.cloned.1.call-start = ((), (), s32[]{:S(2)}) async-start(), calls=%async_computation.4 | async-start | bytes 19464192 | tf_op jit(solution)/shard_map/all_gather | solution.py:353
  8.4 0.7 collective-permute-start
  9.2 0.8 copy-start.9
  11.7 29.3 %all-to-all-start = ((bf16[32,8,128]{2,1,0:T(8,128)(2,1)}), bf16[32,8,128]{2,1,0:T(8,128)(2,1)S(1)}, u32[]{:S(2)}, u32[]{:S(2)}) async-start(bf16[32,8,128]{2,1,0:T(8,128)(2,1)} %broadcast_in_dim.135), calls=%async_computation | async-start | bytes 131072 | tf_op jit(solution)/shard_map/all_to_all | solution.py:362
  41.7 7.4 %copy-start.19 = (s32[128,1]{0,1:T(1,128)S(1)}, s32[128,1]{0,1:T(1,128)}, u32[]{:S(2)}) copy-start(s32[128,1]{0,1:T(1,128)} %param.29) | copy-start | bytes 1540
  41.7 7.6 %copy-start.2 = (bf16[128,128]{1,0:T(8,128)(2,1)S(1)}, bf16[128,128]{1,0:T(8,128)(2,1)}, u32[]{:S(2)}) copy-start(bf16[128,128]{1,0:T(8,128)(2,1)} %c_ref.3) | copy-start | bytes 98308
  41.7 7.6 %copy-start.5 = (f32[4,4096]{1,0:T(4,128)S(1)}, f32[4,4096]{1,0:T(4,128)}, u32[]{:S(2)}) copy-start(f32[4,4096]{1,0:T(4,128)} %conv_ref.1) | copy-start | bytes 196612
  41.7 7.6 %copy-start.6 = (bf16[128,128]{1,0:T(8,128)(2,1)S(1)}, bf16[128,128]{1,0:T(8,128)(2,1)}, u32[]{:S(2)}) copy-start(bf16[128,128]{1,0:T(8,128)(2,1)} %b_ref.1) | copy-start | bytes 98308
  41.7 7.6 %copy-start.7 = (f32[64]{0:T(128)S(1)}, f32[64]{0:T(128)}, u32[]{:S(2)}) copy-start(f32[64]{0:T(128)} %param.21) | copy-start | bytes 772
  42.8 42.4 %all-to-all-start.1 = ((bf16[32,128,128]{2,1,0:T(8,128)(2,1)}), bf16[32,128,128]{2,1,0:T(8,128)(2,1)S(1)}, u32[]{:S(2)}, u32[]{:S(2)}) async-start(bf16[32,128,128]{2,1,0:T(8,128)(2,1)} %broadcast_select_fusion), calls=%async_computation.1 | async-start | bytes 2097152 | tf_op jit(solution)/shard_map/all_to_all | solution.py:373
  49.3 1.2 copy-start.3
  50.6 1.2 copy-start.4
  61.7 1.0 copy-start
  92.0 14.8 %copy-start.1 = (bf16[4096,128]{1,0:T(8,128)(2,1)S(1)}, bf16[4096,128]{1,0:T(8,128)(2,1)}, u32[]{:S(2)}) copy-start(bf16[4096,128]{1,0:T(8,128)(2,1)} %copy-done) | copy-start | bytes 3145732
  92.0 48.5 %all-to-all-start.2 = ((bf16[16,48,1024]{2,1,0:T(8,128)(2,1)}), bf16[16,48,1024]{2,1,0:T(8,128)(2,1)S(1)}, u32[]{:S(2)}, u32[]{:S(2)}) async-start(bf16[16,48,1024]{2,1,0:T(8,128)(2,1)} %bitcast.13), calls=%async_computation.2 | async-start | bytes 3145728 | tf_op jit(solution)/shard_map/all_to_all | solution.py:406
  106.2 3.8 %copy-start.13 = (s32[128]{0:T(128)}, s32[128]{0:T(128)S(1)}, u32[]{:S(2)}) copy-start(s32[128]{0:T(128)S(1)} %get-tuple-element.31) | copy-start | bytes 1540
  181.9 37.6 %collective-permute-start.3 = (bf16[8,131,128]{2,0,1:T(8,128)(2,1)}, bf16[8,131,128]{2,0,1:T(8,128)(2,1)S(1)}, u32[]{:S(2)}, u32[]{:S(2)}) collective-permute-start(bf16[8,131,128]{2,0,1:T(8,128)(2,1)} %bitcast.117), channel_id=1, source_target_pairs={{0,48},{16,0},{32,16},{48,32},{1,49},{17,1},{33,17},{49,33},{2,50}... | collective-permute-start | bytes 804872 | tf_op jit(solution)/shard_map/ppermute | solution.py:301
  186.5 33.5 %collective-permute-start.2 = (bf16[8,131,128]{2,0,1:T(8,128)(2,1)}, bf16[8,131,128]{2,0,1:T(8,128)(2,1)}, u32[]{:S(2)}, u32[]{:S(2)}) collective-permute-start(bf16[8,131,128]{2,0,1:T(8,128)(2,1)} %bitcast.118), channel_id=1, source_target_pairs={{0,32},{16,48},{32,0},{48,16},{1,33},{17,49},{33,1},{49,17},{2,34}... | collective-permute-start | bytes 804872 | tf_op jit(solution)/shard_map/ppermute | solution.py:301
  205.7 9.9 %copy-start.8 = (bf16[8,1,131,128]{3,1,0,2:T(2,128)(2,1)S(1)}, bf16[8,1,131,128]{3,1,0,2:T(2,128)(2,1)}, u32[]{:S(2)}) copy-start(bf16[8,1,131,128]{3,1,0,2:T(2,128)(2,1)} %get-tuple-element.41) | copy-start | bytes 804868
  205.7 84.0 %all-to-all-start.3 = ((bf16[16,48,1024]{2,1,0:T(8,128)(2,1)}), bf16[16,48,1024]{2,1,0:T(8,128)(2,1)S(1)}, u32[]{:S(2)}, u32[]{:S(2)}) async-start(bf16[16,48,1024]{2,1,0:T(8,128)(2,1)} %bitcast.17), calls=%async_computation.3 | async-start | bytes 3145728 | tf_op jit(solution)/shard_map/all_to_all | solution.py:412
  215.7 17.1 %collective-permute-start.1 = (bf16[8,131,128]{2,0,1:T(8,128)(2,1)S(1)}, bf16[8,131,128]{2,0,1:T(8,128)(2,1)S(1)}, u32[]{:S(2)}, u32[]{:S(2)}) collective-permute-start(bf16[8,131,128]{2,0,1:T(8,128)(2,1)S(1)} %bitcast.135), channel_id=1, source_target_pairs={{0,16},{16,32},{32,48},{48,0},{1,17},{17,33},{33,49},{49,1},{2,18}... | collective-permute-start | bytes 804872 | tf_op jit(solution)/shard_map/ppermute | solution.py:301
  233.6 24.2 %collective-permute-start.10 = (bf16[4,131,128]{2,0,1:T(4,128)(2,1)S(1)}, bf16[4,131,128]{2,0,1:T(4,128)(2,1)S(1)}, u32[]{:S(2)}, u32[]{:S(2)}) collective-permute-start(bf16[4,131,128]{2,0,1:T(4,128)(2,1)S(1)} %pad_maximum_fusion.8), channel_id=1, source_target_pairs={{0,448},{64,0},{128,64},{192,128},{256,192},{320,256},{384,320},{4... | collective-permute-start | bytes 402440 | tf_op jit(solution)/shard_map/ppermute | solution.py:312
  235.9 27.8 %collective-permute-start.9 = (bf16[4,131,128]{2,0,1:T(4,128)(2,1)S(1)}, bf16[4,131,128]{2,0,1:T(4,128)(2,1)S(1)}, u32[]{:S(2)}, u32[]{:S(2)}) collective-permute-start(bf16[4,131,128]{2,0,1:T(4,128)(2,1)S(1)} %pad_maximum_fusion.7), channel_id=1, source_target_pairs={{0,384},{64,448},{128,0},{192,64},{256,128},{320,192},{384,256},{4... | collective-permute-start | bytes 402440 | tf_op jit(solution)/shard_map/ppermute | solution.py:312
  238.1 31.2 %collective-permute-start.8 = (bf16[4,131,128]{2,0,1:T(4,128)(2,1)S(1)}, bf16[4,131,128]{2,0,1:T(4,128)(2,1)S(1)}, u32[]{:S(2)}, u32[]{:S(2)}) collective-permute-start(bf16[4,131,128]{2,0,1:T(4,128)(2,1)S(1)} %pad_maximum_fusion.6), channel_id=1, source_target_pairs={{0,320},{64,384},{128,448},{192,0},{256,64},{320,128},{384,192},{4... | collective-permute-start | bytes 402440 | tf_op jit(solution)/shard_map/ppermute | solution.py:312
  242.0 30.2 %collective-permute-start.7 = (bf16[4,131,128]{2,0,1:T(4,128)(2,1)S(1)}, bf16[4,131,128]{2,0,1:T(4,128)(2,1)S(1)}, u32[]{:S(2)}, u32[]{:S(2)}) collective-permute-start(bf16[4,131,128]{2,0,1:T(4,128)(2,1)S(1)} %pad_maximum_fusion.5), channel_id=1, source_target_pairs={{0,256},{64,320},{128,384},{192,448},{256,0},{320,64},{384,128},{4... | collective-permute-start | bytes 402440 | tf_op jit(solution)/shard_map/ppermute | solution.py:312
  249.1 26.1 %collective-permute-start.6 = (bf16[4,131,128]{2,0,1:T(4,128)(2,1)S(1)}, bf16[4,131,128]{2,0,1:T(4,128)(2,1)S(1)}, u32[]{:S(2)}, u32[]{:S(2)}) collective-permute-start(bf16[4,131,128]{2,0,1:T(4,128)(2,1)S(1)} %pad_maximum_fusion.4), channel_id=1, source_target_pairs={{0,192},{64,256},{128,320},{192,384},{256,448},{320,0},{384,64},{4... | collective-permute-start | bytes 402440 | tf_op jit(solution)/shard_map/ppermute | solution.py:312
  257.8 20.2 %collective-permute-start.5 = (bf16[4,131,128]{2,0,1:T(4,128)(2,1)S(1)}, bf16[4,131,128]{2,0,1:T(4,128)(2,1)S(1)}, u32[]{:S(2)}, u32[]{:S(2)}) collective-permute-start(bf16[4,131,128]{2,0,1:T(4,128)(2,1)S(1)} %pad_maximum_fusion.3), channel_id=1, source_target_pairs={{0,128},{64,192},{128,256},{192,320},{256,384},{320,448},{384,0},{... | collective-permute-start | bytes 402440 | tf_op jit(solution)/shard_map/ppermute | solution.py:312
  263.7 17.1 %collective-permute-start.4 = (bf16[4,131,128]{2,0,1:T(4,128)(2,1)S(1)}, bf16[4,131,128]{2,0,1:T(4,128)(2,1)S(1)}, u32[]{:S(2)}, u32[]{:S(2)}) collective-permute-start(bf16[4,131,128]{2,0,1:T(4,128)(2,1)S(1)} %pad_maximum_fusion.2), channel_id=1, source_target_pairs={{0,64},{64,128},{128,192},{192,256},{256,320},{320,384},{384,448},... | collective-permute-start | bytes 402440 | tf_op jit(solution)/shard_map/ppermute | solution.py:312
  283.8 5.9 %copy-start.14 = (s32[128]{0:T(128)S(1)}, s32[128]{0:T(128)}, u32[]{:S(2)}) copy-start(s32[128]{0:T(128)} %copy-done.13) | copy-start | bytes 1540
  288.2 1.9 copy-start.18
  290.1 0.6 copy-start.17
  290.6 0.6 copy-start.12
  291.2 0.7 copy-start.20
Sparse Core Ops, SparseCore 0:
  10.1 166.3 all-gather.1

commit v3 on v2

--- a/solution.py
+++ b/solution.py
@@ -25,6 +25,7 @@
 def mixer_kernel(
     head_size,
     length_ref,
+    row_ref,
     x_ref,
     prior_ref,
     conv_ref,
@@ -35,8 +36,7 @@
     step_ref,
     rate_ref,
     base_ref,
-    state_grad_ref,
-    taps_grad_ref,
+    sent_ref,
     grow_ref,
     series_ref,
     scores_ref,
@@ -85,7 +85,7 @@
     high = scaled.astype(jnp.bfloat16)
     low = (scaled - high.astype(jnp.float32)).astype(jnp.bfloat16)
     c_rows = c_ref[...]
-    state_grad_ref[...] = (
+    state_grad = (
         lax.dot_general(high, c_rows, down, preferred_element_type=jnp.float32)
         + lax.dot_general(low, c_rows, down, preferred_element_type=jnp.float32)
     ).astype(jnp.bfloat16)
@@ -94,51 +94,69 @@
     gate = jax.nn.sigmoid(summed[:early])
     series_grad = conv_grad * gate * (1.0 + summed[:early] * (1.0 - gate))
     one, two, three = (series_grad[k : k + 1] for k in range(3))
-    taps_grad_ref[...] = jnp.zeros_like(taps_grad_ref)
-    taps_grad_ref[0:1] = taps[0] * one
-    taps_grad_ref[1:2] = taps[1] * one + taps[0] * two
-    taps_grad_ref[2:3] = taps[2] * one + taps[1] * two + taps[0] * three
+    places = sent_ref.shape[0]
+    lanes = width // places
+    taps_rows = sent_ref.shape[2] - lanes
+    taps_grad = jnp.concatenate(
+        [
+            taps[0] * one,
+            taps[1] * one + taps[0] * two,
+            taps[2] * one + taps[1] * two + taps[0] * three,
+            jnp.zeros((taps_rows - 3, width), jnp.float32),
+        ],
+        0,
+    ).astype(jnp.bfloat16)
+    for k in range(places):
+        sent_ref[k, 0, :lanes] = state_grad[k * lanes : (k + 1) * lanes]
+        sent_ref[k, 0, lanes:] = taps_grad[:, k * lanes : (k + 1) * lanes]
 
 
 def mixer_base(
-    length, x_rows, prior, conv_weight, skip, grads, b_rows, c_rows, step_size, rate, head_size, block=512
+    length, row, x_rows, prior, conv_weight, skip, grads, b_rows, c_rows, step_size, rate, head_size, owners
 ):
     steps_n, channels = x_rows.shape
     heads, state_n = step_size.shape[1], c_rows.shape[1]
-    whole = lambda *shape: pl.BlockSpec(shape, lambda i: (0,) * len(shape))
-    part = lambda rows: pl.BlockSpec((rows, block), lambda i: (0, i))
+    owners_y, owners_x = owners
+    lanes = channels // (owners_y * owners_x)
+    block = owners_x * lanes
+    whole = lambda *shape: pl.BlockSpec(shape, lambda i, *_: (0,) * len(shape))
+    part = lambda rows: pl.BlockSpec((rows, block), lambda i, *_: (0, i))
+    sent = (owners_x, owners_y, lanes + 16, state_n)
     return pl.pallas_call(
         functools.partial(mixer_kernel, head_size),
-        grid=(channels // block,),
-        in_specs=[
-            pl.BlockSpec(memory_space=pltpu.SMEM),
-            part(steps_n),
-            part(8),
-            part(4),
-            part(1),
-            part(steps_n),
-            whole(steps_n, state_n),
-            whole(steps_n, state_n),
-            whole(steps_n, heads),
-            whole(1, heads),
-        ],
-        out_specs=[
-            part(steps_n),
-            pl.BlockSpec((block, state_n), lambda i: (i, 0)),
-            part(8),
-            whole(steps_n, heads),
-        ],
+        grid_spec=pltpu.PrefetchScalarGridSpec(
+            num_scalar_prefetch=2,
+            grid=(owners_y,),
+            in_specs=[
+                part(steps_n),
+                part(8),
+                part(4),
+                part(1),
+                part(steps_n),
+                whole(steps_n, state_n),
+                whole(steps_n, state_n),
+                whole(steps_n, heads),
+                whole(1, heads),
+            ],
+            out_specs=[
+                part(steps_n),
+                pl.BlockSpec(
+                    (owners_x, 1, lanes + 16, state_n),
+                    lambda i, _, row_ref: (0, lax.rem(i - row_ref[0] + owners_y, owners_y), 0, 0),
+                ),
+                whole(steps_n, heads),
+            ],
+            scratch_shapes=[
+                pltpu.VMEM((8 + steps_n, block), jnp.float32),
+                pltpu.VMEM((steps_n, steps_n), jnp.float32),
+                pltpu.VMEM((8, steps_n), jnp.float32),
+                pltpu.VMEM((steps_n, heads), jnp.float32),
+            ],
+        ),
         out_shape=[
             jax.ShapeDtypeStruct((steps_n, channels), jnp.float32),
-            jax.ShapeDtypeStruct((channels, state_n), jnp.bfloat16),
-            jax.ShapeDtypeStruct((8, channels), jnp.float32),
+            jax.ShapeDtypeStruct(sent, jnp.bfloat16),
             jax.ShapeDtypeStruct((steps_n, heads), jnp.float32),
-        ],
-        scratch_shapes=[
-            pltpu.VMEM((8 + steps_n, block), jnp.float32),
-            pltpu.VMEM((steps_n, steps_n), jnp.float32),
-            pltpu.VMEM((8, steps_n), jnp.float32),
-            pltpu.VMEM((steps_n, heads), jnp.float32),
         ],
         compiler_params=pltpu.CompilerParams(vmem_limit_bytes=32 * 1024 * 1024),
         cost_estimate=pl.CostEstimate(
@@ -146,7 +164,7 @@
             bytes_accessed=10 * steps_n * channels,
             transcendentals=steps_n * channels,
         ),
-    )(length, x_rows, prior, conv_weight, skip, grads, b_rows, c_rows, step_size, rate)
+    )(length, row, x_rows, prior, conv_weight, skip, grads, b_rows, c_rows, step_size, rate)
 
 
 def dispatch_kernel(
@@ -291,33 +309,39 @@
     )(rows, weights)
 
 
-def deliver(parts, members):
-    y, x = lax.axis_index("y"), lax.axis_index(("xh", "xl"))
-    size_y, size_x = parts.shape[:2]
-    column = []
-    for step in range(size_x):
-        piece = lax.dynamic_index_in_dim(parts, (x + step) % size_x, 1, keepdims=False)
-        if step:
-            piece = lax.ppermute(
-                piece, ("xh", "xl"), [(i, (i + step) % size_x) for i in range(size_x)]
-            )
-        column.append(piece)
-    total = None
+def collect_kernel(row_ref, members_ref, *refs):
+    pieces, state_ref, taps_ref, total_ref = refs[:-3], *refs[-3:]
+    size_y, size_x = len(pieces), pieces[0].shape[0]
+    lanes = state_ref.shape[1]
+    total_ref[...] = jnp.zeros_like(total_ref)
     for step in range(size_y):
-        there = (y + step) % size_y
-        piece = jnp.stack(
-            [lax.dynamic_index_in_dim(block, there, 0, keepdims=False) for block in column], 0
-        )
-        if step:
-            piece = lax.ppermute(piece, "y", [(i, (i + step) % size_y) for i in range(size_y)])
+        source = lax.rem(row_ref[0] - step + size_y, size_y)
         for k in range(size_x):
-            second = lax.dynamic_index_in_dim(
-                members, (y - step) % size_y * size_x + (x - k) % size_x, 0, keepdims=False
-            )
-            value = piece[k].astype(jnp.float32)
-            both = jnp.stack([jnp.where(second, 0.0, value), jnp.where(second, value, 0.0)])
-            total = both if total is None else total + both
-    return total
+            member = members_ref[source * size_x + k]
+            total_ref[member] += pieces[step][k].astype(jnp.float32)
+    state_ref[...] = total_ref[:, :lanes]
+    taps_ref[...] = total_ref[:, lanes:]
+
+
+def collect(row, members, pieces, prompts):
+    size_x, rows, lanes = pieces[0].shape
+    vmem, smem = pl.BlockSpec(memory_space=pltpu.VMEM), pl.BlockSpec(memory_space=pltpu.SMEM)
+    return pl.pallas_call(
+        collect_kernel,
+        in_specs=[smem, smem] + [vmem] * len(pieces),
+        out_specs=[vmem, vmem],
+        out_shape=[
+            jax.ShapeDtypeStruct((prompts, rows - 16, lanes), jnp.float32),
+            jax.ShapeDtypeStruct((prompts, 16, lanes), jnp.float32),
+        ],
+        scratch_shapes=[pltpu.VMEM((prompts, rows, lanes), jnp.float32)],
+        compiler_params=pltpu.CompilerParams(vmem_limit_bytes=16 * 1024 * 1024),
+        cost_estimate=pl.CostEstimate(
+            flops=len(pieces) * size_x * rows * lanes,
+            bytes_accessed=2 * len(pieces) * size_x * rows * lanes,
+            transcendentals=0,
+        ),
+    )(row, members, *pieces)
 
 
 def shards(
@@ -352,6 +376,8 @@
     )
     weights = lax.all_gather(swapped, ("y", "xl", "c"), axis=1, tiled=True)
 
+    row = lax.axis_index("y").astype(jnp.int32)[None]
+
     own_taps = jnp.transpose(
         prompt_taps.reshape(prompts, own_heads, taps_n, head_size), (0, 2, 1, 3)
     ).reshape(prompts * taps_n, lanes)
@@ -373,8 +399,9 @@
     state = lax.all_to_all(outgoing_state, PLANE, 0, 0, tiled=True).reshape(row_width, state_n)
 
     step_size = jax.nn.softplus(step_raw)
-    base, grad_s, grad_t, grow = mixer_base(
+    base, outgoing_grad, grow = mixer_base(
         lengths,
+        row,
         ssm_input,
         prior,
         conv_weight,
@@ -385,14 +412,10 @@
         step_size,
         decay_rate[None, :],
         head_size,
-    )
-    outgoing_grad = jnp.concatenate(
-        [
-            grad_s.reshape(owners, state_rows, state_n),
-            jnp.transpose(grad_t[:taps_n].astype(jnp.bfloat16).reshape(taps_n, owners, lanes), (1, 0, 2)),
-        ],
-        1,
-    )
+        (lax.axis_size("y"), lax.axis_size(("xh", "xl"))),
+    )
+    column_grad = lax.all_to_all(outgoing_grad, ("xh", "xl"), 0, 0, tiled=True)
+
     slots = 3 * steps_n // (2 * expert_count)
     width = row_width // GROUPS
     chosen = expert_index[:, 0]
@@ -407,8 +430,8 @@
         outgoing.reshape(lines, GROUPS * slots, width), LINE, 0, 0, tiled=True
     )
     expert_rows = unpack(arrived.reshape(packed_rows, width), slots, lines)
-    weights, outgoing_grad = lax.optimization_barrier((weights, outgoing_grad))
     produced = expert_apply(expert_rows, weights, slots, lines)
+    produced, column_grad = lax.optimization_barrier((produced, column_grad))
     returned = lax.all_to_all(
         produced.reshape(lines, GROUPS * slots, width), LINE, 0, 0, tiled=True
     ).reshape(packed_rows, width)
@@ -425,12 +448,15 @@
         ],
         1,
     )
-    summed = deliver(
-        outgoing_grad.reshape(lax.axis_size("y"), -1, state_rows + taps_n, lanes), members
-    )
-    state_grad = summed[:, :state_rows].reshape(prompts, own_heads, head_size, state_n)
+    size_y = lax.axis_size("y")
+    pieces = [column_grad[:, 0]] + [
+        lax.ppermute(column_grad[:, d], "y", [(i, (i + d) % size_y) for i in range(size_y)])
+        for d in range(1, size_y)
+    ]
+    state_sum, taps_sum = collect(row, members.astype(jnp.int32), pieces, prompts)
+    state_grad = state_sum.reshape(prompts, own_heads, head_size, state_n)
     taps_grad = jnp.transpose(
-        summed[:, state_rows:].reshape(prompts, taps_n, own_heads, head_size), (0, 2, 1, 3)
+        taps_sum[:, :taps_n].reshape(prompts, taps_n, own_heads, head_size), (0, 2, 1, 3)
     ).reshape(prompts, own_heads, taps_n * head_size)
     moe_out = (route_gain * per_token).astype(jnp.bfloat16)
     return (moe_out, state_grad, taps_grad)

time: 304 us -> 269 us (0.88)
  blocking collectives: 0 us -> 47.4 us
  other arithmetic: 39.8 us -> 4.46 us
  starting transfers between devices: 84.8 us -> 65.7 us
  local copies, waits for them, and re-layouts: 20.8 us -> 6.98 us
  waiting for transfers between devices: 104 us -> 92 us
    all_to_all x0 -> x1, blocking collectives: none -> 47.4 us  [shards(): lax.all_to_all(outgoing.reshape(lines, GROUPS * slots, width), LINE, 0, 0...]
    all_to_all x1, waiting for transfers between devices: 30.5 us -> 0.01 us  [shards(): column_grad = lax.all_to_all(outgoing_grad, ('xh', 'xl'), 0, 0, tiled=True)]
    select_n x12 -> x0, other arithmetic: 26.5 us -> none  [the longest x11 24.9 us: deliver(): jnp.where(second, 0.0, value)]
    dynamic_slice x7 -> x0, local copies, waits for them, and re-layouts: 11.2 us -> none  [the longest x4 5.22 us: deliver(): lax.dynamic_index_in_dim(block, there, 0, keepdims=False)]
    all_gather x1, waiting for transfers between devices: 34 us -> 44.5 us  [shards(): weights = lax.all_gather(swapped, ('y', 'xl', 'c'), axis=1, tiled=True)]
    ppermute x10 -> x7, starting transfers between devices: 33.4 us -> 23.4 us  [shards(): lax.ppermute(column_grad[:, d], 'y', [(i, (i + d) % size_y) for i in rang...]
    all_to_all x1, starting transfers between devices: 13 us -> 4.27 us  [shards(): column_grad = lax.all_to_all(outgoing_grad, ('xh', 'xl'), 0, 0, tiled=True)]
    ppermute x10 -> x7, waiting for transfers between devices: 10.4 us -> 17.8 us  [shards(): lax.ppermute(column_grad[:, d], 'y', [(i, (i + d) % size_y) for i in rang...]
  transfers between devices with their start and end apart: 16 -> 13, of which waited for: 5 -> 6; matrix products, arithmetic and copies ran while one was open for 16% -> 2% of each run, Pallas kernels for 11% -> 12%
where the time goes in v3:
time: 269 us; the launch traced here: 267 us
  waiting for transfers between devices  92 us (34%)
  starting transfers between devices  65.7 us (24%)
  blocking collectives  47.4 us (18%)
  Pallas kernels  32.9 us (12%)
  between operations  15.8 us (6%)
  local copies, waits for them, and re-layouts  6.98 us (3%)
  other arithmetic  4.46 us (2%)
    all_to_all x1, blocking collectives, shards(): lax.all_to_all(outgoing.reshape(lines, GROUPS * slots, width), LINE, 0, 0...  47.4 us
    all_gather x1, waiting for transfers between devices, shards(): weights = lax.all_gather(swapped, ('y', 'xl', 'c'), axis=1, tiled=True)  44.5 us
    ppermute x7, starting transfers between devices, shards(): lax.ppermute(column_grad[:, d], 'y', [(i, (i + d) % size_y) for i in rang...  23.4 us
    all_to_all x1, waiting for transfers between devices, shards(): lax.all_to_all(outgoing_state, PLANE, 0, 0, tiled=True)  22.9 us
    all_to_all x1, starting transfers between devices, shards(): lax.all_to_all(jnp.broadcast_to(notice[None], (owners,) + notice.shape),...  21.5 us
    ppermute x7, waiting for transfers between devices, shards(): lax.ppermute(column_grad[:, d], 'y', [(i, (i + d) % size_y) for i in rang...  17.8 us
    pallas_call x1, Pallas kernels, expert_apply(): pl.pallas_call(functools.partial(expert_kernel, slots, sources), grid=(un...  13.1 us
    pallas_call x1, Pallas kernels, mixer_base(): pl.pallas_call(functools.partial(mixer_kernel, head_size), grid_spec=pltp...  10.6 us
  transfers between devices with their start and end apart: 13, of which 6 were waited for; matrix products, arithmetic and copies ran while one was open for 2% of the time, Pallas kernels for 12%

profile of v3, /device:TPU:56, one launch (start us, length us, event | category | flops | bytes accessed | tf_op | source)
XLA Modules:
  0.0 266.9 jit_solution(3215162043186418119)
XLA Ops:
  7.2 0.0 all-gather.2.cloned.1.call-start
  7.3 1.2 pad_maximum_fusion
  8.4 0.7 collective-permute-start
  9.1 0.0 collective-permute-done
  9.2 0.8 copy-done.6
  10.0 0.0 all-gather.2.cloned.1.call-update
  10.7 0.1 reshape.230
  10.8 0.1 reshape.231
  10.9 0.1 pad.10.clone
  10.9 0.1 pad.11.clone
  11.0 0.1 maximum_maximum_fusion
  11.1 0.6 broadcast_in_dim.69
  11.7 21.5 %all-to-all-start = ((bf16[32,8,128]{2,1,0:T(8,128)(2,1)}), bf16[32,8,128]{2,1,0:T(8,128)(2,1)S(1)}, u32[]{:S(2)}, u32[]{:S(2)}) async-start(bf16[32,8,128]{2,1,0:T(8,128)(2,1)} %broadcast_in_dim.69), calls=%async_computation | async-start | bytes 131072 | tf_op jit(solution)/shard_map/all_to_all | solution.py:388
  33.9 0.1 copy.71
  34.1 0.1 broadcast_in_dim.70
  34.1 0.1 broadcast_in_dim_reshape.3.skip_ref
  34.2 6.8 %all-to-all-done = bf16[32,8,128]{2,1,0:T(8,128)(2,1)S(1)} async-done(((bf16[32,8,128]{2,1,0:T(8,128)(2,1)}), bf16[32,8,128]{2,1,0:T(8,128)(2,1)S(1)}, u32[]{:S(2)}, u32[]{:S(2)}) %all-to-all-start) | async-done | bytes 65568 | tf_op jit(solution)/shard_map/all_to_all | solution.py:388
  41.0 0.7 compare_reduce_fusion
  41.7 0.0 copy-start
  41.7 0.0 copy-start.3
  41.7 0.0 copy-start.4
  41.7 0.0 copy-start.5
  41.7 1.1 broadcast_select_fusion
  42.8 6.2 %all-to-all-start.1 = ((bf16[32,128,128]{2,1,0:T(8,128)(2,1)}), bf16[32,128,128]{2,1,0:T(8,128)(2,1)S(1)}, u32[]{:S(2)}, u32[]{:S(2)}) async-start(bf16[32,128,128]{2,1,0:T(8,128)(2,1)} %broadcast_select_fusion), calls=%async_computation.1 | async-start | bytes 2097152 | tf_op jit(solution)/shard_map/all_to_all | solution.py:399
  49.1 0.1 convert_reduce_fusion
  49.3 0.0 copy-start.1
  49.3 1.2 copy-done.1
  50.6 1.2 copy-done.2
  51.8 10.6 %shard_map.184 = (f32[128,4096]{1,0:T(8,128)S(1)}, bf16[4,8,144,128]{3,2,1,0:T(8,128)(2,1)}, f32[128,64]{1,0:T(8,128)S(1)}) custom-call(s32[1]{0:T(128)S(6)} %copy.89.length_ref, s32[1]{0:T(128)} %bitcast.2.row_ref, bf16[128,4096]{1,0:T(8,128)(2,1)S(1)} %copy-done.1, f32[8,4096]{1,0:T(8,128)S(1)} %pad_convert_fusion.prior_ref, f32[4,4096]{1,0:T(4,128)S(1)} %copy-done.3, ...), custom_call_target="tpu_custom_call" | custom-call | flops 1342177280 | bytes 5242880 | tf_op jit(solution)/shard_map/pallas_call | solution.py:125
  62.4 22.9 %all-to-all-done.1 = bf16[32,128,128]{2,1,0:T(8,128)(2,1)S(1)} async-done(((bf16[32,128,128]{2,1,0:T(8,128)(2,1)}), bf16[32,128,128]{2,1,0:T(8,128)(2,1)S(1)}, u32[]{:S(2)}, u32[]{:S(2)}) %all-to-all-start.1) | async-done | bytes 1048608 | tf_op jit(solution)/shard_map/all_to_all | solution.py:399
  85.3 5.6 %shard_map.185 = bf16[768,1024]{1,0:T(8,128)(2,1)S(1)} custom-call(s32[1]{0:T(128)S(6)} %copy.89.length_ref, f32[128,4096]{1,0:T(8,128)S(1)} %get-tuple-element.10.base_ref, bf16[4096,128]{1,0:T(8,128)(2,1)S(1)} %bitcast.63, bf16[128,128]{1,0:T(8,128)(2,1)S(1)} %copy-done, f32[128,64]{1,0:T(8,128)S(1)} %get-tuple-element.11.grow_ref, ...), custom_call_target="tpu_custom_call" | custom-call | flops 939524096 | bytes 4718592 | tf_op jit(solution)/shard_map/pallas_call | solution.py:202
  90.9 47.4 %all_to_all.25 = bf16[16,48,1024]{2,1,0:T(8,128)(2,1)S(1)} all-to-all(bf16[16,48,1024]{2,1,0:T(8,128)(2,1)S(1)} %bitcast.62), channel_id=1, replica_groups=mesh['y'=8,'xh'=2,'xl'=2,'z'=8,'c'=2] {'xh','z'}, dimensions={0} | all-to-all | bytes 3145728 | tf_op jit(solution)/shard_map/all_to_all | solution.py:429
  138.3 4.3 %all-to-all-start.3 = ((bf16[4,8,144,128]{3,2,1,0:T(8,128)(2,1)}), bf16[4,8,144,128]{3,2,1,0:T(8,128)(2,1)}, u32[]{:S(2)}, u32[]{:S(2)}) async-start(bf16[4,8,144,128]{3,2,1,0:T(8,128)(2,1)} %get-tuple-element.12), calls=%async_computation.3 | async-start | bytes 2359296 | tf_op jit(solution)/shard_map/all_to_all | solution.py:417
  142.5 2.1 shard_map.186.rows_ref
  144.6 44.5 %all-gather.2.cloned.1.call-done.weight_ref = bf16[3,768,4096]{2,1,0:T(8,128)(2,1)} async-done(((bf16[3,24,4096]{2,1,0:T(8,128)(2,1)}), bf16[3,768,4096]{2,1,0:T(8,128)(2,1)}) %all-gather.2.cloned.1.call-update) | async-done | bytes 18874384 | tf_op jit(solution)/shard_map/all_gather | solution.py:377
  189.2 13.1 %shard_map.187 = bf16[768,1024]{1,0:T(8,128)(2,1)} custom-call(bf16[192,4096]{1,0:T(8,128)(2,1)S(1)} %shard_map.186.rows_ref, bf16[3,768,4096]{2,1,0:T(8,128)(2,1)} %all-gather.2.cloned.1.call-done.weight_ref), custom_call_target="tpu_custom_call" | custom-call | flops 3623878656 | bytes 22020096 | tf_op jit(solution)/shard_map/pallas_call | solution.py:293
  202.3 0.0 all-to-all-done.3
  202.3 9.6 %all-to-all-start.4 = ((bf16[16,48,1024]{2,1,0:T(8,128)(2,1)}), bf16[16,48,1024]{2,1,0:T(8,128)(2,1)S(1)}, u32[]{:S(2)}, u32[]{:S(2)}) async-start(bf16[16,48,1024]{2,1,0:T(8,128)(2,1)} %bitcast.16), calls=%async_computation.4 | async-start | bytes 3145728 | tf_op jit(solution)/shard_map/all_to_all | solution.py:435
  211.9 1.4 slice_bitcast_fusion
  213.4 2.3 collective-permute-start.1
  215.6 1.9 collective-permute-start.2
  217.6 3.1 %collective-permute-start.3 = (bf16[4,144,128]{2,1,0:T(8,128)(2,1)S(1)}, bf16[4,144,128]{2,1,0:T(8,128)(2,1)S(1)}, u32[]{:S(2)}, u32[]{:S(2)}) collective-permute-start(bf16[4,144,128]{2,1,0:T(8,128)(2,1)S(1)} %get-tuple-element.23), channel_id=1, source_target_pairs={{0,192},{64,256},{128,320},{192,384},{256,448},{320,0},{384,64},{4... | collective-permute-start | bytes 442376 | tf_op jit(solution)/shard_map/ppermute | solution.py:453
  220.7 6.8 %collective-permute-start.4 = (bf16[4,144,128]{2,1,0:T(8,128)(2,1)S(1)}, bf16[4,144,128]{2,1,0:T(8,128)(2,1)S(1)}, u32[]{:S(2)}, u32[]{:S(2)}) collective-permute-start(bf16[4,144,128]{2,1,0:T(8,128)(2,1)S(1)} %get-tuple-element.22), channel_id=1, source_target_pairs={{0,256},{64,320},{128,384},{192,448},{256,0},{320,64},{384,128},{4... | collective-permute-start | bytes 442376 | tf_op jit(solution)/shard_map/ppermute | solution.py:453
  227.6 3.2 %collective-permute-start.5 = (bf16[4,144,128]{2,1,0:T(8,128)(2,1)S(1)}, bf16[4,144,128]{2,1,0:T(8,128)(2,1)S(1)}, u32[]{:S(2)}, u32[]{:S(2)}) collective-permute-start(bf16[4,144,128]{2,1,0:T(8,128)(2,1)S(1)} %get-tuple-element.21), channel_id=1, source_target_pairs={{0,320},{64,384},{128,448},{192,0},{256,64},{320,128},{384,192},{4... | collective-permute-start | bytes 442376 | tf_op jit(solution)/shard_map/ppermute | solution.py:453
  230.8 0.0 collective-permute-done.1.refs_1_
  230.8 3.5 %collective-permute-start.6 = (bf16[4,144,128]{2,1,0:T(8,128)(2,1)S(1)}, bf16[4,144,128]{2,1,0:T(8,128)(2,1)S(1)}, u32[]{:S(2)}, u32[]{:S(2)}) collective-permute-start(bf16[4,144,128]{2,1,0:T(8,128)(2,1)S(1)} %get-tuple-element.20), channel_id=1, source_target_pairs={{0,384},{64,448},{128,0},{192,64},{256,128},{320,192},{384,256},{4... | collective-permute-start | bytes 442376 | tf_op jit(solution)/shard_map/ppermute | solution.py:453
  234.3 0.0 collective-permute-done.2.refs_2_
  234.3 2.5 collective-permute-start.7
  236.8 0.1 collective-permute-done.3.refs_3_
  237.0 0.0 collective-permute-done.4.refs_4_
  237.0 11.9 %collective-permute-done.5.refs_5_ = bf16[4,144,128]{2,1,0:T(8,128)(2,1)S(1)} collective-permute-done((bf16[4,144,128]{2,1,0:T(8,128)(2,1)S(1)}, bf16[4,144,128]{2,1,0:T(8,128)(2,1)S(1)}, u32[]{:S(2)}, u32[]{:S(2)}) %collective-permute-start.5) | collective-permute-done | bytes 147488 | tf_op jit(solution)/shard_map/ppermute | solution.py:453
  248.9 0.0 collective-permute-done.6.refs_6_
  248.9 5.7 %collective-permute-done.7.refs_7_ = bf16[4,144,128]{2,1,0:T(8,128)(2,1)S(1)} collective-permute-done((bf16[4,144,128]{2,1,0:T(8,128)(2,1)S(1)}, bf16[4,144,128]{2,1,0:T(8,128)(2,1)S(1)}, u32[]{:S(2)}, u32[]{:S(2)}) %collective-permute-start.7) | collective-permute-done | bytes 147488 | tf_op jit(solution)/shard_map/ppermute | solution.py:453
  254.6 1.5 shard_map.188
  256.1 0.1 reshape.238
  256.2 0.7 reshape.239
  256.9 0.0 all-to-all-done.4
  256.9 0.4 fusion.1
  257.3 0.4 fusion.3
  257.7 0.4 fusion.4
  258.2 0.0 copy-start.12
  258.2 0.4 fusion.2
  258.6 0.2 copy-done.12
  258.8 1.2 fusion
  (28 shorter events, 0.2 us)
Async XLA Ops:
  7.2 3.5 %copy-start.9 = (bf16[2,2,192]{2,1,0:T(2,128)(2,1)S(1)}, bf16[2,2,192]{2,1,0:T(2,128)(2,1)}, u32[]{:S(2)}) copy-start(bf16[2,2,192]{2,1,0:T(2,128)(2,1)} %param.25) | copy-start | bytes 4612
  7.2 26.8 %copy-start.8 = (f32[128,64]{0,1:T(8,128)S(1)}, f32[128,64]{0,1:T(8,128)}, u32[]{:S(2)}) copy-start(f32[128,64]{0,1:T(8,128)} %param.20) | copy-start | bytes 98308
  7.2 26.9 %copy-start.10 = (f32[64]{0:T(128)S(1)}, f32[64]{0:T(128)}, u32[]{:S(2)}) copy-start(f32[64]{0:T(128)} %param.22) | copy-start | bytes 772
  7.2 27.0 %copy-start.7 = (bf16[2,2,64,128]{3,2,1,0:T(8,128)(2,1)S(1)}, bf16[2,2,64,128]{3,2,1,0:T(8,128)(2,1)}, u32[]{:S(2)}) copy-start(bf16[2,2,64,128]{3,2,1,0:T(8,128)(2,1)} %param.24) | copy-start | bytes 196612
  7.2 182.0 %all-gather.2.cloned.1.call-start = ((), (), s32[]{:S(2)}) async-start(), calls=%async_computation.5 | async-start | bytes 19464192 | tf_op jit(solution)/shard_map/all_gather | solution.py:377
  8.4 0.7 collective-permute-start
  9.2 0.8 copy-start.6
  11.7 29.3 %all-to-all-start = ((bf16[32,8,128]{2,1,0:T(8,128)(2,1)}), bf16[32,8,128]{2,1,0:T(8,128)(2,1)S(1)}, u32[]{:S(2)}, u32[]{:S(2)}) async-start(bf16[32,8,128]{2,1,0:T(8,128)(2,1)} %broadcast_in_dim.69), calls=%async_computation | async-start | bytes 131072 | tf_op jit(solution)/shard_map/all_to_all | solution.py:388
  41.7 7.4 %copy-start.11 = (s32[128,1]{0,1:T(1,128)S(1)}, s32[128,1]{0,1:T(1,128)}, u32[]{:S(2)}) copy-start(s32[128,1]{0,1:T(1,128)} %param.29) | copy-start | bytes 1540
  41.7 7.6 %copy-start = (bf16[128,128]{1,0:T(8,128)(2,1)S(1)}, bf16[128,128]{1,0:T(8,128)(2,1)}, u32[]{:S(2)}) copy-start(bf16[128,128]{1,0:T(8,128)(2,1)} %c_ref.3) | copy-start | bytes 98308
  41.7 7.6 %copy-start.3 = (f32[4,4096]{1,0:T(4,128)S(1)}, f32[4,4096]{1,0:T(4,128)}, u32[]{:S(2)}) copy-start(f32[4,4096]{1,0:T(4,128)} %conv_ref.1) | copy-start | bytes 196612
  41.7 7.6 %copy-start.4 = (bf16[128,128]{1,0:T(8,128)(2,1)S(1)}, bf16[128,128]{1,0:T(8,128)(2,1)}, u32[]{:S(2)}) copy-start(bf16[128,128]{1,0:T(8,128)(2,1)} %b_ref.1) | copy-start | bytes 98308
  41.7 7.6 %copy-start.5 = (f32[64]{0:T(128)S(1)}, f32[64]{0:T(128)}, u32[]{:S(2)}) copy-start(f32[64]{0:T(128)} %param.21) | copy-start | bytes 772
  42.8 42.4 %all-to-all-start.1 = ((bf16[32,128,128]{2,1,0:T(8,128)(2,1)}), bf16[32,128,128]{2,1,0:T(8,128)(2,1)S(1)}, u32[]{:S(2)}, u32[]{:S(2)}) async-start(bf16[32,128,128]{2,1,0:T(8,128)(2,1)} %broadcast_select_fusion), calls=%async_computation.1 | async-start | bytes 2097152 | tf_op jit(solution)/shard_map/all_to_all | solution.py:399
  49.3 1.2 copy-start.1
  50.6 1.2 copy-start.2
  138.3 64.1 %all-to-all-start.3 = ((bf16[4,8,144,128]{3,2,1,0:T(8,128)(2,1)}), bf16[4,8,144,128]{3,2,1,0:T(8,128)(2,1)}, u32[]{:S(2)}, u32[]{:S(2)}) async-start(bf16[4,8,144,128]{3,2,1,0:T(8,128)(2,1)} %get-tuple-element.12), calls=%async_computation.3 | async-start | bytes 2359296 | tf_op jit(solution)/shard_map/all_to_all | solution.py:417
  202.3 54.6 %all-to-all-start.4 = ((bf16[16,48,1024]{2,1,0:T(8,128)(2,1)}), bf16[16,48,1024]{2,1,0:T(8,128)(2,1)S(1)}, u32[]{:S(2)}, u32[]{:S(2)}) async-start(bf16[16,48,1024]{2,1,0:T(8,128)(2,1)} %bitcast.16), calls=%async_computation.4 | async-start | bytes 3145728 | tf_op jit(solution)/shard_map/all_to_all | solution.py:435
  213.4 17.4 %collective-permute-start.1 = (bf16[4,144,128]{2,1,0:T(8,128)(2,1)S(1)}, bf16[4,144,128]{2,1,0:T(8,128)(2,1)S(1)}, u32[]{:S(2)}, u32[]{:S(2)}) collective-permute-start(bf16[4,144,128]{2,1,0:T(8,128)(2,1)S(1)} %get-tuple-element.25), channel_id=1, source_target_pairs={{0,64},{64,128},{128,192},{192,256},{256,320},{320,384},{384,448},... | collective-permute-start | bytes 442376 | tf_op jit(solution)/shard_map/ppermute | solution.py:453
  215.6 18.7 %collective-permute-start.2 = (bf16[4,144,128]{2,1,0:T(8,128)(2,1)S(1)}, bf16[4,144,128]{2,1,0:T(8,128)(2,1)S(1)}, u32[]{:S(2)}, u32[]{:S(2)}) collective-permute-start(bf16[4,144,128]{2,1,0:T(8,128)(2,1)S(1)} %get-tuple-element.24), channel_id=1, source_target_pairs={{0,128},{64,192},{128,256},{192,320},{256,384},{320,448},{384,0},{... | collective-permute-start | bytes 442376 | tf_op jit(solution)/shard_map/ppermute | solution.py:453
  217.6 19.4 %collective-permute-start.3 = (bf16[4,144,128]{2,1,0:T(8,128)(2,1)S(1)}, bf16[4,144,128]{2,1,0:T(8,128)(2,1)S(1)}, u32[]{:S(2)}, u32[]{:S(2)}) collective-permute-start(bf16[4,144,128]{2,1,0:T(8,128)(2,1)S(1)} %get-tuple-element.23), channel_id=1, source_target_pairs={{0,192},{64,256},{128,320},{192,384},{256,448},{320,0},{384,64},{4... | collective-permute-start | bytes 442376 | tf_op jit(solution)/shard_map/ppermute | solution.py:453
  220.7 16.2 %collective-permute-start.4 = (bf16[4,144,128]{2,1,0:T(8,128)(2,1)S(1)}, bf16[4,144,128]{2,1,0:T(8,128)(2,1)S(1)}, u32[]{:S(2)}, u32[]{:S(2)}) collective-permute-start(bf16[4,144,128]{2,1,0:T(8,128)(2,1)S(1)} %get-tuple-element.22), channel_id=1, source_target_pairs={{0,256},{64,320},{128,384},{192,448},{256,0},{320,64},{384,128},{4... | collective-permute-start | bytes 442376 | tf_op jit(solution)/shard_map/ppermute | solution.py:453
  227.6 21.4 %collective-permute-start.5 = (bf16[4,144,128]{2,1,0:T(8,128)(2,1)S(1)}, bf16[4,144,128]{2,1,0:T(8,128)(2,1)S(1)}, u32[]{:S(2)}, u32[]{:S(2)}) collective-permute-start(bf16[4,144,128]{2,1,0:T(8,128)(2,1)S(1)} %get-tuple-element.21), channel_id=1, source_target_pairs={{0,320},{64,384},{128,448},{192,0},{256,64},{320,128},{384,192},{4... | collective-permute-start | bytes 442376 | tf_op jit(solution)/shard_map/ppermute | solution.py:453
  230.8 18.1 %collective-permute-start.6 = (bf16[4,144,128]{2,1,0:T(8,128)(2,1)S(1)}, bf16[4,144,128]{2,1,0:T(8,128)(2,1)S(1)}, u32[]{:S(2)}, u32[]{:S(2)}) collective-permute-start(bf16[4,144,128]{2,1,0:T(8,128)(2,1)S(1)} %get-tuple-element.20), channel_id=1, source_target_pairs={{0,384},{64,448},{128,0},{192,64},{256,128},{320,192},{384,256},{4... | collective-permute-start | bytes 442376 | tf_op jit(solution)/shard_map/ppermute | solution.py:453
  234.3 20.3 %collective-permute-start.7 = (bf16[4,144,128]{2,1,0:T(8,128)(2,1)S(1)}, bf16[4,144,128]{2,1,0:T(8,128)(2,1)S(1)}, u32[]{:S(2)}, u32[]{:S(2)}) collective-permute-start(bf16[4,144,128]{2,1,0:T(8,128)(2,1)S(1)} %get-tuple-element.19), channel_id=1, source_target_pairs={{0,448},{64,0},{128,64},{192,128},{256,192},{320,256},{384,320},{4... | collective-permute-start | bytes 442376 | tf_op jit(solution)/shard_map/ppermute | solution.py:453
  258.2 0.7 copy-start.12
Sparse Core Ops, SparseCore 0:
  10.1 179.0 all-gather.1

commit v4 on v3

--- a/solution.py
+++ b/solution.py
@@ -10,7 +10,7 @@
 
 AXES = ("y", "xh", "xl", "z", "c")
 PLANE = ("y", "xh", "xl")
-LINE = ("xh", "z")
+LINE = ("xh", "xl", "z")
 GROUPS = 4
 
 
@@ -344,6 +344,13 @@
     )(row, members, *pieces)
 
 
+def neighbours(size_x, size_z):
+    return [
+        [x * size_z + z for x in (low, size_x - 1 - low) for z in range(size_z)]
+        for low in range(size_x // 2)
+    ]
+
+
 def shards(
     ssm_input,
     b_inputs,
@@ -367,13 +374,16 @@
     prompts, own_heads, head_size, state_n = prompt_state.shape
     taps_n, lanes = prompt_taps.shape[2] // head_size, own_heads * head_size
     owners = lax.axis_size(PLANE)
-    lines, expert_count = lax.axis_size(LINE), lax.axis_size(("z", "c"))
+    lines, expert_count = lax.axis_size(("xh", "z")), lax.axis_size(("z", "c"))
     state_rows = own_heads * head_size
 
     stacked = jnp.concatenate([gate_weight, up_weight, down_weight], 0)
-    swapped = lax.ppermute(
-        stacked, ("xh", "c"), [(a * 2 + b, b * 2 + a) for a in range(2) for b in range(2)]
-    )
+    size_x, size_z = lax.axis_size(("xh", "xl")), lax.axis_size("z")
+    swap = []
+    for x in range(size_x):
+        half, other = x // (size_x // 2), size_x - 1 - x
+        swap += [(x * 2 + half, x * 2 + half), (x * 2 + 1 - half, other * 2 + half)]
+    swapped = lax.ppermute(stacked, ("xh", "xl", "c"), swap)
     weights = lax.all_gather(swapped, ("y", "xl", "c"), axis=1, tiled=True)
 
     row = lax.axis_index("y").astype(jnp.int32)[None]
@@ -427,13 +437,23 @@
     packed_rows = lines * GROUPS * slots
     outgoing = dispatch(lengths, base, state, c_readout, grow, spot, head_size, slots, packed_rows)
     arrived = lax.all_to_all(
-        outgoing.reshape(lines, GROUPS * slots, width), LINE, 0, 0, tiled=True
+        outgoing.reshape(lines, GROUPS * slots, width),
+        LINE,
+        0,
+        0,
+        tiled=True,
+        axis_index_groups=neighbours(size_x, size_z),
     )
     expert_rows = unpack(arrived.reshape(packed_rows, width), slots, lines)
     produced = expert_apply(expert_rows, weights, slots, lines)
     produced, column_grad = lax.optimization_barrier((produced, column_grad))
     returned = lax.all_to_all(
-        produced.reshape(lines, GROUPS * slots, width), LINE, 0, 0, tiled=True
+        produced.reshape(lines, GROUPS * slots, width),
+        LINE,
+        0,
+        0,
+        tiled=True,
+        axis_index_groups=neighbours(size_x, size_z),
     ).reshape(packed_rows, width)
     spots = lax.iota(jnp.int32, packed_rows)
     placing = [

time: 269 us -> 251 us (0.933)
  waiting for transfers between devices: 92 us -> 75.5 us
    all_gather x1, waiting for transfers between devices: 44.5 us -> 28.6 us  [shards(): weights = lax.all_gather(swapped, ('y', 'xl', 'c'), axis=1, tiled=True)]
  transfers between devices with their start and end apart: 13 -> 13, of which waited for: 6 -> 5; matrix products, arithmetic and copies ran while one was open for 2% -> 2% of each run, Pallas kernels for 12% -> 13%
where the time goes in v4:
time: 251 us; the launch traced here: 249 us
  waiting for transfers between devices  75.5 us (30%)
  starting transfers between devices  64.5 us (26%)
  blocking collectives  46.8 us (19%)
  Pallas kernels  32.9 us (13%)
  between operations  15.8 us (6%)
  local copies, waits for them, and re-layouts  6.98 us (3%)
  other arithmetic  4.46 us (2%)
    all_to_all x1, blocking collectives, shards(): lax.all_to_all(outgoing.reshape(lines, GROUPS * slots, width), LINE, 0, 0...  46.8 us
    all_gather x1, waiting for transfers between devices, shards(): weights = lax.all_gather(swapped, ('y', 'xl', 'c'), axis=1, tiled=True)  28.6 us
    ppermute x7, starting transfers between devices, shards(): lax.ppermute(column_grad[:, d], 'y', [(i, (i + d) % size_y) for i in rang...  23.4 us
    all_to_all x1, waiting for transfers between devices, shards(): lax.all_to_all(outgoing_state, PLANE, 0, 0, tiled=True)  22.6 us
    all_to_all x1, starting transfers between devices, shards(): lax.all_to_all(jnp.broadcast_to(notice[None], (owners,) + notice.shape),...  21 us
    ppermute x7, waiting for transfers between devices, shards(): lax.ppermute(column_grad[:, d], 'y', [(i, (i + d) % size_y) for i in rang...  17.6 us
    pallas_call x1, Pallas kernels, expert_apply(): pl.pallas_call(functools.partial(expert_kernel, slots, sources), grid=(un...  13.1 us
    pallas_call x1, Pallas kernels, mixer_base(): pl.pallas_call(functools.partial(mixer_kernel, head_size), grid_spec=pltp...  10.6 us
  transfers between devices with their start and end apart: 13, of which 5 were waited for; matrix products, arithmetic and copies ran while one was open for 2% of the time, Pallas kernels for 13%

profile of v4, /device:TPU:56, one launch (start us, length us, event | category | flops | bytes accessed | tf_op | source)
XLA Modules:
  0.0 248.6 jit_solution(5817697988038155386)
XLA Ops:
  7.2 0.0 all-gather.2.cloned.1.call-start
  7.3 1.2 pad_maximum_fusion
  8.4 0.7 collective-permute-start
  9.1 0.0 collective-permute-done
  9.2 0.8 copy-done.6
  10.0 0.0 all-gather.2.cloned.1.call-update
  10.7 0.1 reshape.230
  10.8 0.1 reshape.231
  10.9 0.1 pad.10.clone
  10.9 0.1 pad.11.clone
  11.0 0.1 maximum_maximum_fusion
  11.1 0.6 broadcast_in_dim.69
  11.7 21.0 %all-to-all-start = ((bf16[32,8,128]{2,1,0:T(8,128)(2,1)}), bf16[32,8,128]{2,1,0:T(8,128)(2,1)S(1)}, u32[]{:S(2)}, u32[]{:S(2)}) async-start(bf16[32,8,128]{2,1,0:T(8,128)(2,1)} %broadcast_in_dim.69), calls=%async_computation | async-start | bytes 131072 | tf_op jit(solution)/shard_map/all_to_all | solution.py:398
  33.4 0.1 copy.71
  33.5 0.1 broadcast_in_dim.70
  33.6 0.1 broadcast_in_dim_reshape.3.skip_ref
  33.7 6.7 %all-to-all-done = bf16[32,8,128]{2,1,0:T(8,128)(2,1)S(1)} async-done(((bf16[32,8,128]{2,1,0:T(8,128)(2,1)}), bf16[32,8,128]{2,1,0:T(8,128)(2,1)S(1)}, u32[]{:S(2)}, u32[]{:S(2)}) %all-to-all-start) | async-done | bytes 65568 | tf_op jit(solution)/shard_map/all_to_all | solution.py:398
  40.4 0.7 compare_reduce_fusion
  41.1 0.0 copy-start
  41.1 0.0 copy-start.3
  41.1 0.0 copy-start.4
  41.1 0.0 copy-start.5
  41.1 1.1 broadcast_select_fusion
  42.2 6.2 %all-to-all-start.1 = ((bf16[32,128,128]{2,1,0:T(8,128)(2,1)}), bf16[32,128,128]{2,1,0:T(8,128)(2,1)S(1)}, u32[]{:S(2)}, u32[]{:S(2)}) async-start(bf16[32,128,128]{2,1,0:T(8,128)(2,1)} %broadcast_select_fusion), calls=%async_computation.1 | async-start | bytes 2097152 | tf_op jit(solution)/shard_map/all_to_all | solution.py:409
  48.5 0.1 convert_reduce_fusion
  48.8 0.0 copy-start.1
  48.8 1.2 copy-done.1
  50.0 1.2 copy-done.2
  51.2 10.6 %shard_map.184 = (f32[128,4096]{1,0:T(8,128)S(1)}, bf16[4,8,144,128]{3,2,1,0:T(8,128)(2,1)}, f32[128,64]{1,0:T(8,128)S(1)}) custom-call(s32[1]{0:T(128)S(6)} %copy.89.length_ref, s32[1]{0:T(128)} %bitcast.2.row_ref, bf16[128,4096]{1,0:T(8,128)(2,1)S(1)} %copy-done.1, f32[8,4096]{1,0:T(8,128)S(1)} %pad_convert_fusion.prior_ref, f32[4,4096]{1,0:T(4,128)S(1)} %copy-done.3, ...), custom_call_target="tpu_custom_call" | custom-call | flops 1342177280 | bytes 5242880 | tf_op jit(solution)/shard_map/pallas_call | solution.py:125
  61.8 22.6 %all-to-all-done.1 = bf16[32,128,128]{2,1,0:T(8,128)(2,1)S(1)} async-done(((bf16[32,128,128]{2,1,0:T(8,128)(2,1)}), bf16[32,128,128]{2,1,0:T(8,128)(2,1)S(1)}, u32[]{:S(2)}, u32[]{:S(2)}) %all-to-all-start.1) | async-done | bytes 1048608 | tf_op jit(solution)/shard_map/all_to_all | solution.py:409
  84.4 5.6 %shard_map.185 = bf16[768,1024]{1,0:T(8,128)(2,1)S(1)} custom-call(s32[1]{0:T(128)S(6)} %copy.89.length_ref, f32[128,4096]{1,0:T(8,128)S(1)} %get-tuple-element.10.base_ref, bf16[4096,128]{1,0:T(8,128)(2,1)S(1)} %bitcast.63, bf16[128,128]{1,0:T(8,128)(2,1)S(1)} %copy-done, f32[128,64]{1,0:T(8,128)S(1)} %get-tuple-element.11.grow_ref, ...), custom_call_target="tpu_custom_call" | custom-call | flops 939524096 | bytes 4718592 | tf_op jit(solution)/shard_map/pallas_call | solution.py:202
  90.0 46.8 %all_to_all.25 = bf16[16,48,1024]{2,1,0:T(8,128)(2,1)S(1)} all-to-all(bf16[16,48,1024]{2,1,0:T(8,128)(2,1)S(1)} %bitcast.62), channel_id=1, replica_groups={{0,2,4,6,8,10,12,14,48,50,52,54,56,58,60,62},{16,18,20,22,24,26,28,30,3..., dimensions={0} | all-to-all | bytes 3145728 | tf_op jit(solution)/shard_map/all_to_all | solution.py:439
  136.8 4.3 %all-to-all-start.3 = ((bf16[4,8,144,128]{3,2,1,0:T(8,128)(2,1)}), bf16[4,8,144,128]{3,2,1,0:T(8,128)(2,1)}, u32[]{:S(2)}, u32[]{:S(2)}) async-start(bf16[4,8,144,128]{3,2,1,0:T(8,128)(2,1)} %get-tuple-element.12), calls=%async_computation.3 | async-start | bytes 2359296 | tf_op jit(solution)/shard_map/all_to_all | solution.py:427
  141.1 2.1 shard_map.186.rows_ref
  143.2 28.6 %all-gather.2.cloned.1.call-done.weight_ref = bf16[3,768,4096]{2,1,0:T(8,128)(2,1)} async-done(((bf16[3,24,4096]{2,1,0:T(8,128)(2,1)}), bf16[3,768,4096]{2,1,0:T(8,128)(2,1)}) %all-gather.2.cloned.1.call-update) | async-done | bytes 18874384 | tf_op jit(solution)/shard_map/all_gather | solution.py:387
  171.8 13.1 %shard_map.187 = bf16[768,1024]{1,0:T(8,128)(2,1)} custom-call(bf16[192,4096]{1,0:T(8,128)(2,1)S(1)} %shard_map.186.rows_ref, bf16[3,768,4096]{2,1,0:T(8,128)(2,1)} %all-gather.2.cloned.1.call-done.weight_ref), custom_call_target="tpu_custom_call" | custom-call | flops 3623878656 | bytes 22020096 | tf_op jit(solution)/shard_map/pallas_call | solution.py:293
  184.9 0.0 all-to-all-done.3
  184.9 8.9 %all-to-all-start.4 = ((bf16[16,48,1024]{2,1,0:T(8,128)(2,1)}), bf16[16,48,1024]{2,1,0:T(8,128)(2,1)S(1)}, u32[]{:S(2)}, u32[]{:S(2)}) async-start(bf16[16,48,1024]{2,1,0:T(8,128)(2,1)} %bitcast.16), calls=%async_computation.4 | async-start | bytes 3145728 | tf_op jit(solution)/shard_map/all_to_all | solution.py:450
  193.8 1.4 slice_bitcast_fusion
  195.3 2.4 collective-permute-start.1
  197.7 1.9 collective-permute-start.2
  199.7 1.9 collective-permute-start.3
  201.6 7.9 %collective-permute-start.4 = (bf16[4,144,128]{2,1,0:T(8,128)(2,1)S(1)}, bf16[4,144,128]{2,1,0:T(8,128)(2,1)S(1)}, u32[]{:S(2)}, u32[]{:S(2)}) collective-permute-start(bf16[4,144,128]{2,1,0:T(8,128)(2,1)S(1)} %get-tuple-element.22), channel_id=1, source_target_pairs={{0,256},{64,320},{128,384},{192,448},{256,0},{320,64},{384,128},{4... | collective-permute-start | bytes 442376 | tf_op jit(solution)/shard_map/ppermute | solution.py:473
  209.5 2.8 %collective-permute-start.5 = (bf16[4,144,128]{2,1,0:T(8,128)(2,1)S(1)}, bf16[4,144,128]{2,1,0:T(8,128)(2,1)S(1)}, u32[]{:S(2)}, u32[]{:S(2)}) collective-permute-start(bf16[4,144,128]{2,1,0:T(8,128)(2,1)S(1)} %get-tuple-element.21), channel_id=1, source_target_pairs={{0,320},{64,384},{128,448},{192,0},{256,64},{320,128},{384,192},{4... | collective-permute-start | bytes 442376 | tf_op jit(solution)/shard_map/ppermute | solution.py:473
  212.3 0.0 collective-permute-done.1.refs_1_
  212.3 3.9 %collective-permute-start.6 = (bf16[4,144,128]{2,1,0:T(8,128)(2,1)S(1)}, bf16[4,144,128]{2,1,0:T(8,128)(2,1)S(1)}, u32[]{:S(2)}, u32[]{:S(2)}) collective-permute-start(bf16[4,144,128]{2,1,0:T(8,128)(2,1)S(1)} %get-tuple-element.20), channel_id=1, source_target_pairs={{0,384},{64,448},{128,0},{192,64},{256,128},{320,192},{384,256},{4... | collective-permute-start | bytes 442376 | tf_op jit(solution)/shard_map/ppermute | solution.py:473
  216.2 0.0 collective-permute-done.2.refs_2_
  216.2 2.5 collective-permute-start.7
  218.7 0.0 collective-permute-done.3.refs_3_
  218.8 0.0 collective-permute-done.4.refs_4_
  218.8 11.5 %collective-permute-done.5.refs_5_ = bf16[4,144,128]{2,1,0:T(8,128)(2,1)S(1)} collective-permute-done((bf16[4,144,128]{2,1,0:T(8,128)(2,1)S(1)}, bf16[4,144,128]{2,1,0:T(8,128)(2,1)S(1)}, u32[]{:S(2)}, u32[]{:S(2)}) %collective-permute-start.5) | collective-permute-done | bytes 147488 | tf_op jit(solution)/shard_map/ppermute | solution.py:473
  230.2 0.0 collective-permute-done.6.refs_6_
  230.2 6.1 %collective-permute-done.7.refs_7_ = bf16[4,144,128]{2,1,0:T(8,128)(2,1)S(1)} collective-permute-done((bf16[4,144,128]{2,1,0:T(8,128)(2,1)S(1)}, bf16[4,144,128]{2,1,0:T(8,128)(2,1)S(1)}, u32[]{:S(2)}, u32[]{:S(2)}) %collective-permute-start.7) | collective-permute-done | bytes 147488 | tf_op jit(solution)/shard_map/ppermute | solution.py:473
  236.3 1.5 shard_map.188
  237.8 0.1 reshape.238
  237.9 0.7 reshape.239
  238.6 0.0 all-to-all-done.4
  238.6 0.4 fusion.1
  239.0 0.4 fusion.3
  239.4 0.4 fusion.4
  239.9 0.0 copy-start.12
  239.9 0.4 fusion.2
  240.3 0.2 copy-done.12
  240.5 1.2 fusion
  (28 shorter events, 0.2 us)
Async XLA Ops:
  7.2 3.5 %copy-start.9 = (bf16[2,2,192]{2,1,0:T(2,128)(2,1)S(1)}, bf16[2,2,192]{2,1,0:T(2,128)(2,1)}, u32[]{:S(2)}) copy-start(bf16[2,2,192]{2,1,0:T(2,128)(2,1)} %param.25) | copy-start | bytes 4612
  7.2 26.2 %copy-start.8 = (f32[128,64]{0,1:T(8,128)S(1)}, f32[128,64]{0,1:T(8,128)}, u32[]{:S(2)}) copy-start(f32[128,64]{0,1:T(8,128)} %param.20) | copy-start | bytes 98308
  7.2 26.3 %copy-start.10 = (f32[64]{0:T(128)S(1)}, f32[64]{0:T(128)}, u32[]{:S(2)}) copy-start(f32[64]{0:T(128)} %param.22) | copy-start | bytes 772
  7.2 26.5 %copy-start.7 = (bf16[2,2,64,128]{3,2,1,0:T(8,128)(2,1)S(1)}, bf16[2,2,64,128]{3,2,1,0:T(8,128)(2,1)}, u32[]{:S(2)}) copy-start(bf16[2,2,64,128]{3,2,1,0:T(8,128)(2,1)} %param.24) | copy-start | bytes 196612
  7.2 164.6 %all-gather.2.cloned.1.call-start = ((), (), s32[]{:S(2)}) async-start(), calls=%async_computation.5 | async-start | bytes 19464192 | tf_op jit(solution)/shard_map/all_gather | solution.py:387
  8.4 0.7 collective-permute-start
  9.2 0.8 copy-start.6
  11.7 28.7 %all-to-all-start = ((bf16[32,8,128]{2,1,0:T(8,128)(2,1)}), bf16[32,8,128]{2,1,0:T(8,128)(2,1)S(1)}, u32[]{:S(2)}, u32[]{:S(2)}) async-start(bf16[32,8,128]{2,1,0:T(8,128)(2,1)} %broadcast_in_dim.69), calls=%async_computation | async-start | bytes 131072 | tf_op jit(solution)/shard_map/all_to_all | solution.py:398
  41.1 7.4 %copy-start.11 = (s32[128,1]{0,1:T(1,128)S(1)}, s32[128,1]{0,1:T(1,128)}, u32[]{:S(2)}) copy-start(s32[128,1]{0,1:T(1,128)} %param.29) | copy-start | bytes 1540
  41.1 7.7 %copy-start = (bf16[128,128]{1,0:T(8,128)(2,1)S(1)}, bf16[128,128]{1,0:T(8,128)(2,1)}, u32[]{:S(2)}) copy-start(bf16[128,128]{1,0:T(8,128)(2,1)} %c_ref.3) | copy-start | bytes 98308
  41.1 7.7 %copy-start.3 = (f32[4,4096]{1,0:T(4,128)S(1)}, f32[4,4096]{1,0:T(4,128)}, u32[]{:S(2)}) copy-start(f32[4,4096]{1,0:T(4,128)} %conv_ref.1) | copy-start | bytes 196612
  41.1 7.7 %copy-start.4 = (bf16[128,128]{1,0:T(8,128)(2,1)S(1)}, bf16[128,128]{1,0:T(8,128)(2,1)}, u32[]{:S(2)}) copy-start(bf16[128,128]{1,0:T(8,128)(2,1)} %b_ref.1) | copy-start | bytes 98308
  41.1 7.6 %copy-start.5 = (f32[64]{0:T(128)S(1)}, f32[64]{0:T(128)}, u32[]{:S(2)}) copy-start(f32[64]{0:T(128)} %param.21) | copy-start | bytes 772
  42.2 42.2 %all-to-all-start.1 = ((bf16[32,128,128]{2,1,0:T(8,128)(2,1)}), bf16[32,128,128]{2,1,0:T(8,128)(2,1)S(1)}, u32[]{:S(2)}, u32[]{:S(2)}) async-start(bf16[32,128,128]{2,1,0:T(8,128)(2,1)} %broadcast_select_fusion), calls=%async_computation.1 | async-start | bytes 2097152 | tf_op jit(solution)/shard_map/all_to_all | solution.py:409
  48.8 1.2 copy-start.1
  50.0 1.2 copy-start.2
  136.8 48.1 %all-to-all-start.3 = ((bf16[4,8,144,128]{3,2,1,0:T(8,128)(2,1)}), bf16[4,8,144,128]{3,2,1,0:T(8,128)(2,1)}, u32[]{:S(2)}, u32[]{:S(2)}) async-start(bf16[4,8,144,128]{3,2,1,0:T(8,128)(2,1)} %get-tuple-element.12), calls=%async_computation.3 | async-start | bytes 2359296 | tf_op jit(solution)/shard_map/all_to_all | solution.py:427
  184.9 53.7 %all-to-all-start.4 = ((bf16[16,48,1024]{2,1,0:T(8,128)(2,1)}), bf16[16,48,1024]{2,1,0:T(8,128)(2,1)S(1)}, u32[]{:S(2)}, u32[]{:S(2)}) async-start(bf16[16,48,1024]{2,1,0:T(8,128)(2,1)} %bitcast.16), calls=%async_computation.4 | async-start | bytes 3145728 | tf_op jit(solution)/shard_map/all_to_all | solution.py:450
  195.3 17.0 %collective-permute-start.1 = (bf16[4,144,128]{2,1,0:T(8,128)(2,1)S(1)}, bf16[4,144,128]{2,1,0:T(8,128)(2,1)S(1)}, u32[]{:S(2)}, u32[]{:S(2)}) collective-permute-start(bf16[4,144,128]{2,1,0:T(8,128)(2,1)S(1)} %get-tuple-element.25), channel_id=1, source_target_pairs={{0,64},{64,128},{128,192},{192,256},{256,320},{320,384},{384,448},... | collective-permute-start | bytes 442376 | tf_op jit(solution)/shard_map/ppermute | solution.py:473
  197.7 18.5 %collective-permute-start.2 = (bf16[4,144,128]{2,1,0:T(8,128)(2,1)S(1)}, bf16[4,144,128]{2,1,0:T(8,128)(2,1)S(1)}, u32[]{:S(2)}, u32[]{:S(2)}) collective-permute-start(bf16[4,144,128]{2,1,0:T(8,128)(2,1)S(1)} %get-tuple-element.24), channel_id=1, source_target_pairs={{0,128},{64,192},{128,256},{192,320},{256,384},{320,448},{384,0},{... | collective-permute-start | bytes 442376 | tf_op jit(solution)/shard_map/ppermute | solution.py:473
  199.7 19.1 %collective-permute-start.3 = (bf16[4,144,128]{2,1,0:T(8,128)(2,1)S(1)}, bf16[4,144,128]{2,1,0:T(8,128)(2,1)S(1)}, u32[]{:S(2)}, u32[]{:S(2)}) collective-permute-start(bf16[4,144,128]{2,1,0:T(8,128)(2,1)S(1)} %get-tuple-element.23), channel_id=1, source_target_pairs={{0,192},{64,256},{128,320},{192,384},{256,448},{320,0},{384,64},{4... | collective-permute-start | bytes 442376 | tf_op jit(solution)/shard_map/ppermute | solution.py:473
  201.6 17.2 %collective-permute-start.4 = (bf16[4,144,128]{2,1,0:T(8,128)(2,1)S(1)}, bf16[4,144,128]{2,1,0:T(8,128)(2,1)S(1)}, u32[]{:S(2)}, u32[]{:S(2)}) collective-permute-start(bf16[4,144,128]{2,1,0:T(8,128)(2,1)S(1)} %get-tuple-element.22), channel_id=1, source_target_pairs={{0,256},{64,320},{128,384},{192,448},{256,0},{320,64},{384,128},{4... | collective-permute-start | bytes 442376 | tf_op jit(solution)/shard_map/ppermute | solution.py:473
  209.5 20.8 %collective-permute-start.5 = (bf16[4,144,128]{2,1,0:T(8,128)(2,1)S(1)}, bf16[4,144,128]{2,1,0:T(8,128)(2,1)S(1)}, u32[]{:S(2)}, u32[]{:S(2)}) collective-permute-start(bf16[4,144,128]{2,1,0:T(8,128)(2,1)S(1)} %get-tuple-element.21), channel_id=1, source_target_pairs={{0,320},{64,384},{128,448},{192,0},{256,64},{320,128},{384,192},{4... | collective-permute-start | bytes 442376 | tf_op jit(solution)/shard_map/ppermute | solution.py:473
  212.3 17.9 %collective-permute-start.6 = (bf16[4,144,128]{2,1,0:T(8,128)(2,1)S(1)}, bf16[4,144,128]{2,1,0:T(8,128)(2,1)S(1)}, u32[]{:S(2)}, u32[]{:S(2)}) collective-permute-start(bf16[4,144,128]{2,1,0:T(8,128)(2,1)S(1)} %get-tuple-element.20), channel_id=1, source_target_pairs={{0,384},{64,448},{128,0},{192,64},{256,128},{320,192},{384,256},{4... | collective-permute-start | bytes 442376 | tf_op jit(solution)/shard_map/ppermute | solution.py:473
  216.2 20.1 %collective-permute-start.7 = (bf16[4,144,128]{2,1,0:T(8,128)(2,1)S(1)}, bf16[4,144,128]{2,1,0:T(8,128)(2,1)S(1)}, u32[]{:S(2)}, u32[]{:S(2)}) collective-permute-start(bf16[4,144,128]{2,1,0:T(8,128)(2,1)S(1)} %get-tuple-element.19), channel_id=1, source_target_pairs={{0,448},{64,0},{128,64},{192,128},{256,192},{320,256},{384,320},{4... | collective-permute-start | bytes 442376 | tf_op jit(solution)/shard_map/ppermute | solution.py:473
  239.9 0.7 copy-start.12
Sparse Core Ops, SparseCore 0:
  10.1 161.5 all-gather.1

commit v5 on v4

--- a/solution.py
+++ b/solution.py
@@ -309,39 +309,62 @@
     )(rows, weights)
 
 
-def collect_kernel(row_ref, members_ref, *refs):
-    pieces, state_ref, taps_ref, total_ref = refs[:-3], *refs[-3:]
-    size_y, size_x = len(pieces), pieces[0].shape[0]
+def presum_kernel(row_ref, members_ref, column_ref, out_ref, total_ref):
+    size_x = column_ref.shape[0]
+    total_ref[...] = jnp.zeros_like(total_ref)
+    for k in range(size_x):
+        member = members_ref[row_ref[0] * size_x + k]
+        total_ref[member] += column_ref[k, 0].astype(jnp.float32)
+    out_ref[0] = total_ref[...].astype(jnp.bfloat16)
+
+
+def presum(row, members, column, prompts):
+    size_x, size_y, rows, lanes = column.shape
+    smem = pl.BlockSpec(memory_space=pltpu.SMEM)
+    return pl.pallas_call(
+        presum_kernel,
+        grid=(size_y,),
+        in_specs=[smem, smem, pl.BlockSpec((size_x, 1, rows, lanes), lambda i: (0, i, 0, 0))],
+        out_specs=pl.BlockSpec((1, prompts, rows, lanes), lambda i: (i, 0, 0, 0)),
+        out_shape=jax.ShapeDtypeStruct((size_y, prompts, rows, lanes), jnp.bfloat16),
+        scratch_shapes=[pltpu.VMEM((prompts, rows, lanes), jnp.float32)],
+        compiler_params=pltpu.CompilerParams(vmem_limit_bytes=16 * 1024 * 1024),
+        cost_estimate=pl.CostEstimate(
+            flops=size_x * size_y * rows * lanes,
+            bytes_accessed=3 * size_x * size_y * rows * lanes,
+            transcendentals=0,
+        ),
+    )(row, members, column)
+
+
+def collect_kernel(*refs):
+    pieces, (state_ref, taps_ref) = refs[:-2], refs[-2:]
     lanes = state_ref.shape[1]
-    total_ref[...] = jnp.zeros_like(total_ref)
-    for step in range(size_y):
-        source = lax.rem(row_ref[0] - step + size_y, size_y)
-        for k in range(size_x):
-            member = members_ref[source * size_x + k]
-            total_ref[member] += pieces[step][k].astype(jnp.float32)
-    state_ref[...] = total_ref[:, :lanes]
-    taps_ref[...] = total_ref[:, lanes:]
-
-
-def collect(row, members, pieces, prompts):
-    size_x, rows, lanes = pieces[0].shape
-    vmem, smem = pl.BlockSpec(memory_space=pltpu.VMEM), pl.BlockSpec(memory_space=pltpu.SMEM)
+    total = pieces[0][...].astype(jnp.float32)
+    for piece in pieces[1:]:
+        total = total + piece[...].astype(jnp.float32)
+    state_ref[...] = total[:, :lanes]
+    taps_ref[...] = total[:, lanes:]
+
+
+def collect(pieces):
+    prompts, rows, lanes = pieces[0].shape
+    vmem = pl.BlockSpec(memory_space=pltpu.VMEM)
     return pl.pallas_call(
         collect_kernel,
-        in_specs=[smem, smem] + [vmem] * len(pieces),
+        in_specs=[vmem] * len(pieces),
         out_specs=[vmem, vmem],
         out_shape=[
             jax.ShapeDtypeStruct((prompts, rows - 16, lanes), jnp.float32),
             jax.ShapeDtypeStruct((prompts, 16, lanes), jnp.float32),
         ],
-        scratch_shapes=[pltpu.VMEM((prompts, rows, lanes), jnp.float32)],
         compiler_params=pltpu.CompilerParams(vmem_limit_bytes=16 * 1024 * 1024),
         cost_estimate=pl.CostEstimate(
-            flops=len(pieces) * size_x * rows * lanes,
-            bytes_accessed=2 * len(pieces) * size_x * rows * lanes,
+            flops=len(pieces) * prompts * rows * lanes,
+            bytes_accessed=2 * len(pieces) * prompts * rows * lanes,
             transcendentals=0,
         ),
-    )(row, members, *pieces)
+    )(*pieces)
 
 
 def neighbours(size_x, size_z):
@@ -424,7 +447,6 @@
         head_size,
         (lax.axis_size("y"), lax.axis_size(("xh", "xl"))),
     )
-    column_grad = lax.all_to_all(outgoing_grad, ("xh", "xl"), 0, 0, tiled=True)
 
     slots = 3 * steps_n // (2 * expert_count)
     width = row_width // GROUPS
@@ -444,9 +466,12 @@
         tiled=True,
         axis_index_groups=neighbours(size_x, size_z),
     )
+    arrived, outgoing_grad = lax.optimization_barrier((arrived, outgoing_grad))
+    column_grad = lax.all_to_all(outgoing_grad, ("xh", "xl"), 0, 0, tiled=True)
     expert_rows = unpack(arrived.reshape(packed_rows, width), slots, lines)
     produced = expert_apply(expert_rows, weights, slots, lines)
-    produced, column_grad = lax.optimization_barrier((produced, column_grad))
+    row_grad = presum(row, members.astype(jnp.int32), column_grad, prompts)
+    produced, row_grad = lax.optimization_barrier((produced, row_grad))
     returned = lax.all_to_all(
         produced.reshape(lines, GROUPS * slots, width),
         LINE,
@@ -469,11 +494,11 @@
         1,
     )
     size_y = lax.axis_size("y")
-    pieces = [column_grad[:, 0]] + [
-        lax.ppermute(column_grad[:, d], "y", [(i, (i + d) % size_y) for i in range(size_y)])
+    pieces = [row_grad[0]] + [
+        lax.ppermute(row_grad[d], "y", [(i, (i + d) % size_y) for i in range(size_y)])
         for d in range(1, size_y)
     ]
-    state_sum, taps_sum = collect(row, members.astype(jnp.int32), pieces, prompts)
+    state_sum, taps_sum = collect(pieces)
     state_grad = state_sum.reshape(prompts, own_heads, head_size, state_n)
     taps_grad = jnp.transpose(
         taps_sum[:, :taps_n].reshape(prompts, taps_n, own_heads, head_size), (0, 2, 1, 3)

time: 251 us -> 245 us (0.976)
  waiting for transfers between devices: 75.5 us -> 70.5 us
    all_gather x1, waiting for transfers between devices: 28.6 us -> 2.48 us  [shards(): weights = lax.all_gather(swapped, ('y', 'xl', 'c'), axis=1, tiled=True)]
    all_to_all x1, waiting for transfers between devices: 0.01 us -> 24.5 us  [shards(): column_grad = lax.all_to_all(outgoing_grad, ('xh', 'xl'), 0, 0, tiled=True)]
    ppermute x7, waiting for transfers between devices: 17.6 us -> 7.05 us  [shards(): lax.ppermute(row_grad[d], 'y', [(i, (i + d) % size_y) for i in range(size...]
    all_to_all x1, waiting for transfers between devices: 0.01 us -> 7.56 us  [shards(): lax.all_to_all(produced.reshape(lines, GROUPS * slots, width), LINE, 0, 0...]
    unnamed x27 -> x33, local copies, waits for them, and re-layouts: 3.63 us -> 5.8 us
  transfers between devices with their start and end apart: 13 -> 13, of which waited for: 5 -> 8; matrix products, arithmetic and copies ran while one was open for 2% -> 2% of each run, Pallas kernels for 13% -> 8%
where the time goes in v5:
time: 245 us; the launch traced here: 243 us
  waiting for transfers between devices  70.5 us (29%)
  starting transfers between devices  63.7 us (26%)
  blocking collectives  46.8 us (19%)
  Pallas kernels  32.7 us (13%)
  between operations  15.8 us (6%)
  local copies, waits for them, and re-layouts  7.76 us (3%)
  other arithmetic  4.46 us (2%)
    all_to_all x1, blocking collectives, shards(): lax.all_to_all(outgoing.reshape(lines, GROUPS * slots, width), LINE, 0, 0...  46.8 us
    all_to_all x1, waiting for transfers between devices, shards(): column_grad = lax.all_to_all(outgoing_grad, ('xh', 'xl'), 0, 0, tiled=True)  24.5 us
    ppermute x7, starting transfers between devices, shards(): lax.ppermute(row_grad[d], 'y', [(i, (i + d) % size_y) for i in range(size...  23.4 us
    all_to_all x1, waiting for transfers between devices, shards(): lax.all_to_all(outgoing_state, PLANE, 0, 0, tiled=True)  22.3 us
    all_to_all x1, starting transfers between devices, shards(): lax.all_to_all(jnp.broadcast_to(notice[None], (owners,) + notice.shape),...  21 us
    pallas_call x1, Pallas kernels, expert_apply(): pl.pallas_call(functools.partial(expert_kernel, slots, sources), grid=(un...  13.2 us
    pallas_call x1, Pallas kernels, mixer_base(): pl.pallas_call(functools.partial(mixer_kernel, head_size), grid_spec=pltp...  9.9 us
    all_to_all x1, starting transfers between devices, shards(): lax.all_to_all(produced.reshape(lines, GROUPS * slots, width), LINE, 0, 0...  8.88 us
  transfers between devices with their start and end apart: 13, of which 8 were waited for; matrix products, arithmetic and copies ran while one was open for 2% of the time, Pallas kernels for 8%

profile of v5, /device:TPU:56, one launch (start us, length us, event | category | flops | bytes accessed | tf_op | source)
XLA Modules:
  0.0 243.5 jit_solution(105824879513684352)
XLA Ops:
  7.2 0.0 all-gather.2.cloned.1.call-start
  7.3 1.2 pad_maximum_fusion
  8.4 0.7 collective-permute-start
  9.1 0.0 collective-permute-done
  9.2 0.8 copy-done.9
  10.0 0.0 all-gather.2.cloned.1.call-update
  10.7 0.1 reshape.230
  10.8 0.1 reshape.231
  10.9 0.1 pad.10.clone
  11.0 0.1 pad.11.clone
  11.0 0.1 maximum_maximum_fusion
  11.1 0.6 broadcast_in_dim.69
  11.7 21.0 %all-to-all-start = ((bf16[32,8,128]{2,1,0:T(8,128)(2,1)}), bf16[32,8,128]{2,1,0:T(8,128)(2,1)S(1)}, u32[]{:S(2)}, u32[]{:S(2)}) async-start(bf16[32,8,128]{2,1,0:T(8,128)(2,1)} %broadcast_in_dim.69), calls=%async_computation | async-start | bytes 131072 | tf_op jit(solution)/shard_map/all_to_all | solution.py:421
  33.4 0.1 copy.53
  33.5 0.1 broadcast_in_dim.70
  33.6 0.1 broadcast_in_dim_reshape.3.skip_ref
  33.7 6.7 %all-to-all-done = bf16[32,8,128]{2,1,0:T(8,128)(2,1)S(1)} async-done(((bf16[32,8,128]{2,1,0:T(8,128)(2,1)}), bf16[32,8,128]{2,1,0:T(8,128)(2,1)S(1)}, u32[]{:S(2)}, u32[]{:S(2)}) %all-to-all-start) | async-done | bytes 65568 | tf_op jit(solution)/shard_map/all_to_all | solution.py:421
  40.4 0.7 compare_reduce_fusion
  41.1 0.0 copy-start.3
  41.1 0.0 copy-start.6
  41.1 0.0 copy-start.7
  41.1 0.0 copy-start.8
  41.1 1.1 broadcast_select_fusion
  42.2 6.2 %all-to-all-start.1 = ((bf16[32,128,128]{2,1,0:T(8,128)(2,1)}), bf16[32,128,128]{2,1,0:T(8,128)(2,1)S(1)}, u32[]{:S(2)}, u32[]{:S(2)}) async-start(bf16[32,128,128]{2,1,0:T(8,128)(2,1)} %broadcast_select_fusion), calls=%async_computation.1 | async-start | bytes 2097152 | tf_op jit(solution)/shard_map/all_to_all | solution.py:432
  48.5 0.1 convert_reduce_fusion
  48.8 0.0 copy-start.4
  48.8 1.2 copy-done.4
  50.0 1.2 copy-done.5
  51.2 9.9 %shard_map.184 = (f32[128,4096]{1,0:T(8,128)S(1)}, bf16[4,8,144,128]{3,2,1,0:T(8,128)(2,1)S(1)}, f32[128,64]{1,0:T(8,128)S(1)}) custom-call(s32[1]{0:T(128)S(6)} %copy.61.length_ref, s32[1]{0:T(128)} %bitcast.2.row_ref, bf16[128,4096]{1,0:T(8,128)(2,1)S(1)} %copy-done.4, f32[8,4096]{1,0:T(8,128)S(1)} %pad_convert_fusion.prior_ref, f32[4,4096]{1,0:T(4,128)S(1)} %copy-done.6, ...), custom_call_target="tpu_custom_call" | custom-call | flops 1342177280 | bytes 5242880 | tf_op jit(solution)/shard_map/pallas_call | solution.py:125
  61.1 1.0 copy-done.2
  62.1 22.3 %all-to-all-done.1 = bf16[32,128,128]{2,1,0:T(8,128)(2,1)S(1)} async-done(((bf16[32,128,128]{2,1,0:T(8,128)(2,1)}), bf16[32,128,128]{2,1,0:T(8,128)(2,1)S(1)}, u32[]{:S(2)}, u32[]{:S(2)}) %all-to-all-start.1) | async-done | bytes 1048608 | tf_op jit(solution)/shard_map/all_to_all | solution.py:432
  84.4 5.6 %shard_map.185 = bf16[768,1024]{1,0:T(8,128)(2,1)S(1)} custom-call(s32[1]{0:T(128)S(6)} %copy.61.length_ref, f32[128,4096]{1,0:T(8,128)S(1)} %get-tuple-element.12.base_ref, bf16[4096,128]{1,0:T(8,128)(2,1)S(1)} %bitcast.63, bf16[128,128]{1,0:T(8,128)(2,1)S(1)} %copy-done.3, f32[128,64]{1,0:T(8,128)S(1)} %get-tuple-element.13.grow_ref, ...), custom_call_target="tpu_custom_call" | custom-call | flops 939524096 | bytes 4718592 | tf_op jit(solution)/shard_map/pallas_call | solution.py:202
  90.0 46.8 %all_to_all.25 = bf16[16,48,1024]{2,1,0:T(8,128)(2,1)S(1)} all-to-all(bf16[16,48,1024]{2,1,0:T(8,128)(2,1)S(1)} %bitcast.62), channel_id=1, replica_groups={{0,2,4,6,8,10,12,14,48,50,52,54,56,58,60,62},{16,18,20,22,24,26,28,30,3..., dimensions={0} | all-to-all | bytes 3145728 | tf_op jit(solution)/shard_map/all_to_all | solution.py:461
  136.8 3.5 %all-to-all-start.3 = ((bf16[4,8,144,128]{3,2,1,0:T(8,128)(2,1)}), bf16[4,8,144,128]{3,2,1,0:T(8,128)(2,1)S(1)}, u32[]{:S(2)}, u32[]{:S(2)}) async-start(bf16[4,8,144,128]{3,2,1,0:T(8,128)(2,1)} %copy-done.2), calls=%async_computation.3 | async-start | bytes 2359296 | tf_op jit(solution)/shard_map/all_to_all | solution.py:470
  140.4 2.1 shard_map.186.rows_ref
  142.5 1.1 copy-done
  143.6 24.5 %all-to-all-done.3.column_ref = bf16[4,8,144,128]{3,2,1,0:T(8,128)(2,1)S(1)} async-done(((bf16[4,8,144,128]{3,2,1,0:T(8,128)(2,1)}), bf16[4,8,144,128]{3,2,1,0:T(8,128)(2,1)S(1)}, u32[]{:S(2)}, u32[]{:S(2)}) %all-to-all-start.3) | async-done | bytes 1179680 | tf_op jit(solution)/shard_map/all_to_all | solution.py:470
  168.1 1.2 shard_map.188
  169.3 2.5 %all-gather.2.cloned.1.call-done.weight_ref = bf16[3,768,4096]{2,1,0:T(8,128)(2,1)} async-done(((bf16[3,24,4096]{2,1,0:T(8,128)(2,1)}), bf16[3,768,4096]{2,1,0:T(8,128)(2,1)}) %all-gather.2.cloned.1.call-update) | async-done | bytes 18874384 | tf_op jit(solution)/shard_map/all_gather | solution.py:410
  171.8 13.2 %shard_map.187 = bf16[768,1024]{1,0:T(8,128)(2,1)} custom-call(bf16[192,4096]{1,0:T(8,128)(2,1)S(1)} %copy-done.1, bf16[3,768,4096]{2,1,0:T(8,128)(2,1)} %all-gather.2.cloned.1.call-done.weight_ref), custom_call_target="tpu_custom_call" | custom-call | flops 3623878656 | bytes 22020096 | tf_op jit(solution)/shard_map/pallas_call | solution.py:293
  184.9 8.9 %all-to-all-start.4 = ((bf16[16,48,1024]{2,1,0:T(8,128)(2,1)}), bf16[16,48,1024]{2,1,0:T(8,128)(2,1)S(1)}, u32[]{:S(2)}, u32[]{:S(2)}) async-start(bf16[16,48,1024]{2,1,0:T(8,128)(2,1)} %bitcast.16), calls=%async_computation.4 | async-start | bytes 3145728 | tf_op jit(solution)/shard_map/all_to_all | solution.py:475
  193.9 2.5 %collective-permute-start.1 = (bf16[2,144,128]{2,1,0:T(8,128)(2,1)S(1)}, bf16[2,144,128]{2,1,0:T(8,128)(2,1)S(1)}, u32[]{:S(2)}, u32[]{:S(2)}) collective-permute-start(bf16[2,144,128]{2,1,0:T(8,128)(2,1)S(1)} %get-tuple-element.29), channel_id=1, source_target_pairs={{0,64},{64,128},{128,192},{192,256},{256,320},{320,384},{384,448},... | collective-permute-start | bytes 221192 | tf_op jit(solution)/shard_map/ppermute | solution.py:498
  196.4 1.9 collective-permute-start.2
  198.3 1.9 collective-permute-start.3
  200.2 7.8 %collective-permute-start.4 = (bf16[2,144,128]{2,1,0:T(8,128)(2,1)S(1)}, bf16[2,144,128]{2,1,0:T(8,128)(2,1)S(1)}, u32[]{:S(2)}, u32[]{:S(2)}) collective-permute-start(bf16[2,144,128]{2,1,0:T(8,128)(2,1)S(1)} %get-tuple-element.26), channel_id=1, source_target_pairs={{0,256},{64,320},{128,384},{192,448},{256,0},{320,64},{384,128},{4... | collective-permute-start | bytes 221192 | tf_op jit(solution)/shard_map/ppermute | solution.py:498
  208.1 2.9 %collective-permute-start.5 = (bf16[2,144,128]{2,1,0:T(8,128)(2,1)S(1)}, bf16[2,144,128]{2,1,0:T(8,128)(2,1)S(1)}, u32[]{:S(2)}, u32[]{:S(2)}) collective-permute-start(bf16[2,144,128]{2,1,0:T(8,128)(2,1)S(1)} %get-tuple-element.25), channel_id=1, source_target_pairs={{0,320},{64,384},{128,448},{192,0},{256,64},{320,128},{384,192},{4... | collective-permute-start | bytes 221192 | tf_op jit(solution)/shard_map/ppermute | solution.py:498
  211.0 0.0 collective-permute-done.1.refs_1_
  211.0 3.9 %collective-permute-start.6 = (bf16[2,144,128]{2,1,0:T(8,128)(2,1)S(1)}, bf16[2,144,128]{2,1,0:T(8,128)(2,1)S(1)}, u32[]{:S(2)}, u32[]{:S(2)}) collective-permute-start(bf16[2,144,128]{2,1,0:T(8,128)(2,1)S(1)} %get-tuple-element.24), channel_id=1, source_target_pairs={{0,384},{64,448},{128,0},{192,64},{256,128},{320,192},{384,256},{4... | collective-permute-start | bytes 221192 | tf_op jit(solution)/shard_map/ppermute | solution.py:498
  214.9 2.5 %collective-permute-start.7 = (bf16[2,144,128]{2,1,0:T(8,128)(2,1)S(1)}, bf16[2,144,128]{2,1,0:T(8,128)(2,1)S(1)}, u32[]{:S(2)}, u32[]{:S(2)}) collective-permute-start(bf16[2,144,128]{2,1,0:T(8,128)(2,1)S(1)} %get-tuple-element.23), channel_id=1, source_target_pairs={{0,448},{64,0},{128,64},{192,128},{256,192},{320,256},{384,320},{4... | collective-permute-start | bytes 221192 | tf_op jit(solution)/shard_map/ppermute | solution.py:498
  217.3 0.0 collective-permute-done.3.refs_3_
  217.4 3.8 %collective-permute-done.5.refs_5_ = bf16[2,144,128]{2,1,0:T(8,128)(2,1)S(1)} collective-permute-done((bf16[2,144,128]{2,1,0:T(8,128)(2,1)S(1)}, bf16[2,144,128]{2,1,0:T(8,128)(2,1)S(1)}, u32[]{:S(2)}, u32[]{:S(2)}) %collective-permute-start.5) | collective-permute-done | bytes 73760 | tf_op jit(solution)/shard_map/ppermute | solution.py:498
  221.1 0.3 collective-permute-done.6.refs_6_
  221.5 2.9 %collective-permute-done.7.refs_7_ = bf16[2,144,128]{2,1,0:T(8,128)(2,1)S(1)} collective-permute-done((bf16[2,144,128]{2,1,0:T(8,128)(2,1)S(1)}, bf16[2,144,128]{2,1,0:T(8,128)(2,1)S(1)}, u32[]{:S(2)}, u32[]{:S(2)}) %collective-permute-start.7) | collective-permute-done | bytes 73760 | tf_op jit(solution)/shard_map/ppermute | solution.py:498
  224.4 0.7 shard_map.189
  225.1 0.1 reshape.238
  225.2 0.7 reshape.239
  225.9 7.6 %all-to-all-done.4 = bf16[16,48,1024]{2,1,0:T(8,128)(2,1)S(1)} async-done(((bf16[16,48,1024]{2,1,0:T(8,128)(2,1)}), bf16[16,48,1024]{2,1,0:T(8,128)(2,1)S(1)}, u32[]{:S(2)}, u32[]{:S(2)}) %all-to-all-start.4) | async-done | bytes 1572896 | tf_op jit(solution)/shard_map/all_to_all | solution.py:475
  233.5 0.4 fusion.1
  233.9 0.4 fusion.3
  234.3 0.4 fusion.4
  234.8 0.0 copy-start.15
  234.8 0.4 fusion.2
  235.2 0.2 copy-done.15
  235.4 1.2 fusion
  (35 shorter events, 0.3 us)
Async XLA Ops:
  7.2 3.5 %copy-start.12 = (bf16[2,2,192]{2,1,0:T(2,128)(2,1)S(1)}, bf16[2,2,192]{2,1,0:T(2,128)(2,1)}, u32[]{:S(2)}) copy-start(bf16[2,2,192]{2,1,0:T(2,128)(2,1)} %param.25) | copy-start | bytes 4612
  7.2 26.2 %copy-start.11 = (f32[128,64]{0,1:T(8,128)S(1)}, f32[128,64]{0,1:T(8,128)}, u32[]{:S(2)}) copy-start(f32[128,64]{0,1:T(8,128)} %param.20) | copy-start | bytes 98308
  7.2 26.3 %copy-start.13 = (f32[64]{0:T(128)S(1)}, f32[64]{0:T(128)}, u32[]{:S(2)}) copy-start(f32[64]{0:T(128)} %param.22) | copy-start | bytes 772
  7.2 26.5 %copy-start.10 = (bf16[2,2,64,128]{3,2,1,0:T(8,128)(2,1)S(1)}, bf16[2,2,64,128]{3,2,1,0:T(8,128)(2,1)}, u32[]{:S(2)}) copy-start(bf16[2,2,64,128]{3,2,1,0:T(8,128)(2,1)} %param.24) | copy-start | bytes 196612
  7.2 164.6 %all-gather.2.cloned.1.call-start = ((), (), s32[]{:S(2)}) async-start(), calls=%async_computation.5 | async-start | bytes 19464192 | tf_op jit(solution)/shard_map/all_gather | solution.py:410
  8.4 0.7 collective-permute-start
  9.2 0.9 copy-start.9
  11.7 28.7 %all-to-all-start = ((bf16[32,8,128]{2,1,0:T(8,128)(2,1)}), bf16[32,8,128]{2,1,0:T(8,128)(2,1)S(1)}, u32[]{:S(2)}, u32[]{:S(2)}) async-start(bf16[32,8,128]{2,1,0:T(8,128)(2,1)} %broadcast_in_dim.69), calls=%async_computation | async-start | bytes 131072 | tf_op jit(solution)/shard_map/all_to_all | solution.py:421
  41.1 7.4 %copy-start.14 = (s32[128,1]{0,1:T(1,128)S(1)}, s32[128,1]{0,1:T(1,128)}, u32[]{:S(2)}) copy-start(s32[128,1]{0,1:T(1,128)} %param.29) | copy-start | bytes 1540
  41.1 7.7 %copy-start.3 = (bf16[128,128]{1,0:T(8,128)(2,1)S(1)}, bf16[128,128]{1,0:T(8,128)(2,1)}, u32[]{:S(2)}) copy-start(bf16[128,128]{1,0:T(8,128)(2,1)} %c_ref.3) | copy-start | bytes 98308
  41.1 7.7 %copy-start.6 = (f32[4,4096]{1,0:T(4,128)S(1)}, f32[4,4096]{1,0:T(4,128)}, u32[]{:S(2)}) copy-start(f32[4,4096]{1,0:T(4,128)} %conv_ref.1) | copy-start | bytes 196612
  41.1 7.7 %copy-start.7 = (bf16[128,128]{1,0:T(8,128)(2,1)S(1)}, bf16[128,128]{1,0:T(8,128)(2,1)}, u32[]{:S(2)}) copy-start(bf16[128,128]{1,0:T(8,128)(2,1)} %b_ref.1) | copy-start | bytes 98308
  41.1 7.6 %copy-start.8 = (f32[64]{0:T(128)S(1)}, f32[64]{0:T(128)}, u32[]{:S(2)}) copy-start(f32[64]{0:T(128)} %param.21) | copy-start | bytes 772
  42.2 42.2 %all-to-all-start.1 = ((bf16[32,128,128]{2,1,0:T(8,128)(2,1)}), bf16[32,128,128]{2,1,0:T(8,128)(2,1)S(1)}, u32[]{:S(2)}, u32[]{:S(2)}) async-start(bf16[32,128,128]{2,1,0:T(8,128)(2,1)} %broadcast_select_fusion), calls=%async_computation.1 | async-start | bytes 2097152 | tf_op jit(solution)/shard_map/all_to_all | solution.py:432
  48.8 1.2 copy-start.4
  50.0 1.2 copy-start.5
  61.1 1.0 copy-start.2
  136.8 31.3 %all-to-all-start.3 = ((bf16[4,8,144,128]{3,2,1,0:T(8,128)(2,1)}), bf16[4,8,144,128]{3,2,1,0:T(8,128)(2,1)S(1)}, u32[]{:S(2)}, u32[]{:S(2)}) async-start(bf16[4,8,144,128]{3,2,1,0:T(8,128)(2,1)} %copy-done.2), calls=%async_computation.3 | async-start | bytes 2359296 | tf_op jit(solution)/shard_map/all_to_all | solution.py:470
  142.5 1.1 copy-start
  168.1 3.7 %copy-start.1 = (bf16[192,4096]{1,0:T(8,128)(2,1)S(1)}, bf16[192,4096]{1,0:T(8,128)(2,1)}, u32[]{:S(2)}) copy-start(bf16[192,4096]{1,0:T(8,128)(2,1)} %copy-done) | copy-start | bytes 4718596
  184.9 48.5 %all-to-all-start.4 = ((bf16[16,48,1024]{2,1,0:T(8,128)(2,1)}), bf16[16,48,1024]{2,1,0:T(8,128)(2,1)S(1)}, u32[]{:S(2)}, u32[]{:S(2)}) async-start(bf16[16,48,1024]{2,1,0:T(8,128)(2,1)} %bitcast.16), calls=%async_computation.4 | async-start | bytes 3145728 | tf_op jit(solution)/shard_map/all_to_all | solution.py:475
  193.9 17.1 %collective-permute-start.1 = (bf16[2,144,128]{2,1,0:T(8,128)(2,1)S(1)}, bf16[2,144,128]{2,1,0:T(8,128)(2,1)S(1)}, u32[]{:S(2)}, u32[]{:S(2)}) collective-permute-start(bf16[2,144,128]{2,1,0:T(8,128)(2,1)S(1)} %get-tuple-element.29), channel_id=1, source_target_pairs={{0,64},{64,128},{128,192},{192,256},{256,320},{320,384},{384,448},... | collective-permute-start | bytes 221192 | tf_op jit(solution)/shard_map/ppermute | solution.py:498
  196.4 18.5 %collective-permute-start.2 = (bf16[2,144,128]{2,1,0:T(8,128)(2,1)S(1)}, bf16[2,144,128]{2,1,0:T(8,128)(2,1)S(1)}, u32[]{:S(2)}, u32[]{:S(2)}) collective-permute-start(bf16[2,144,128]{2,1,0:T(8,128)(2,1)S(1)} %get-tuple-element.28), channel_id=1, source_target_pairs={{0,128},{64,192},{128,256},{192,320},{256,384},{320,448},{384,0},{... | collective-permute-start | bytes 221192 | tf_op jit(solution)/shard_map/ppermute | solution.py:498
  198.3 19.1 %collective-permute-start.3 = (bf16[2,144,128]{2,1,0:T(8,128)(2,1)S(1)}, bf16[2,144,128]{2,1,0:T(8,128)(2,1)S(1)}, u32[]{:S(2)}, u32[]{:S(2)}) collective-permute-start(bf16[2,144,128]{2,1,0:T(8,128)(2,1)S(1)} %get-tuple-element.27), channel_id=1, source_target_pairs={{0,192},{64,256},{128,320},{192,384},{256,448},{320,0},{384,64},{4... | collective-permute-start | bytes 221192 | tf_op jit(solution)/shard_map/ppermute | solution.py:498
  200.2 17.1 %collective-permute-start.4 = (bf16[2,144,128]{2,1,0:T(8,128)(2,1)S(1)}, bf16[2,144,128]{2,1,0:T(8,128)(2,1)S(1)}, u32[]{:S(2)}, u32[]{:S(2)}) collective-permute-start(bf16[2,144,128]{2,1,0:T(8,128)(2,1)S(1)} %get-tuple-element.26), channel_id=1, source_target_pairs={{0,256},{64,320},{128,384},{192,448},{256,0},{320,64},{384,128},{4... | collective-permute-start | bytes 221192 | tf_op jit(solution)/shard_map/ppermute | solution.py:498
  208.1 13.1 %collective-permute-start.5 = (bf16[2,144,128]{2,1,0:T(8,128)(2,1)S(1)}, bf16[2,144,128]{2,1,0:T(8,128)(2,1)S(1)}, u32[]{:S(2)}, u32[]{:S(2)}) collective-permute-start(bf16[2,144,128]{2,1,0:T(8,128)(2,1)S(1)} %get-tuple-element.25), channel_id=1, source_target_pairs={{0,320},{64,384},{128,448},{192,0},{256,64},{320,128},{384,192},{4... | collective-permute-start | bytes 221192 | tf_op jit(solution)/shard_map/ppermute | solution.py:498
  211.0 10.5 %collective-permute-start.6 = (bf16[2,144,128]{2,1,0:T(8,128)(2,1)S(1)}, bf16[2,144,128]{2,1,0:T(8,128)(2,1)S(1)}, u32[]{:S(2)}, u32[]{:S(2)}) collective-permute-start(bf16[2,144,128]{2,1,0:T(8,128)(2,1)S(1)} %get-tuple-element.24), channel_id=1, source_target_pairs={{0,384},{64,448},{128,0},{192,64},{256,128},{320,192},{384,256},{4... | collective-permute-start | bytes 221192 | tf_op jit(solution)/shard_map/ppermute | solution.py:498
  214.9 9.6 %collective-permute-start.7 = (bf16[2,144,128]{2,1,0:T(8,128)(2,1)S(1)}, bf16[2,144,128]{2,1,0:T(8,128)(2,1)S(1)}, u32[]{:S(2)}, u32[]{:S(2)}) collective-permute-start(bf16[2,144,128]{2,1,0:T(8,128)(2,1)S(1)} %get-tuple-element.23), channel_id=1, source_target_pairs={{0,448},{64,0},{128,64},{192,128},{256,192},{320,256},{384,320},{4... | collective-permute-start | bytes 221192 | tf_op jit(solution)/shard_map/ppermute | solution.py:498
  234.8 0.7 copy-start.15
Sparse Core Ops, SparseCore 0:
  10.2 161.5 all-gather.1

commit v6 on v5

--- a/solution.py
+++ b/solution.py
@@ -107,8 +107,9 @@
         0,
     ).astype(jnp.bfloat16)
     for k in range(places):
-        sent_ref[k, 0, :lanes] = state_grad[k * lanes : (k + 1) * lanes]
-        sent_ref[k, 0, lanes:] = taps_grad[:, k * lanes : (k + 1) * lanes]
+        slot = lax.rem(k - row_ref[1] + places, places)
+        sent_ref[slot, 0, :lanes] = state_grad[k * lanes : (k + 1) * lanes]
+        sent_ref[slot, 0, lanes:] = taps_grad[:, k * lanes : (k + 1) * lanes]
 
 
 def mixer_base(
@@ -172,8 +173,13 @@
 ):
     group = pl.program_id(0)
     steps_n, width = base_ref.shape
+    size_x, size_y = state_ref.shape[:2]
+    lanes = width // (size_x * size_y)
+    state = jnp.concatenate(
+        [state_ref[x, y, :lanes] for y in range(size_y) for x in range(size_x)], 0
+    )
     carried = lax.dot_general(
-        c_ref[...], state_ref[...], (((1,), (1,)), ((), ())), preferred_element_type=jnp.float32
+        c_ref[...], state, (((1,), (1,)), ((), ())), preferred_element_type=jnp.float32
     )
     grow = spread(grow_ref[...], group * width, width, head_size)
     live = lax.broadcasted_iota(jnp.int32, (steps_n, width), 0) < length_ref[0]
@@ -198,14 +204,15 @@
 
 def dispatch(length, base, state, c_rows, grow, spot, head_size, slots, packed):
     steps_n, channels = base.shape
-    state_n, heads, width = state.shape[1], grow.shape[1], channels // GROUPS
+    size_x, size_y, state_rows, state_n = state.shape
+    heads, width = grow.shape[1], channels // GROUPS
     return pl.pallas_call(
         functools.partial(dispatch_kernel, head_size, slots),
         grid=(GROUPS,),
         in_specs=[
             pl.BlockSpec(memory_space=pltpu.SMEM),
             pl.BlockSpec((steps_n, width), lambda g: (0, g)),
-            pl.BlockSpec((width, state_n), lambda g: (g, 0)),
+            pl.BlockSpec((size_x, size_y // GROUPS, state_rows, state_n), lambda g: (0, g, 0, 0)),
             pl.BlockSpec((steps_n, state_n), lambda g: (0, 0)),
             pl.BlockSpec((steps_n, heads), lambda g: (0, 0)),
             pl.BlockSpec((1, steps_n), lambda g: (0, 0)),
@@ -309,32 +316,58 @@
     )(rows, weights)
 
 
-def presum_kernel(row_ref, members_ref, column_ref, out_ref, total_ref):
-    size_x = column_ref.shape[0]
+def combine_kernel(slots, spot_ref, gain_ref, returned_ref, out_ref):
+    steps_n, packed = out_ref.shape[0], returned_ref.shape[0]
+    spots = lax.broadcasted_iota(jnp.int32, (steps_n, packed), 1)
+    pick = (spots == spot_ref[...] + pl.program_id(0) * slots).astype(jnp.bfloat16)
+    rows = jnp.dot(pick, returned_ref[...], preferred_element_type=jnp.float32)
+    out_ref[...] = (gain_ref[...] * rows).astype(jnp.bfloat16)
+
+
+def combine(spot, gain, returned, slots):
+    packed, width = returned.shape
+    steps_n = spot.shape[0]
+    column = pl.BlockSpec((steps_n, 1), lambda g: (0, 0))
+    return pl.pallas_call(
+        functools.partial(combine_kernel, slots),
+        grid=(GROUPS,),
+        in_specs=[column, column, pl.BlockSpec((packed, width), lambda g: (0, 0))],
+        out_specs=pl.BlockSpec((steps_n, width), lambda g: (0, g)),
+        out_shape=jax.ShapeDtypeStruct((steps_n, GROUPS * width), jnp.bfloat16),
+        compiler_params=pltpu.CompilerParams(vmem_limit_bytes=24 * 1024 * 1024),
+        cost_estimate=pl.CostEstimate(
+            flops=2 * GROUPS * steps_n * packed * width,
+            bytes_accessed=2 * packed * width + 2 * GROUPS * steps_n * width,
+            transcendentals=0,
+        ),
+    )(spot, gain, returned)
+
+
+def presum_kernel(members_ref, *refs):
+    pieces, (out_ref, total_ref) = refs[:-2], refs[-2:]
     total_ref[...] = jnp.zeros_like(total_ref)
-    for k in range(size_x):
-        member = members_ref[row_ref[0] * size_x + k]
-        total_ref[member] += column_ref[k, 0].astype(jnp.float32)
+    for k, piece in enumerate(pieces):
+        total_ref[members_ref[k]] += piece[0].astype(jnp.float32)
     out_ref[0] = total_ref[...].astype(jnp.bfloat16)
 
 
-def presum(row, members, column, prompts):
-    size_x, size_y, rows, lanes = column.shape
+def presum(members, pieces, prompts):
+    size_y, rows, lanes = pieces[0].shape
     smem = pl.BlockSpec(memory_space=pltpu.SMEM)
     return pl.pallas_call(
         presum_kernel,
         grid=(size_y,),
-        in_specs=[smem, smem, pl.BlockSpec((size_x, 1, rows, lanes), lambda i: (0, i, 0, 0))],
+        in_specs=[smem] + [pl.BlockSpec((1, rows, lanes), lambda i: (i, 0, 0))] * len(pieces),
         out_specs=pl.BlockSpec((1, prompts, rows, lanes), lambda i: (i, 0, 0, 0)),
         out_shape=jax.ShapeDtypeStruct((size_y, prompts, rows, lanes), jnp.bfloat16),
         scratch_shapes=[pltpu.VMEM((prompts, rows, lanes), jnp.float32)],
         compiler_params=pltpu.CompilerParams(vmem_limit_bytes=16 * 1024 * 1024),
         cost_estimate=pl.CostEstimate(
-            flops=size_x * size_y * rows * lanes,
-            bytes_accessed=3 * size_x * size_y * rows * lanes,
+            flops=len(pieces) * size_y * rows * lanes,
+            bytes_accessed=3 * len(pieces) * size_y * rows * lanes,
             transcendentals=0,
         ),
-    )(row, members, column)
+    )(members, *pieces)
 
 
 def collect_kernel(*refs):
@@ -396,7 +429,6 @@
     steps_n, row_width = ssm_input.shape
     prompts, own_heads, head_size, state_n = prompt_state.shape
     taps_n, lanes = prompt_taps.shape[2] // head_size, own_heads * head_size
-    owners = lax.axis_size(PLANE)
     lines, expert_count = lax.axis_size(("xh", "z")), lax.axis_size(("z", "c"))
     state_rows = own_heads * head_size
 
@@ -409,32 +441,50 @@
     swapped = lax.ppermute(stacked, ("xh", "xl", "c"), swap)
     weights = lax.all_gather(swapped, ("y", "xl", "c"), axis=1, tiled=True)
 
-    row = lax.axis_index("y").astype(jnp.int32)[None]
+    size_y = lax.axis_size("y")
+    x_axes = ("xh", "xl")
+    x_index = lax.axis_index(x_axes).astype(jnp.int32)
+    place_here = jnp.stack([lax.axis_index("y").astype(jnp.int32), x_index])
 
     own_taps = jnp.transpose(
         prompt_taps.reshape(prompts, own_heads, taps_n, head_size), (0, 2, 1, 3)
-    ).reshape(prompts * taps_n, lanes)
-    own_member = jnp.broadcast_to(group_index.astype(jnp.bfloat16)[:, None], (1, lanes))
-    notice = jnp.concatenate(
-        [own_taps, own_member, jnp.zeros((7 - prompts * taps_n, lanes), jnp.bfloat16)], 0
-    )
-    notices = lax.all_to_all(
-        jnp.broadcast_to(notice[None], (owners,) + notice.shape), PLANE, 0, 0, tiled=True
-    )
-    members = notices[:, prompts * taps_n, 0] > 0.5
-    mine = group_index[0] == 1
-    prior = jnp.where(mine, notices[:, taps_n : 2 * taps_n], notices[:, :taps_n])
-    prior = jnp.transpose(prior, (1, 0, 2)).reshape(taps_n, row_width).astype(jnp.float32)
+    ).reshape(prompts, taps_n, lanes)
+    held = jnp.concatenate(
+        [
+            prompt_state.reshape(prompts, state_rows, state_n),
+            own_taps,
+            jnp.zeros((prompts, 16 - taps_n, lanes), jnp.bfloat16),
+        ],
+        1,
+    )
+    column_state = lax.all_to_all(
+        jnp.broadcast_to(held[None], (size_y,) + held.shape), "y", 0, 0, tiled=True
+    )
+    back = [group_index] + [
+        lax.ppermute(group_index, x_axes, [(i, (i + d) % size_x) for i in range(size_x)])
+        for d in range(1, size_x)
+    ]
+    behind = jnp.concatenate(back)
+    steps_back = (x_index - lax.iota(jnp.int32, size_x)) % size_x
+    picked = steps_back[:, None] == lax.iota(jnp.int32, size_x)[None, :]
+    row_members = jnp.sum(jnp.where(picked, behind[None, :], 0), axis=1)
+    state = lax.all_to_all(
+        jnp.where(
+            (row_members == 1)[:, None, None, None], column_state[:, 1][None], column_state[:, 0][None]
+        ),
+        x_axes,
+        0,
+        0,
+        tiled=True,
+    )
+    prior = jnp.transpose(state[:, :, state_rows : state_rows + taps_n], (2, 1, 0, 3))
+    prior = prior.reshape(taps_n, row_width).astype(jnp.float32)
     prior = jnp.concatenate([jnp.zeros((8 - taps_n, row_width), jnp.float32), prior], 0)
-
-    held = prompt_state.reshape(prompts, state_rows, state_n)
-    outgoing_state = jnp.where(members[:, None, None], held[1][None], held[0][None])
-    state = lax.all_to_all(outgoing_state, PLANE, 0, 0, tiled=True).reshape(row_width, state_n)
 
     step_size = jax.nn.softplus(step_raw)
     base, outgoing_grad, grow = mixer_base(
         lengths,
-        row,
+        place_here,
         ssm_input,
         prior,
         conv_weight,
@@ -445,7 +495,7 @@
         step_size,
         decay_rate[None, :],
         head_size,
-        (lax.axis_size("y"), lax.axis_size(("xh", "xl"))),
+        (size_y, size_x),
     )
 
     slots = 3 * steps_n // (2 * expert_count)
@@ -466,12 +516,16 @@
         tiled=True,
         axis_index_groups=neighbours(size_x, size_z),
     )
-    arrived, outgoing_grad = lax.optimization_barrier((arrived, outgoing_grad))
-    column_grad = lax.all_to_all(outgoing_grad, ("xh", "xl"), 0, 0, tiled=True)
     expert_rows = unpack(arrived.reshape(packed_rows, width), slots, lines)
+    weights, *leaving = lax.optimization_barrier(
+        (weights, *(outgoing_grad[d] for d in range(size_x)))
+    )
+    column_grad = [leaving[0]] + [
+        lax.ppermute(leaving[d], x_axes, [(i, (i + d) % size_x) for i in range(size_x)])
+        for d in range(1, size_x)
+    ]
     produced = expert_apply(expert_rows, weights, slots, lines)
-    row_grad = presum(row, members.astype(jnp.int32), column_grad, prompts)
-    produced, row_grad = lax.optimization_barrier((produced, row_grad))
+    row_grad = presum(behind, column_grad, prompts)
     returned = lax.all_to_all(
         produced.reshape(lines, GROUPS * slots, width),
         LINE,
@@ -480,20 +534,6 @@
         tiled=True,
         axis_index_groups=neighbours(size_x, size_z),
     ).reshape(packed_rows, width)
-    spots = lax.iota(jnp.int32, packed_rows)
-    placing = [
-        (spots[:, None] == spot + group * slots).astype(jnp.bfloat16) for group in range(GROUPS)
-    ]
-    per_token = jnp.concatenate(
-        [
-            lax.dot_general(
-                placing[group], returned, (((0,), (0,)), ((), ())), preferred_element_type=jnp.float32
-            )
-            for group in range(GROUPS)
-        ],
-        1,
-    )
-    size_y = lax.axis_size("y")
     pieces = [row_grad[0]] + [
         lax.ppermute(row_grad[d], "y", [(i, (i + d) % size_y) for i in range(size_y)])
         for d in range(1, size_y)
@@ -503,7 +543,7 @@
     taps_grad = jnp.transpose(
         taps_sum[:, :taps_n].reshape(prompts, taps_n, own_heads, head_size), (0, 2, 1, 3)
     ).reshape(prompts, own_heads, taps_n * head_size)
-    moe_out = (route_gain * per_token).astype(jnp.bfloat16)
+    moe_out = combine(jnp.transpose(spot), route_gain, returned, slots)
     return (moe_out, state_grad, taps_grad)
 
 

time: 245 us -> 249 us (1.016)
  blocking collectives: 46.8 us -> 0 us
  waiting for transfers between devices: 70.5 us -> 95.2 us
  starting transfers between devices: 63.7 us -> 86.8 us
  Pallas kernels: 32.7 us -> 37.1 us
    all_to_all x1 -> x0, blocking collectives: 46.8 us -> none  [shards(): lax.all_to_all(outgoing.reshape(lines, GROUPS * slots, width), LINE, 0, 0...]
    ppermute x0 -> x6, starting transfers between devices: none -> 30.3 us  [the longest x3 19.3 us: shards(): lax.ppermute(group_index, x_axes, [(i, (i + d) % size_x) for i in range(s...]
    ppermute x0 -> x6, waiting for transfers between devices: none -> 23.1 us  [the longest x3 19.8 us: shards(): lax.ppermute(leaving[d], x_axes, [(i, (i + d) % size_x) for i in range(si...]
    all_to_all x3, waiting for transfers between devices: 53.4 us -> 63.7 us  [the longest x1 35.6 us: shards(): lax.all_to_all(outgoing.reshape(lines, GROUPS * slots, width), LINE, 0, 0...]
    all_to_all x1, waiting for transfers between devices: 7.56 us -> 0.01 us  [shards(): lax.all_to_all(produced.reshape(lines, GROUPS * slots, width), LINE, 0, 0...]
    all_to_all x3, starting transfers between devices: 30.8 us -> 23.4 us  [the longest x1 11.1 us: shards(): lax.all_to_all(outgoing.reshape(lines, GROUPS * slots, width), LINE, 0, 0...]
    pallas_call x1 -> x2, Pallas kernels: 1.21 us -> 3.79 us  [the longest x1 2.71 us: combine(): pl.pallas_call(functools.partial(combine_kernel, slots), grid=(GROUPS,),...]
    unnamed x33 -> x35, local copies, waits for them, and re-layouts: 5.8 us -> 3.65 us
  transfers between devices with their start and end apart: 13 -> 19, of which waited for: 8 -> 9; matrix products, arithmetic and copies ran while one was open for 2% -> 3% of each run, Pallas kernels for 8% -> 9%
where the time goes in v6:
time: 249 us; the launch traced here: 247 us
  waiting for transfers between devices  95.2 us (38%)
  starting transfers between devices  86.8 us (35%)
  Pallas kernels  37.1 us (15%)
  between operations  15.8 us (6%)
  local copies, waits for them, and re-layouts  7.07 us (3%)
  other arithmetic  5.03 us (2%)
    all_to_all x1, waiting for transfers between devices, shards(): lax.all_to_all(outgoing.reshape(lines, GROUPS * slots, width), LINE, 0, 0...  35.6 us
    all_to_all x1, waiting for transfers between devices, shards(): lax.all_to_all(jnp.where((row_members == 1)[:, None, None, None], column_...  28.1 us
    ppermute x7, starting transfers between devices, shards(): lax.ppermute(row_grad[d], 'y', [(i, (i + d) % size_y) for i in range(size...  23.3 us
    ppermute x3, waiting for transfers between devices, shards(): lax.ppermute(leaving[d], x_axes, [(i, (i + d) % size_x) for i in range(si...  19.8 us
    ppermute x3, starting transfers between devices, shards(): lax.ppermute(group_index, x_axes, [(i, (i + d) % size_x) for i in range(s...  19.3 us
    pallas_call x1, Pallas kernels, expert_apply(): pl.pallas_call(functools.partial(expert_kernel, slots, sources), grid=(un...  13.1 us
    all_to_all x1, starting transfers between devices, shards(): lax.all_to_all(outgoing.reshape(lines, GROUPS * slots, width), LINE, 0, 0...  11.1 us
    ppermute x3, starting transfers between devices, shards(): lax.ppermute(leaving[d], x_axes, [(i, (i + d) % size_x) for i in range(si...  11 us
  transfers between devices with their start and end apart: 19, of which 9 were waited for; matrix products, arithmetic and copies ran while one was open for 3% of the time, Pallas kernels for 9%

profile of v6, /device:TPU:56, one launch (start us, length us, event | category | flops | bytes accessed | tf_op | source)
XLA Modules:
  0.0 247.0 jit_solution(6054374334972345075)
XLA Ops:
  7.2 0.0 all-gather.2.cloned.1.call-start
  7.2 1.2 pad_maximum_fusion
  8.4 0.7 collective-permute-start.3
  9.1 0.8 copy-done.6
  10.0 0.0 all-gather.2.cloned.1.call-update
  10.0 0.1 reshape.175
  10.1 0.1 reshape.184
  10.2 0.1 pad.7.clone
  10.3 0.1 maximum_maximum_fusion
  10.3 0.9 broadcast_in_dim.67
  11.2 8.6 %all-to-all-start = ((bf16[8,2,144,128]{3,2,1,0:T(8,128)(2,1)}), bf16[8,2,144,128]{3,2,1,0:T(8,128)(2,1)S(1)}, u32[]{:S(2)}, u32[]{:S(2)}) async-start(bf16[8,2,144,128]{3,2,1,0:T(8,128)(2,1)} %broadcast_in_dim.67), calls=%async_computation | async-start | bytes 1179648 | tf_op jit(solution)/shard_map/all_to_all | solution.py:460
  19.9 14.6 %collective-permute-start.2 = (s32[1]{0:T(128)}, s32[1]{0:T(128)}, u32[]{:S(2)}, u32[]{:S(2)}) collective-permute-start(s32[1]{0:T(128)} %param.26), channel_id=1, source_target_pairs={{0,48},{16,0},{32,16},{48,32},{1,49},{17,1},{33,17},{49,33},{2,50}... | collective-permute-start | bytes 20 | tf_op jit(solution)/shard_map/ppermute | solution.py:464
  34.5 1.9 collective-permute-start.1
  36.4 2.8 %collective-permute-start = (s32[1]{0:T(128)}, s32[1]{0:T(128)}, u32[]{:S(2)}, u32[]{:S(2)}) collective-permute-start(s32[1]{0:T(128)} %param.26), channel_id=1, source_target_pairs={{0,16},{16,32},{32,48},{48,0},{1,17},{17,33},{33,49},{49,1},{2,18}... | collective-permute-start | bytes 20 | tf_op jit(solution)/shard_map/ppermute | solution.py:464
  39.9 1.8 collective-permute-done.1
  41.6 1.5 collective-permute-done
  43.1 2.0 pad_add_fusion.1.members_ref
  45.1 0.2 select_reduce_fusion
  45.4 1.2 broadcast_select_fusion
  46.6 0.0 copy-start.3
  46.6 0.0 copy-start.4
  46.6 3.7 %all-to-all-start.1 = ((bf16[4,8,144,128]{3,2,1,0:T(8,128)(2,1)}), bf16[4,8,144,128]{3,2,1,0:T(8,128)(2,1)S(1)}, u32[]{:S(2)}, u32[]{:S(2)}) async-start(bf16[4,8,144,128]{3,2,1,0:T(8,128)(2,1)} %broadcast_select_fusion), calls=%async_computation.1 | async-start | bytes 2359296 | tf_op jit(solution)/shard_map/all_to_all | solution.py:471
  51.0 0.1 broadcast_in_dim.72
  51.1 0.1 broadcast_in_dim_reshape.3.skip_ref
  51.2 0.1 copy.104
  51.3 0.1 pad_add_fusion.row_ref
  51.4 0.1 convert_reduce_fusion
  51.6 28.1 %all-to-all-done.1.state_ref = bf16[4,8,144,128]{3,2,1,0:T(8,128)(2,1)S(1)} async-done(((bf16[4,8,144,128]{3,2,1,0:T(8,128)(2,1)}), bf16[4,8,144,128]{3,2,1,0:T(8,128)(2,1)S(1)}, u32[]{:S(2)}, u32[]{:S(2)}) %all-to-all-start.1) | async-done | bytes 1179680 | tf_op jit(solution)/shard_map/all_to_all | solution.py:471
  79.8 0.0 copy-start.1
  79.8 1.2 copy-done.1
  81.0 1.2 copy-done.2
  82.2 10.5 %shard_map.184 = (f32[128,4096]{1,0:T(8,128)S(1)}, bf16[4,8,144,128]{3,2,1,0:T(8,128)(2,1)S(1)}, f32[128,64]{1,0:T(8,128)S(1)}) custom-call(s32[1]{0:T(128)S(6)} %copy.117.length_ref, s32[2]{0:T(128)S(1)} %pad_add_fusion.row_ref, bf16[128,4096]{1,0:T(8,128)(2,1)S(1)} %copy-done.1, f32[8,4096]{1,0:T(8,128)S(1)} %pad_convert_fusion.prior_ref, ...), custom_call_target="tpu_custom_call" | custom-call | flops 1342177280 | bytes 5242880 | tf_op jit(solution)/shard_map/pallas_call | solution.py:126
  92.8 6.8 %shard_map.185 = bf16[768,1024]{1,0:T(8,128)(2,1)} custom-call(s32[1]{0:T(128)S(6)} %copy.117.length_ref, f32[128,4096]{1,0:T(8,128)S(1)} %get-tuple-element.13.base_ref, bf16[4,8,144,128]{3,2,1,0:T(8,128)(2,1)S(1)} %all-to-all-done.1.state_ref, bf16[128,128]{1,0:T(8,128)(2,1)S(1)} %copy-done, f32[128,64]{1,0:T(8,128)S(1)} %get-tuple-element.14.grow_ref, ...), custom_call_target="tpu_custom_call" | custom-call | flops 939524096 | bytes 4718592 | tf_op jit(solution)/shard_map/pallas_call | solution.py:209
  99.6 11.1 %all-to-all-start.2 = ((bf16[16,48,1024]{2,1,0:T(8,128)(2,1)}), bf16[16,48,1024]{2,1,0:T(8,128)(2,1)S(1)}, u32[]{:S(2)}, u32[]{:S(2)}) async-start(bf16[16,48,1024]{2,1,0:T(8,128)(2,1)} %bitcast.12), calls=%async_computation.2 | async-start | bytes 3145728 | tf_op jit(solution)/shard_map/all_to_all | solution.py:511
  110.7 1.0 slice_bitcast_fusion.2
  111.6 35.6 %all-to-all-done.2 = bf16[16,48,1024]{2,1,0:T(8,128)(2,1)S(1)} async-done(((bf16[16,48,1024]{2,1,0:T(8,128)(2,1)}), bf16[16,48,1024]{2,1,0:T(8,128)(2,1)S(1)}, u32[]{:S(2)}, u32[]{:S(2)}) %all-to-all-start.2) | async-done | bytes 1572896 | tf_op jit(solution)/shard_map/all_to_all | solution.py:511
  147.3 2.1 shard_map.186.rows_ref
  149.3 1.9 all-gather.2.cloned.1.call-done.weight_ref
  151.2 13.1 %shard_map.187 = bf16[768,1024]{1,0:T(8,128)(2,1)} custom-call(bf16[192,4096]{1,0:T(8,128)(2,1)S(1)} %shard_map.186.rows_ref, bf16[3,768,4096]{2,1,0:T(8,128)(2,1)} %all-gather.2.cloned.1.call-done.weight_ref), custom_call_target="tpu_custom_call" | custom-call | flops 3623878656 | bytes 22020096 | tf_op jit(solution)/shard_map/pallas_call | solution.py:300
  164.4 9.0 %all-to-all-start.3 = ((bf16[16,48,1024]{2,1,0:T(8,128)(2,1)}), bf16[16,48,1024]{2,1,0:T(8,128)(2,1)S(1)}, u32[]{:S(2)}, u32[]{:S(2)}) async-start(bf16[16,48,1024]{2,1,0:T(8,128)(2,1)} %bitcast.18), calls=%async_computation.3 | async-start | bytes 3145728 | tf_op jit(solution)/shard_map/all_to_all | solution.py:529
  173.4 2.5 %collective-permute-start.4 = (bf16[8,144,128]{2,1,0:T(8,128)(2,1)S(1)}, bf16[8,144,128]{2,1,0:T(8,128)(2,1)S(1)}, u32[]{:S(2)}, u32[]{:S(2)}) collective-permute-start(bf16[8,144,128]{2,1,0:T(8,128)(2,1)S(1)} %copy-done.9), channel_id=1, source_target_pairs={{0,16},{16,32},{32,48},{48,0},{1,17},{17,33},{33,49},{49,1},{2,18}... | collective-permute-start | bytes 884744 | tf_op jit(solution)/shard_map/ppermute | solution.py:524
  176.0 5.9 %collective-permute-start.5 = (bf16[8,144,128]{2,1,0:T(8,128)(2,1)S(1)}, bf16[8,144,128]{2,1,0:T(8,128)(2,1)S(1)}, u32[]{:S(2)}, u32[]{:S(2)}) collective-permute-start(bf16[8,144,128]{2,1,0:T(8,128)(2,1)S(1)} %copy-done.8), channel_id=1, source_target_pairs={{0,32},{16,48},{32,0},{48,16},{1,33},{17,49},{33,1},{49,17},{2,34}... | collective-permute-start | bytes 884744 | tf_op jit(solution)/shard_map/ppermute | solution.py:524
  181.9 2.5 %collective-permute-start.6 = (bf16[8,144,128]{2,1,0:T(8,128)(2,1)S(1)}, bf16[8,144,128]{2,1,0:T(8,128)(2,1)S(1)}, u32[]{:S(2)}, u32[]{:S(2)}) collective-permute-start(bf16[8,144,128]{2,1,0:T(8,128)(2,1)S(1)} %copy-done.7), channel_id=1, source_target_pairs={{0,48},{16,0},{32,16},{48,32},{1,49},{17,1},{33,17},{49,33},{2,50}... | collective-permute-start | bytes 884744 | tf_op jit(solution)/shard_map/ppermute | solution.py:524
  184.5 19.8 %collective-permute-done.4.refs_1_ = bf16[8,144,128]{2,1,0:T(8,128)(2,1)S(1)} collective-permute-done((bf16[8,144,128]{2,1,0:T(8,128)(2,1)S(1)}, bf16[8,144,128]{2,1,0:T(8,128)(2,1)S(1)}, u32[]{:S(2)}, u32[]{:S(2)}) %collective-permute-start.4) | collective-permute-done | bytes 294944 | tf_op jit(solution)/shard_map/ppermute | solution.py:524
  204.2 1.1 shard_map.189
  205.4 2.4 collective-permute-start.7
  207.8 1.9 collective-permute-start.8
  209.8 0.1 copy.93
  209.9 0.1 copy.100
  210.0 0.1 copy.96
  210.2 2.3 collective-permute-start.9
  212.5 7.4 %collective-permute-start.10 = (bf16[2,144,128]{2,1,0:T(8,128)(2,1)S(1)}, bf16[2,144,128]{2,1,0:T(8,128)(2,1)S(1)}, u32[]{:S(2)}, u32[]{:S(2)}) collective-permute-start(bf16[2,144,128]{2,1,0:T(8,128)(2,1)S(1)} %get-tuple-element.30), channel_id=1, source_target_pairs={{0,256},{64,320},{128,384},{192,448},{256,0},{320,64},{384,128},{4... | collective-permute-start | bytes 221192 | tf_op jit(solution)/shard_map/ppermute | solution.py:538
  219.9 2.8 %collective-permute-start.11 = (bf16[2,144,128]{2,1,0:T(8,128)(2,1)S(1)}, bf16[2,144,128]{2,1,0:T(8,128)(2,1)S(1)}, u32[]{:S(2)}, u32[]{:S(2)}) collective-permute-start(bf16[2,144,128]{2,1,0:T(8,128)(2,1)S(1)} %get-tuple-element.29), channel_id=1, source_target_pairs={{0,320},{64,384},{128,448},{192,0},{256,64},{320,128},{384,192},{4... | collective-permute-start | bytes 221192 | tf_op jit(solution)/shard_map/ppermute | solution.py:538
  222.8 3.9 %collective-permute-start.12 = (bf16[2,144,128]{2,1,0:T(8,128)(2,1)S(1)}, bf16[2,144,128]{2,1,0:T(8,128)(2,1)S(1)}, u32[]{:S(2)}, u32[]{:S(2)}) collective-permute-start(bf16[2,144,128]{2,1,0:T(8,128)(2,1)S(1)} %get-tuple-element.28), channel_id=1, source_target_pairs={{0,384},{64,448},{128,0},{192,64},{256,128},{320,192},{384,256},{4... | collective-permute-start | bytes 221192 | tf_op jit(solution)/shard_map/ppermute | solution.py:538
  226.7 2.5 %collective-permute-start.13 = (bf16[2,144,128]{2,1,0:T(8,128)(2,1)S(1)}, bf16[2,144,128]{2,1,0:T(8,128)(2,1)S(1)}, u32[]{:S(2)}, u32[]{:S(2)}) collective-permute-start(bf16[2,144,128]{2,1,0:T(8,128)(2,1)S(1)} %get-tuple-element.27), channel_id=1, source_target_pairs={{0,448},{64,0},{128,64},{192,128},{256,192},{320,256},{384,320},{4... | collective-permute-start | bytes 221192 | tf_op jit(solution)/shard_map/ppermute | solution.py:538
  229.2 0.1 fusion.3.spot_ref
  229.3 0.1 copy.109.gain_ref
  229.4 3.0 %collective-permute-done.11.refs_5_ = bf16[2,144,128]{2,1,0:T(8,128)(2,1)S(1)} collective-permute-done((bf16[2,144,128]{2,1,0:T(8,128)(2,1)S(1)}, bf16[2,144,128]{2,1,0:T(8,128)(2,1)S(1)}, u32[]{:S(2)}, u32[]{:S(2)}) %collective-permute-start.11) | collective-permute-done | bytes 73760 | tf_op jit(solution)/shard_map/ppermute | solution.py:538
  232.4 1.0 collective-permute-done.12.refs_6_
  233.5 2.5 %collective-permute-done.13.refs_7_ = bf16[2,144,128]{2,1,0:T(8,128)(2,1)S(1)} collective-permute-done((bf16[2,144,128]{2,1,0:T(8,128)(2,1)S(1)}, bf16[2,144,128]{2,1,0:T(8,128)(2,1)S(1)}, u32[]{:S(2)}, u32[]{:S(2)}) %collective-permute-start.13) | collective-permute-done | bytes 73760 | tf_op jit(solution)/shard_map/ppermute | solution.py:538
  235.9 0.7 shard_map.190
  236.7 0.1 reshape.182
  236.8 0.7 reshape.183
  237.4 2.7 %shard_map.188 = bf16[128,4096]{1,0:T(8,128)(2,1)} custom-call(s32[128,1]{1,0:T(8,128)S(1)} %fusion.3.spot_ref, f32[128,1]{1,0:T(8,128)S(1)} %copy.109.gain_ref, bf16[768,1024]{1,0:T(8,128)(2,1)S(1)} %bitcast.62), custom_call_target="tpu_custom_call" | custom-call | flops 805306368 | bytes 2621440 | tf_op jit(solution)/shard_map/pallas_call | solution.py:331
  (52 shorter events, 0.3 us)
Async XLA Ops:
  7.2 2.8 %copy-start.12 = (bf16[2,2,192]{2,1,0:T(2,128)(2,1)S(1)}, bf16[2,2,192]{2,1,0:T(2,128)(2,1)}, u32[]{:S(2)}) copy-start(bf16[2,2,192]{2,1,0:T(2,128)(2,1)} %param.25) | copy-start | bytes 4612
  7.2 3.1 %copy-start.10 = (bf16[2,2,64,128]{3,2,1,0:T(8,128)(2,1)S(1)}, bf16[2,2,64,128]{3,2,1,0:T(8,128)(2,1)}, u32[]{:S(2)}) copy-start(bf16[2,2,64,128]{3,2,1,0:T(8,128)(2,1)} %param.24) | copy-start | bytes 196612
  7.2 144.1 %all-gather.2.cloned.1.call-start = ((), (), s32[]{:S(2)}) async-start(), calls=%async_computation.4 | async-start | bytes 19464192 | tf_op jit(solution)/shard_map/all_gather | solution.py:442
  8.4 0.7 collective-permute-start.3
  9.1 0.8 copy-start.6
  11.2 34.1 %all-to-all-start = ((bf16[8,2,144,128]{3,2,1,0:T(8,128)(2,1)}), bf16[8,2,144,128]{3,2,1,0:T(8,128)(2,1)S(1)}, u32[]{:S(2)}, u32[]{:S(2)}) async-start(bf16[8,2,144,128]{3,2,1,0:T(8,128)(2,1)} %broadcast_in_dim.67), calls=%async_computation | async-start | bytes 1179648 | tf_op jit(solution)/shard_map/all_to_all | solution.py:460
  19.9 20.0 %collective-permute-start.2 = (s32[1]{0:T(128)}, s32[1]{0:T(128)}, u32[]{:S(2)}, u32[]{:S(2)}) collective-permute-start(s32[1]{0:T(128)} %param.26), channel_id=1, source_target_pairs={{0,48},{16,0},{32,16},{48,32},{1,49},{17,1},{33,17},{49,33},{2,50}... | collective-permute-start | bytes 20 | tf_op jit(solution)/shard_map/ppermute | solution.py:464
  34.5 7.2 %collective-permute-start.1 = (s32[1]{0:T(128)}, s32[1]{0:T(128)}, u32[]{:S(2)}, u32[]{:S(2)}) collective-permute-start(s32[1]{0:T(128)} %param.26), channel_id=1, source_target_pairs={{0,32},{16,48},{32,0},{48,16},{1,33},{17,49},{33,1},{49,17},{2,34}... | collective-permute-start | bytes 20 | tf_op jit(solution)/shard_map/ppermute | solution.py:464
  36.4 6.7 %collective-permute-start = (s32[1]{0:T(128)}, s32[1]{0:T(128)}, u32[]{:S(2)}, u32[]{:S(2)}) collective-permute-start(s32[1]{0:T(128)} %param.26), channel_id=1, source_target_pairs={{0,16},{16,32},{32,48},{48,0},{1,17},{17,33},{33,49},{49,1},{2,18}... | collective-permute-start | bytes 20 | tf_op jit(solution)/shard_map/ppermute | solution.py:464
  46.6 4.4 %copy-start.13 = (f32[64]{0:T(128)S(1)}, f32[64]{0:T(128)}, u32[]{:S(2)}) copy-start(f32[64]{0:T(128)} %param.22) | copy-start | bytes 772
  46.6 4.6 %copy-start.11 = (f32[128,64]{0,1:T(8,128)S(1)}, f32[128,64]{0,1:T(8,128)}, u32[]{:S(2)}) copy-start(f32[128,64]{0,1:T(8,128)} %param.20) | copy-start | bytes 98308
  46.6 4.8 %copy-start.14 = (s32[128,1]{0,1:T(1,128)S(1)}, s32[128,1]{0,1:T(1,128)}, u32[]{:S(2)}) copy-start(s32[128,1]{0,1:T(1,128)} %param.29) | copy-start | bytes 1540
  46.6 33.1 %copy-start = (bf16[128,128]{1,0:T(8,128)(2,1)S(1)}, bf16[128,128]{1,0:T(8,128)(2,1)}, u32[]{:S(2)}) copy-start(bf16[128,128]{1,0:T(8,128)(2,1)} %c_ref.3) | copy-start | bytes 98308
  46.6 33.1 %copy-start.3 = (f32[4,4096]{1,0:T(4,128)S(1)}, f32[4,4096]{1,0:T(4,128)}, u32[]{:S(2)}) copy-start(f32[4,4096]{1,0:T(4,128)} %conv_ref.1) | copy-start | bytes 196612
  46.6 33.1 %copy-start.4 = (bf16[128,128]{1,0:T(8,128)(2,1)S(1)}, bf16[128,128]{1,0:T(8,128)(2,1)}, u32[]{:S(2)}) copy-start(bf16[128,128]{1,0:T(8,128)(2,1)} %b_ref.1) | copy-start | bytes 98308
  46.6 33.1 %copy-start.5 = (f32[64]{0:T(128)S(1)}, f32[64]{0:T(128)}, u32[]{:S(2)}) copy-start(f32[64]{0:T(128)} %param.21) | copy-start | bytes 772
  46.6 33.0 %all-to-all-start.1 = ((bf16[4,8,144,128]{3,2,1,0:T(8,128)(2,1)}), bf16[4,8,144,128]{3,2,1,0:T(8,128)(2,1)S(1)}, u32[]{:S(2)}, u32[]{:S(2)}) async-start(bf16[4,8,144,128]{3,2,1,0:T(8,128)(2,1)} %broadcast_select_fusion), calls=%async_computation.1 | async-start | bytes 2359296 | tf_op jit(solution)/shard_map/all_to_all | solution.py:471
  79.8 1.2 copy-start.1
  81.0 1.2 copy-start.2
  99.6 47.7 %all-to-all-start.2 = ((bf16[16,48,1024]{2,1,0:T(8,128)(2,1)}), bf16[16,48,1024]{2,1,0:T(8,128)(2,1)S(1)}, u32[]{:S(2)}, u32[]{:S(2)}) async-start(bf16[16,48,1024]{2,1,0:T(8,128)(2,1)} %bitcast.12), calls=%async_computation.2 | async-start | bytes 3145728 | tf_op jit(solution)/shard_map/all_to_all | solution.py:511
  164.4 9.1 %copy-start.9 = (bf16[8,144,128]{2,1,0:T(8,128)(2,1)S(1)}, bf16[8,144,128]{2,1,0:T(8,128)(2,1)}, u32[]{:S(2)}) copy-start(bf16[8,144,128]{2,1,0:T(8,128)(2,1)} %get-tuple-element.18) | copy-start | bytes 884740
  164.4 11.6 %copy-start.8 = (bf16[8,144,128]{2,1,0:T(8,128)(2,1)S(1)}, bf16[8,144,128]{2,1,0:T(8,128)(2,1)}, u32[]{:S(2)}) copy-start(bf16[8,144,128]{2,1,0:T(8,128)(2,1)} %get-tuple-element.19) | copy-start | bytes 884740
  164.4 17.5 %copy-start.7 = (bf16[8,144,128]{2,1,0:T(8,128)(2,1)S(1)}, bf16[8,144,128]{2,1,0:T(8,128)(2,1)}, u32[]{:S(2)}) copy-start(bf16[8,144,128]{2,1,0:T(8,128)(2,1)} %get-tuple-element.20) | copy-start | bytes 884740
  164.4 73.1 %all-to-all-start.3 = ((bf16[16,48,1024]{2,1,0:T(8,128)(2,1)}), bf16[16,48,1024]{2,1,0:T(8,128)(2,1)S(1)}, u32[]{:S(2)}, u32[]{:S(2)}) async-start(bf16[16,48,1024]{2,1,0:T(8,128)(2,1)} %bitcast.18), calls=%async_computation.3 | async-start | bytes 3145728 | tf_op jit(solution)/shard_map/all_to_all | solution.py:529
  173.4 30.8 %collective-permute-start.4 = (bf16[8,144,128]{2,1,0:T(8,128)(2,1)S(1)}, bf16[8,144,128]{2,1,0:T(8,128)(2,1)S(1)}, u32[]{:S(2)}, u32[]{:S(2)}) collective-permute-start(bf16[8,144,128]{2,1,0:T(8,128)(2,1)S(1)} %copy-done.9), channel_id=1, source_target_pairs={{0,16},{16,32},{32,48},{48,0},{1,17},{17,33},{33,49},{49,1},{2,18}... | collective-permute-start | bytes 884744 | tf_op jit(solution)/shard_map/ppermute | solution.py:524
  176.0 28.2 %collective-permute-start.5 = (bf16[8,144,128]{2,1,0:T(8,128)(2,1)S(1)}, bf16[8,144,128]{2,1,0:T(8,128)(2,1)S(1)}, u32[]{:S(2)}, u32[]{:S(2)}) collective-permute-start(bf16[8,144,128]{2,1,0:T(8,128)(2,1)S(1)} %copy-done.8), channel_id=1, source_target_pairs={{0,32},{16,48},{32,0},{48,16},{1,33},{17,49},{33,1},{49,17},{2,34}... | collective-permute-start | bytes 884744 | tf_op jit(solution)/shard_map/ppermute | solution.py:524
  181.9 22.3 %collective-permute-start.6 = (bf16[8,144,128]{2,1,0:T(8,128)(2,1)S(1)}, bf16[8,144,128]{2,1,0:T(8,128)(2,1)S(1)}, u32[]{:S(2)}, u32[]{:S(2)}) collective-permute-start(bf16[8,144,128]{2,1,0:T(8,128)(2,1)S(1)} %copy-done.7), channel_id=1, source_target_pairs={{0,48},{16,0},{32,16},{48,32},{1,49},{17,1},{33,17},{49,33},{2,50}... | collective-permute-start | bytes 884744 | tf_op jit(solution)/shard_map/ppermute | solution.py:524
  205.3 24.0 %copy-start.15 = (f32[128,1]{0,1:T(1,128)S(1)}, f32[128,1]{0,1:T(1,128)}, u32[]{:S(2)}) copy-start(f32[128,1]{0,1:T(1,128)} %param.30) | copy-start | bytes 1540
  205.4 17.4 %collective-permute-start.7 = (bf16[2,144,128]{2,1,0:T(8,128)(2,1)S(1)}, bf16[2,144,128]{2,1,0:T(8,128)(2,1)S(1)}, u32[]{:S(2)}, u32[]{:S(2)}) collective-permute-start(bf16[2,144,128]{2,1,0:T(8,128)(2,1)S(1)} %get-tuple-element.33), channel_id=1, source_target_pairs={{0,64},{64,128},{128,192},{192,256},{256,320},{320,384},{384,448},... | collective-permute-start | bytes 221192 | tf_op jit(solution)/shard_map/ppermute | solution.py:538
  207.8 18.9 %collective-permute-start.8 = (bf16[2,144,128]{2,1,0:T(8,128)(2,1)S(1)}, bf16[2,144,128]{2,1,0:T(8,128)(2,1)S(1)}, u32[]{:S(2)}, u32[]{:S(2)}) collective-permute-start(bf16[2,144,128]{2,1,0:T(8,128)(2,1)S(1)} %get-tuple-element.32), channel_id=1, source_target_pairs={{0,128},{64,192},{128,256},{192,320},{256,384},{320,448},{384,0},{... | collective-permute-start | bytes 221192 | tf_op jit(solution)/shard_map/ppermute | solution.py:538
  210.2 19.3 %collective-permute-start.9 = (bf16[2,144,128]{2,1,0:T(8,128)(2,1)S(1)}, bf16[2,144,128]{2,1,0:T(8,128)(2,1)S(1)}, u32[]{:S(2)}, u32[]{:S(2)}) collective-permute-start(bf16[2,144,128]{2,1,0:T(8,128)(2,1)S(1)} %get-tuple-element.31), channel_id=1, source_target_pairs={{0,192},{64,256},{128,320},{192,384},{256,448},{320,0},{384,64},{4... | collective-permute-start | bytes 221192 | tf_op jit(solution)/shard_map/ppermute | solution.py:538
  212.5 16.9 %collective-permute-start.10 = (bf16[2,144,128]{2,1,0:T(8,128)(2,1)S(1)}, bf16[2,144,128]{2,1,0:T(8,128)(2,1)S(1)}, u32[]{:S(2)}, u32[]{:S(2)}) collective-permute-start(bf16[2,144,128]{2,1,0:T(8,128)(2,1)S(1)} %get-tuple-element.30), channel_id=1, source_target_pairs={{0,256},{64,320},{128,384},{192,448},{256,0},{320,64},{384,128},{4... | collective-permute-start | bytes 221192 | tf_op jit(solution)/shard_map/ppermute | solution.py:538
  219.9 12.5 %collective-permute-start.11 = (bf16[2,144,128]{2,1,0:T(8,128)(2,1)S(1)}, bf16[2,144,128]{2,1,0:T(8,128)(2,1)S(1)}, u32[]{:S(2)}, u32[]{:S(2)}) collective-permute-start(bf16[2,144,128]{2,1,0:T(8,128)(2,1)S(1)} %get-tuple-element.29), channel_id=1, source_target_pairs={{0,320},{64,384},{128,448},{192,0},{256,64},{320,128},{384,192},{4... | collective-permute-start | bytes 221192 | tf_op jit(solution)/shard_map/ppermute | solution.py:538
  222.8 10.7 %collective-permute-start.12 = (bf16[2,144,128]{2,1,0:T(8,128)(2,1)S(1)}, bf16[2,144,128]{2,1,0:T(8,128)(2,1)S(1)}, u32[]{:S(2)}, u32[]{:S(2)}) collective-permute-start(bf16[2,144,128]{2,1,0:T(8,128)(2,1)S(1)} %get-tuple-element.28), channel_id=1, source_target_pairs={{0,384},{64,448},{128,0},{192,64},{256,128},{320,192},{384,256},{4... | collective-permute-start | bytes 221192 | tf_op jit(solution)/shard_map/ppermute | solution.py:538
  226.7 9.2 %collective-permute-start.13 = (bf16[2,144,128]{2,1,0:T(8,128)(2,1)S(1)}, bf16[2,144,128]{2,1,0:T(8,128)(2,1)S(1)}, u32[]{:S(2)}, u32[]{:S(2)}) collective-permute-start(bf16[2,144,128]{2,1,0:T(8,128)(2,1)S(1)} %get-tuple-element.27), channel_id=1, source_target_pairs={{0,448},{64,0},{128,64},{192,128},{256,192},{320,256},{384,320},{4... | collective-permute-start | bytes 221192 | tf_op jit(solution)/shard_map/ppermute | solution.py:538
Sparse Core Ops, SparseCore 0:
  10.1 141.0 all-gather.1

commit v7 on v6

--- a/solution.py
+++ b/solution.py
@@ -107,9 +107,8 @@
         0,
     ).astype(jnp.bfloat16)
     for k in range(places):
-        slot = lax.rem(k - row_ref[1] + places, places)
-        sent_ref[slot, 0, :lanes] = state_grad[k * lanes : (k + 1) * lanes]
-        sent_ref[slot, 0, lanes:] = taps_grad[:, k * lanes : (k + 1) * lanes]
+        sent_ref[k, 0, :lanes] = state_grad[k * lanes : (k + 1) * lanes]
+        sent_ref[k, 0, lanes:] = taps_grad[:, k * lanes : (k + 1) * lanes]
 
 
 def mixer_base(
@@ -343,31 +342,30 @@
     )(spot, gain, returned)
 
 
-def presum_kernel(members_ref, *refs):
-    pieces, (out_ref, total_ref) = refs[:-2], refs[-2:]
+def presum_kernel(members_ref, column_ref, out_ref, total_ref):
     total_ref[...] = jnp.zeros_like(total_ref)
-    for k, piece in enumerate(pieces):
-        total_ref[members_ref[k]] += piece[0].astype(jnp.float32)
+    for k in range(column_ref.shape[0]):
+        total_ref[members_ref[k]] += column_ref[k, 0].astype(jnp.float32)
     out_ref[0] = total_ref[...].astype(jnp.bfloat16)
 
 
-def presum(members, pieces, prompts):
-    size_y, rows, lanes = pieces[0].shape
+def presum(members, column, prompts):
+    size_x, size_y, rows, lanes = column.shape
     smem = pl.BlockSpec(memory_space=pltpu.SMEM)
     return pl.pallas_call(
         presum_kernel,
         grid=(size_y,),
-        in_specs=[smem] + [pl.BlockSpec((1, rows, lanes), lambda i: (i, 0, 0))] * len(pieces),
+        in_specs=[smem, pl.BlockSpec((size_x, 1, rows, lanes), lambda i: (0, i, 0, 0))],
         out_specs=pl.BlockSpec((1, prompts, rows, lanes), lambda i: (i, 0, 0, 0)),
         out_shape=jax.ShapeDtypeStruct((size_y, prompts, rows, lanes), jnp.bfloat16),
         scratch_shapes=[pltpu.VMEM((prompts, rows, lanes), jnp.float32)],
         compiler_params=pltpu.CompilerParams(vmem_limit_bytes=16 * 1024 * 1024),
         cost_estimate=pl.CostEstimate(
-            flops=len(pieces) * size_y * rows * lanes,
-            bytes_accessed=3 * len(pieces) * size_y * rows * lanes,
+            flops=size_x * size_y * rows * lanes,
+            bytes_accessed=3 * size_x * size_y * rows * lanes,
             transcendentals=0,
         ),
-    )(members, *pieces)
+    )(members, column)
 
 
 def collect_kernel(*refs):
@@ -444,7 +442,7 @@
     size_y = lax.axis_size("y")
     x_axes = ("xh", "xl")
     x_index = lax.axis_index(x_axes).astype(jnp.int32)
-    place_here = jnp.stack([lax.axis_index("y").astype(jnp.int32), x_index])
+    row = lax.axis_index("y").astype(jnp.int32)[None]
 
     own_taps = jnp.transpose(
         prompt_taps.reshape(prompts, own_heads, taps_n, head_size), (0, 2, 1, 3)
@@ -484,7 +482,7 @@
     step_size = jax.nn.softplus(step_raw)
     base, outgoing_grad, grow = mixer_base(
         lengths,
-        place_here,
+        row,
         ssm_input,
         prior,
         conv_weight,
@@ -516,16 +514,12 @@
         tiled=True,
         axis_index_groups=neighbours(size_x, size_z),
     )
+    arrived, outgoing_grad = lax.optimization_barrier((arrived, outgoing_grad))
+    column_grad = lax.all_to_all(outgoing_grad, x_axes, 0, 0, tiled=True)
     expert_rows = unpack(arrived.reshape(packed_rows, width), slots, lines)
-    weights, *leaving = lax.optimization_barrier(
-        (weights, *(outgoing_grad[d] for d in range(size_x)))
-    )
-    column_grad = [leaving[0]] + [
-        lax.ppermute(leaving[d], x_axes, [(i, (i + d) % size_x) for i in range(size_x)])
-        for d in range(1, size_x)
-    ]
     produced = expert_apply(expert_rows, weights, slots, lines)
-    row_grad = presum(behind, column_grad, prompts)
+    produced, column_grad = lax.optimization_barrier((produced, column_grad))
+    row_grad = presum(row_members, column_grad, prompts)
     returned = lax.all_to_all(
         produced.reshape(lines, GROUPS * slots, width),
         LINE,

time: 249 us -> 230 us (0.924)
  waiting for transfers between devices: 95.2 us -> 46.9 us
  blocking collectives: 0 us -> 46.2 us
  starting transfers between devices: 86.8 us -> 71.4 us
    all_to_all x0 -> x1, blocking collectives: none -> 46.2 us  [shards(): lax.all_to_all(outgoing.reshape(lines, GROUPS * slots, width), LINE, 0, 0...]
    all_to_all x1, waiting for transfers between devices: 35.6 us -> 0.01 us  [shards(): column_grad = lax.all_to_all(outgoing_grad, x_axes, 0, 0, tiled=True)]
    ppermute x3 -> x0, waiting for transfers between devices: 19.8 us -> none  [shards(): lax.ppermute(leaving[d], x_axes, [(i, (i + d) % size_x) for i in range(si...]
    ppermute x3 -> x0, starting transfers between devices: 11 us -> none  [shards(): lax.ppermute(leaving[d], x_axes, [(i, (i + d) % size_x) for i in range(si...]
    all_to_all x1, starting transfers between devices: 11.1 us -> 3.53 us  [shards(): column_grad = lax.all_to_all(outgoing_grad, x_axes, 0, 0, tiled=True)]
    all_to_all x1, waiting for transfers between devices: 0.01 us -> 3.95 us  [shards(): lax.all_to_all(produced.reshape(lines, GROUPS * slots, width), LINE, 0, 0...]
    all_gather x1, waiting for transfers between devices: 1.91 us -> 4.88 us  [shards(): weights = lax.all_gather(swapped, ('y', 'xl', 'c'), axis=1, tiled=True)]
  transfers between devices with their start and end apart: 19 -> 16, of which waited for: 9 -> 6; matrix products, arithmetic and copies ran while one was open for 3% -> 3% of each run, Pallas kernels for 9% -> 14%
where the time goes in v7:
time: 230 us; the launch traced here: 229 us
  starting transfers between devices  71.4 us (31%)
  waiting for transfers between devices  46.9 us (20%)
  blocking collectives  46.2 us (20%)
  Pallas kernels  35.5 us (15%)
  between operations  15.8 us (7%)
  local copies, waits for them, and re-layouts  8.45 us (4%)
  other arithmetic  5.03 us (2%)
    all_to_all x1, blocking collectives, shards(): lax.all_to_all(outgoing.reshape(lines, GROUPS * slots, width), LINE, 0, 0...  46.2 us
    all_to_all x1, waiting for transfers between devices, shards(): lax.all_to_all(jnp.where((row_members == 1)[:, None, None, None], column_...  27.7 us
    ppermute x7, starting transfers between devices, shards(): lax.ppermute(row_grad[d], 'y', [(i, (i + d) % size_y) for i in range(size...  24.6 us
    ppermute x3, starting transfers between devices, shards(): lax.ppermute(group_index, x_axes, [(i, (i + d) % size_x) for i in range(s...  20.1 us
    pallas_call x1, Pallas kernels, expert_apply(): pl.pallas_call(functools.partial(expert_kernel, slots, sources), grid=(un...  13.1 us
    all_to_all x1, starting transfers between devices, shards(): lax.all_to_all(produced.reshape(lines, GROUPS * slots, width), LINE, 0, 0...  10.2 us
    pallas_call x1, Pallas kernels, mixer_base(): pl.pallas_call(functools.partial(mixer_kernel, head_size), grid_spec=pltp...  9.91 us
    all_to_all x1, starting transfers between devices, shards(): lax.all_to_all(jnp.broadcast_to(held[None], (size_y,) + held.shape), 'y',...  8.62 us
  transfers between devices with their start and end apart: 16, of which 6 were waited for; matrix products, arithmetic and copies ran while one was open for 3% of the time, Pallas kernels for 14%

profile of v7, /device:TPU:56, one launch (start us, length us, event | category | flops | bytes accessed | tf_op | source)
XLA Modules:
  0.0 229.3 jit_solution(5873505826850233485)
XLA Ops:
  7.2 0.0 all-gather.2.cloned.1.call-start
  7.2 1.2 pad_maximum_fusion
  8.4 0.7 collective-permute-start.3
  9.1 0.8 copy-done.9
  10.0 0.0 all-gather.2.cloned.1.call-update
  10.0 0.1 reshape.175
  10.1 0.1 reshape.184
  10.2 0.1 pad.7.clone
  10.3 0.1 maximum_maximum_fusion
  10.4 0.9 broadcast_in_dim.71
  11.3 8.6 %all-to-all-start = ((bf16[8,2,144,128]{3,2,1,0:T(8,128)(2,1)}), bf16[8,2,144,128]{3,2,1,0:T(8,128)(2,1)S(1)}, u32[]{:S(2)}, u32[]{:S(2)}) async-start(bf16[8,2,144,128]{3,2,1,0:T(8,128)(2,1)} %broadcast_in_dim.71), calls=%async_computation | async-start | bytes 1179648 | tf_op jit(solution)/shard_map/all_to_all | solution.py:458
  19.9 1.9 collective-permute-start
  21.8 16.1 %collective-permute-start.1 = (s32[1]{0:T(128)}, s32[1]{0:T(128)}, u32[]{:S(2)}, u32[]{:S(2)}) collective-permute-start(s32[1]{0:T(128)} %param.26), channel_id=1, source_target_pairs={{0,32},{16,48},{32,0},{48,16},{1,33},{17,49},{33,1},{49,17},{2,34}... | collective-permute-start | bytes 20 | tf_op jit(solution)/shard_map/ppermute | solution.py:462
  37.9 2.1 collective-permute-start.2
  40.7 0.0 collective-permute-done.1
  40.7 2.7 %collective-permute-done.2 = s32[1]{0:T(128)} collective-permute-done((s32[1]{0:T(128)}, s32[1]{0:T(128)}, u32[]{:S(2)}, u32[]{:S(2)}) %collective-permute-start.2) | collective-permute-done | bytes 36 | tf_op jit(solution)/shard_map/ppermute | solution.py:462
  43.4 2.1 pad_add_fusion
  45.5 0.2 select_reduce_fusion.members_ref
  45.7 0.0 all-to-all-done
  45.7 1.2 broadcast_select_fusion
  47.0 0.0 copy-start.4
  47.0 0.0 copy-start.6
  47.0 0.0 copy-start.7
  47.0 0.0 copy-start.8
  47.0 3.7 %all-to-all-start.1 = ((bf16[4,8,144,128]{3,2,1,0:T(8,128)(2,1)}), bf16[4,8,144,128]{3,2,1,0:T(8,128)(2,1)S(1)}, u32[]{:S(2)}, u32[]{:S(2)}) async-start(bf16[4,8,144,128]{3,2,1,0:T(8,128)(2,1)} %broadcast_select_fusion), calls=%async_computation.1 | async-start | bytes 2359296 | tf_op jit(solution)/shard_map/all_to_all | solution.py:469
  51.4 0.1 copy.104
  51.5 0.1 broadcast_in_dim.76
  51.6 0.1 broadcast_in_dim_reshape.3.skip_ref
  51.7 0.1 convert_reduce_fusion
  51.8 27.7 %all-to-all-done.1.state_ref = bf16[4,8,144,128]{3,2,1,0:T(8,128)(2,1)S(1)} async-done(((bf16[4,8,144,128]{3,2,1,0:T(8,128)(2,1)}), bf16[4,8,144,128]{3,2,1,0:T(8,128)(2,1)S(1)}, u32[]{:S(2)}, u32[]{:S(2)}) %all-to-all-start.1) | async-done | bytes 1179680 | tf_op jit(solution)/shard_map/all_to_all | solution.py:469
  79.7 0.0 copy-start.5
  79.7 1.2 copy-done.5
  80.9 9.9 %shard_map.184 = (f32[128,4096]{1,0:T(8,128)S(1)}, bf16[4,8,144,128]{3,2,1,0:T(8,128)(2,1)S(1)}, f32[128,64]{1,0:T(8,128)S(1)}) custom-call(s32[1]{0:T(128)S(6)} %copy.117.length_ref, s32[1]{0:T(128)} %bitcast.2.row_ref, bf16[128,4096]{1,0:T(8,128)(2,1)S(1)} %copy-done.4, f32[8,4096]{1,0:T(8,128)S(1)} %pad_convert_fusion.prior_ref, f32[4,4096]{1,0:T(4,128)S(1)} %copy-done.6, ...), custom_call_target="tpu_custom_call" | custom-call | flops 1342177280 | bytes 5242880 | tf_op jit(solution)/shard_map/pallas_call | solution.py:125
  90.8 1.0 copy-done.2
  91.8 5.7 %shard_map.185 = bf16[768,1024]{1,0:T(8,128)(2,1)S(1)} custom-call(s32[1]{0:T(128)S(6)} %copy.117.length_ref, f32[128,4096]{1,0:T(8,128)S(1)} %get-tuple-element.12.base_ref, bf16[4,8,144,128]{3,2,1,0:T(8,128)(2,1)S(1)} %all-to-all-done.1.state_ref, bf16[128,128]{1,0:T(8,128)(2,1)S(1)} %copy-done.3, f32[128,64]{1,0:T(8,128)S(1)} %get-tuple-element.13.grow_ref, ...), custom_call_target="tpu_custom_call" | custom-call | flops 939524096 | bytes 4718592 | tf_op jit(solution)/shard_map/pallas_call | solution.py:208
  97.5 46.2 %all_to_all.25 = bf16[16,48,1024]{2,1,0:T(8,128)(2,1)S(1)} all-to-all(bf16[16,48,1024]{2,1,0:T(8,128)(2,1)S(1)} %bitcast.53), channel_id=1, replica_groups={{0,2,4,6,8,10,12,14,48,50,52,54,56,58,60,62},{16,18,20,22,24,26,28,30,3..., dimensions={0} | all-to-all | bytes 3145728 | tf_op jit(solution)/shard_map/all_to_all | solution.py:509
  143.7 3.5 %all-to-all-start.3 = ((bf16[4,8,144,128]{3,2,1,0:T(8,128)(2,1)}), bf16[4,8,144,128]{3,2,1,0:T(8,128)(2,1)S(1)}, u32[]{:S(2)}, u32[]{:S(2)}) async-start(bf16[4,8,144,128]{3,2,1,0:T(8,128)(2,1)} %copy-done.2), calls=%async_computation.3 | async-start | bytes 2359296 | tf_op jit(solution)/shard_map/all_to_all | solution.py:518
  147.2 2.1 shard_map.186.rows_ref
  149.3 1.1 copy-done
  150.5 4.9 %all-gather.2.cloned.1.call-done.weight_ref = bf16[3,768,4096]{2,1,0:T(8,128)(2,1)} async-done(((bf16[3,24,4096]{2,1,0:T(8,128)(2,1)}), bf16[3,768,4096]{2,1,0:T(8,128)(2,1)}) %all-gather.2.cloned.1.call-update) | async-done | bytes 18874384 | tf_op jit(solution)/shard_map/all_gather | solution.py:440
  155.3 1.4 copy-done.1
  156.7 13.1 %shard_map.187 = bf16[768,1024]{1,0:T(8,128)(2,1)} custom-call(bf16[192,4096]{1,0:T(8,128)(2,1)S(1)} %copy-done.1, bf16[3,768,4096]{2,1,0:T(8,128)(2,1)} %all-gather.2.cloned.1.call-done.weight_ref), custom_call_target="tpu_custom_call" | custom-call | flops 3623878656 | bytes 22020096 | tf_op jit(solution)/shard_map/pallas_call | solution.py:299
  169.9 10.2 %all-to-all-start.4 = ((bf16[16,48,1024]{2,1,0:T(8,128)(2,1)}), bf16[16,48,1024]{2,1,0:T(8,128)(2,1)S(1)}, u32[]{:S(2)}, u32[]{:S(2)}) async-start(bf16[16,48,1024]{2,1,0:T(8,128)(2,1)} %bitcast.13), calls=%async_computation.4 | async-start | bytes 3145728 | tf_op jit(solution)/shard_map/all_to_all | solution.py:523
  180.1 1.2 shard_map.189
  181.3 0.0 copy-start.15
  181.4 1.9 collective-permute-start.10
  183.3 5.1 %collective-permute-start.4 = (bf16[2,144,128]{2,1,0:T(8,128)(2,1)S(1)}, bf16[2,144,128]{2,1,0:T(8,128)(2,1)S(1)}, u32[]{:S(2)}, u32[]{:S(2)}) collective-permute-start(bf16[2,144,128]{2,1,0:T(8,128)(2,1)S(1)} %get-tuple-element.27), channel_id=1, source_target_pairs={{0,64},{64,128},{128,192},{192,256},{256,320},{320,384},{384,448},... | collective-permute-start | bytes 221192 | tf_op jit(solution)/shard_map/ppermute | solution.py:532
  188.4 0.1 copy.93
  188.5 0.1 copy.100
  188.7 0.1 copy.96
  188.8 1.9 collective-permute-start.5
  190.7 1.9 collective-permute-start.6
  192.7 7.8 %collective-permute-start.7 = (bf16[2,144,128]{2,1,0:T(8,128)(2,1)S(1)}, bf16[2,144,128]{2,1,0:T(8,128)(2,1)S(1)}, u32[]{:S(2)}, u32[]{:S(2)}) collective-permute-start(bf16[2,144,128]{2,1,0:T(8,128)(2,1)S(1)} %get-tuple-element.24), channel_id=1, source_target_pairs={{0,256},{64,320},{128,384},{192,448},{256,0},{320,64},{384,128},{4... | collective-permute-start | bytes 221192 | tf_op jit(solution)/shard_map/ppermute | solution.py:532
  200.5 1.9 collective-permute-start.8
  202.4 3.9 %collective-permute-start.9 = (bf16[2,144,128]{2,1,0:T(8,128)(2,1)S(1)}, bf16[2,144,128]{2,1,0:T(8,128)(2,1)S(1)}, u32[]{:S(2)}, u32[]{:S(2)}) collective-permute-start(bf16[2,144,128]{2,1,0:T(8,128)(2,1)S(1)} %get-tuple-element.22), channel_id=1, source_target_pairs={{0,384},{64,448},{128,0},{192,64},{256,128},{320,192},{384,256},{4... | collective-permute-start | bytes 221192 | tf_op jit(solution)/shard_map/ppermute | solution.py:532
  206.4 0.1 fusion.3.spot_ref
  206.5 0.1 copy.109.gain_ref
  206.6 6.2 %collective-permute-done.8.refs_5_ = bf16[2,144,128]{2,1,0:T(8,128)(2,1)S(1)} collective-permute-done((bf16[2,144,128]{2,1,0:T(8,128)(2,1)S(1)}, bf16[2,144,128]{2,1,0:T(8,128)(2,1)S(1)}, u32[]{:S(2)}, u32[]{:S(2)}) %collective-permute-start.8) | collective-permute-done | bytes 73760 | tf_op jit(solution)/shard_map/ppermute | solution.py:532
  212.8 1.4 collective-permute-done.9.refs_6_
  214.3 0.7 shard_map.190
  215.0 0.1 reshape.182
  215.1 0.7 reshape.183
  215.8 4.0 %all-to-all-done.4 = bf16[16,48,1024]{2,1,0:T(8,128)(2,1)S(1)} async-done(((bf16[16,48,1024]{2,1,0:T(8,128)(2,1)}), bf16[16,48,1024]{2,1,0:T(8,128)(2,1)S(1)}, u32[]{:S(2)}, u32[]{:S(2)}) %all-to-all-start.4) | async-done | bytes 1572896 | tf_op jit(solution)/shard_map/all_to_all | solution.py:523
  219.7 2.8 %shard_map.188 = bf16[128,4096]{1,0:T(8,128)(2,1)} custom-call(s32[128,1]{1,0:T(8,128)S(1)} %fusion.3.spot_ref, f32[128,1]{1,0:T(8,128)S(1)} %copy.109.gain_ref, bf16[768,1024]{1,0:T(8,128)(2,1)S(1)} %bitcast.54), custom_call_target="tpu_custom_call" | custom-call | flops 805306368 | bytes 2621440 | tf_op jit(solution)/shard_map/pallas_call | solution.py:330
  (45 shorter events, 0.3 us)
Async XLA Ops:
  7.2 2.8 %copy-start.12 = (bf16[2,2,192]{2,1,0:T(2,128)(2,1)S(1)}, bf16[2,2,192]{2,1,0:T(2,128)(2,1)}, u32[]{:S(2)}) copy-start(bf16[2,2,192]{2,1,0:T(2,128)(2,1)} %param.25) | copy-start | bytes 4612
  7.2 3.1 %copy-start.10 = (bf16[2,2,64,128]{3,2,1,0:T(8,128)(2,1)S(1)}, bf16[2,2,64,128]{3,2,1,0:T(8,128)(2,1)}, u32[]{:S(2)}) copy-start(bf16[2,2,64,128]{3,2,1,0:T(8,128)(2,1)} %param.24) | copy-start | bytes 196612
  7.2 148.2 %all-gather.2.cloned.1.call-start = ((), (), s32[]{:S(2)}) async-start(), calls=%async_computation.5 | async-start | bytes 19464192 | tf_op jit(solution)/shard_map/all_gather | solution.py:440
  8.4 0.7 collective-permute-start.3
  9.1 0.8 copy-start.9
  11.3 34.4 %all-to-all-start = ((bf16[8,2,144,128]{3,2,1,0:T(8,128)(2,1)}), bf16[8,2,144,128]{3,2,1,0:T(8,128)(2,1)S(1)}, u32[]{:S(2)}, u32[]{:S(2)}) async-start(bf16[8,2,144,128]{3,2,1,0:T(8,128)(2,1)} %broadcast_in_dim.71), calls=%async_computation | async-start | bytes 1179648 | tf_op jit(solution)/shard_map/all_to_all | solution.py:458
  19.9 20.8 %collective-permute-start = (s32[1]{0:T(128)}, s32[1]{0:T(128)}, u32[]{:S(2)}, u32[]{:S(2)}) collective-permute-start(s32[1]{0:T(128)} %param.26), channel_id=1, source_target_pairs={{0,16},{16,32},{32,48},{48,0},{1,17},{17,33},{33,49},{49,1},{2,18}... | collective-permute-start | bytes 20 | tf_op jit(solution)/shard_map/ppermute | solution.py:462
  21.8 18.9 %collective-permute-start.1 = (s32[1]{0:T(128)}, s32[1]{0:T(128)}, u32[]{:S(2)}, u32[]{:S(2)}) collective-permute-start(s32[1]{0:T(128)} %param.26), channel_id=1, source_target_pairs={{0,32},{16,48},{32,0},{48,16},{1,33},{17,49},{33,1},{49,17},{2,34}... | collective-permute-start | bytes 20 | tf_op jit(solution)/shard_map/ppermute | solution.py:462
  37.9 5.5 %collective-permute-start.2 = (s32[1]{0:T(128)}, s32[1]{0:T(128)}, u32[]{:S(2)}, u32[]{:S(2)}) collective-permute-start(s32[1]{0:T(128)} %param.26), channel_id=1, source_target_pairs={{0,48},{16,0},{32,16},{48,32},{1,49},{17,1},{33,17},{49,33},{2,50}... | collective-permute-start | bytes 20 | tf_op jit(solution)/shard_map/ppermute | solution.py:462
  46.9 4.4 %copy-start.11 = (f32[128,64]{0,1:T(8,128)S(1)}, f32[128,64]{0,1:T(8,128)}, u32[]{:S(2)}) copy-start(f32[128,64]{0,1:T(8,128)} %param.20) | copy-start | bytes 98308
  46.9 4.5 %copy-start.13 = (f32[64]{0:T(128)S(1)}, f32[64]{0:T(128)}, u32[]{:S(2)}) copy-start(f32[64]{0:T(128)} %param.22) | copy-start | bytes 772
  46.9 4.7 %copy-start.14 = (s32[128,1]{0,1:T(1,128)S(1)}, s32[128,1]{0,1:T(1,128)}, u32[]{:S(2)}) copy-start(s32[128,1]{0,1:T(1,128)} %param.29) | copy-start | bytes 1540
  46.9 32.7 %copy-start.3 = (bf16[128,128]{1,0:T(8,128)(2,1)S(1)}, bf16[128,128]{1,0:T(8,128)(2,1)}, u32[]{:S(2)}) copy-start(bf16[128,128]{1,0:T(8,128)(2,1)} %c_ref.3) | copy-start | bytes 98308
  47.0 32.7 %copy-start.4 = (bf16[128,4096]{1,0:T(8,128)(2,1)S(1)}, bf16[128,4096]{1,0:T(8,128)(2,1)}, u32[]{:S(2)}) copy-start(bf16[128,4096]{1,0:T(8,128)(2,1)} %x_ref.1) | copy-start | bytes 3145732
  47.0 32.7 %copy-start.6 = (f32[4,4096]{1,0:T(4,128)S(1)}, f32[4,4096]{1,0:T(4,128)}, u32[]{:S(2)}) copy-start(f32[4,4096]{1,0:T(4,128)} %conv_ref.1) | copy-start | bytes 196612
  47.0 32.7 %copy-start.7 = (bf16[128,128]{1,0:T(8,128)(2,1)S(1)}, bf16[128,128]{1,0:T(8,128)(2,1)}, u32[]{:S(2)}) copy-start(bf16[128,128]{1,0:T(8,128)(2,1)} %b_ref.1) | copy-start | bytes 98308
  47.0 32.7 %copy-start.8 = (f32[64]{0:T(128)S(1)}, f32[64]{0:T(128)}, u32[]{:S(2)}) copy-start(f32[64]{0:T(128)} %param.21) | copy-start | bytes 772
  47.0 32.5 %all-to-all-start.1 = ((bf16[4,8,144,128]{3,2,1,0:T(8,128)(2,1)}), bf16[4,8,144,128]{3,2,1,0:T(8,128)(2,1)S(1)}, u32[]{:S(2)}, u32[]{:S(2)}) async-start(bf16[4,8,144,128]{3,2,1,0:T(8,128)(2,1)} %broadcast_select_fusion), calls=%async_computation.1 | async-start | bytes 2359296 | tf_op jit(solution)/shard_map/all_to_all | solution.py:469
  79.7 1.2 copy-start.5
  90.8 1.0 copy-start.2
  143.7 26.2 %all-to-all-start.3 = ((bf16[4,8,144,128]{3,2,1,0:T(8,128)(2,1)}), bf16[4,8,144,128]{3,2,1,0:T(8,128)(2,1)S(1)}, u32[]{:S(2)}, u32[]{:S(2)}) async-start(bf16[4,8,144,128]{3,2,1,0:T(8,128)(2,1)} %copy-done.2), calls=%async_computation.3 | async-start | bytes 2359296 | tf_op jit(solution)/shard_map/all_to_all | solution.py:518
  149.3 1.1 copy-start
  155.3 1.4 copy-start.1
  169.9 49.8 %all-to-all-start.4 = ((bf16[16,48,1024]{2,1,0:T(8,128)(2,1)}), bf16[16,48,1024]{2,1,0:T(8,128)(2,1)S(1)}, u32[]{:S(2)}, u32[]{:S(2)}) async-start(bf16[16,48,1024]{2,1,0:T(8,128)(2,1)} %bitcast.13), calls=%async_computation.4 | async-start | bytes 3145728 | tf_op jit(solution)/shard_map/all_to_all | solution.py:523
  181.3 25.2 %copy-start.15 = (f32[128,1]{0,1:T(1,128)S(1)}, f32[128,1]{0,1:T(1,128)}, u32[]{:S(2)}) copy-start(f32[128,1]{0,1:T(1,128)} %param.30) | copy-start | bytes 1540
  181.4 19.1 %collective-permute-start.10 = (bf16[2,144,128]{2,1,0:T(8,128)(2,1)S(1)}, bf16[2,144,128]{2,1,0:T(8,128)(2,1)S(1)}, u32[]{:S(2)}, u32[]{:S(2)}) collective-permute-start(bf16[2,144,128]{2,1,0:T(8,128)(2,1)S(1)} %get-tuple-element.21), channel_id=1, source_target_pairs={{0,448},{64,0},{128,64},{192,128},{256,192},{320,256},{384,320},{4... | collective-permute-start | bytes 221192 | tf_op jit(solution)/shard_map/ppermute | solution.py:532
  183.3 19.1 %collective-permute-start.4 = (bf16[2,144,128]{2,1,0:T(8,128)(2,1)S(1)}, bf16[2,144,128]{2,1,0:T(8,128)(2,1)S(1)}, u32[]{:S(2)}, u32[]{:S(2)}) collective-permute-start(bf16[2,144,128]{2,1,0:T(8,128)(2,1)S(1)} %get-tuple-element.27), channel_id=1, source_target_pairs={{0,64},{64,128},{128,192},{192,256},{256,320},{320,384},{384,448},... | collective-permute-start | bytes 221192 | tf_op jit(solution)/shard_map/ppermute | solution.py:532
  188.8 17.8 %collective-permute-start.5 = (bf16[2,144,128]{2,1,0:T(8,128)(2,1)S(1)}, bf16[2,144,128]{2,1,0:T(8,128)(2,1)S(1)}, u32[]{:S(2)}, u32[]{:S(2)}) collective-permute-start(bf16[2,144,128]{2,1,0:T(8,128)(2,1)S(1)} %get-tuple-element.26), channel_id=1, source_target_pairs={{0,128},{64,192},{128,256},{192,320},{256,384},{320,448},{384,0},{... | collective-permute-start | bytes 221192 | tf_op jit(solution)/shard_map/ppermute | solution.py:532
  190.7 15.9 %collective-permute-start.6 = (bf16[2,144,128]{2,1,0:T(8,128)(2,1)S(1)}, bf16[2,144,128]{2,1,0:T(8,128)(2,1)S(1)}, u32[]{:S(2)}, u32[]{:S(2)}) collective-permute-start(bf16[2,144,128]{2,1,0:T(8,128)(2,1)S(1)} %get-tuple-element.25), channel_id=1, source_target_pairs={{0,192},{64,256},{128,320},{192,384},{256,448},{320,0},{384,64},{4... | collective-permute-start | bytes 221192 | tf_op jit(solution)/shard_map/ppermute | solution.py:532
  192.7 13.9 %collective-permute-start.7 = (bf16[2,144,128]{2,1,0:T(8,128)(2,1)S(1)}, bf16[2,144,128]{2,1,0:T(8,128)(2,1)S(1)}, u32[]{:S(2)}, u32[]{:S(2)}) collective-permute-start(bf16[2,144,128]{2,1,0:T(8,128)(2,1)S(1)} %get-tuple-element.24), channel_id=1, source_target_pairs={{0,256},{64,320},{128,384},{192,448},{256,0},{320,64},{384,128},{4... | collective-permute-start | bytes 221192 | tf_op jit(solution)/shard_map/ppermute | solution.py:532
  200.5 12.3 %collective-permute-start.8 = (bf16[2,144,128]{2,1,0:T(8,128)(2,1)S(1)}, bf16[2,144,128]{2,1,0:T(8,128)(2,1)S(1)}, u32[]{:S(2)}, u32[]{:S(2)}) collective-permute-start(bf16[2,144,128]{2,1,0:T(8,128)(2,1)S(1)} %get-tuple-element.23), channel_id=1, source_target_pairs={{0,320},{64,384},{128,448},{192,0},{256,64},{320,128},{384,192},{4... | collective-permute-start | bytes 221192 | tf_op jit(solution)/shard_map/ppermute | solution.py:532
  202.4 11.8 %collective-permute-start.9 = (bf16[2,144,128]{2,1,0:T(8,128)(2,1)S(1)}, bf16[2,144,128]{2,1,0:T(8,128)(2,1)S(1)}, u32[]{:S(2)}, u32[]{:S(2)}) collective-permute-start(bf16[2,144,128]{2,1,0:T(8,128)(2,1)S(1)} %get-tuple-element.22), channel_id=1, source_target_pairs={{0,384},{64,448},{128,0},{192,64},{256,128},{320,192},{384,256},{4... | collective-permute-start | bytes 221192 | tf_op jit(solution)/shard_map/ppermute | solution.py:532
Sparse Core Ops, SparseCore 0:
  10.1 145.1 all-gather.1

commit v8 on v7

--- a/solution.py
+++ b/solution.py
@@ -158,7 +158,7 @@
             jax.ShapeDtypeStruct(sent, jnp.bfloat16),
             jax.ShapeDtypeStruct((steps_n, heads), jnp.float32),
         ],
-        compiler_params=pltpu.CompilerParams(vmem_limit_bytes=32 * 1024 * 1024),
+        compiler_params=pltpu.CompilerParams(vmem_limit_bytes=58 * 1024 * 1024),
         cost_estimate=pl.CostEstimate(
             flops=20 * steps_n * channels * state_n,
             bytes_accessed=10 * steps_n * channels,
@@ -252,7 +252,7 @@
         in_specs=[pl.BlockSpec((packed, width), lambda g: (0, 0))],
         out_specs=pl.BlockSpec((count, width), lambda g: (0, g)),
         out_shape=jax.ShapeDtypeStruct((count, GROUPS * width), jnp.bfloat16),
-        compiler_params=pltpu.CompilerParams(vmem_limit_bytes=24 * 1024 * 1024),
+        compiler_params=pltpu.CompilerParams(vmem_limit_bytes=58 * 1024 * 1024),
         cost_estimate=pl.CostEstimate(
             flops=2 * GROUPS * count * packed * width,
             bytes_accessed=4 * packed * width,
@@ -306,7 +306,7 @@
         out_specs=pl.BlockSpec((packed, width), lambda i: (0, 0)),
         out_shape=jax.ShapeDtypeStruct((packed, width), jnp.bfloat16),
         scratch_shapes=[pltpu.VMEM((count, channels), jnp.float32)],
-        compiler_params=pltpu.CompilerParams(vmem_limit_bytes=48 * 1024 * 1024),
+        compiler_params=pltpu.CompilerParams(vmem_limit_bytes=58 * 1024 * 1024),
         cost_estimate=pl.CostEstimate(
             flops=6 * count * units * channels,
             bytes_accessed=6 * units * channels + 4 * packed * width,

time: 230 us -> 227 us (0.987)
  waiting for transfers between devices: 46.9 us -> 40.8 us
  Pallas kernels: 35.5 us -> 40.1 us
    all_gather x1, waiting for transfers between devices: 4.88 us -> 0.01 us  [shards(): weights = lax.all_gather(swapped, ('y', 'xl', 'c'), axis=1, tiled=True)]
    pallas_call x1, Pallas kernels: 2.09 us -> 4.52 us  [unpack(): pl.pallas_call(functools.partial(unpack_kernel, slots, sources), grid=(GR...]
    unnamed x35 -> x23, local copies, waits for them, and re-layouts: 5.98 us -> 3.68 us
  transfers between devices with their start and end apart: 16 -> 16, of which waited for: 6 -> 5; matrix products, arithmetic and copies ran while one was open for 3% -> 4% of each run, Pallas kernels for 14% -> 17%
where the time goes in v8:
time: 227 us; the launch traced here: 226 us
  starting transfers between devices  70.4 us (31%)
  blocking collectives  46.2 us (20%)
  waiting for transfers between devices  40.8 us (18%)
  Pallas kernels  40.1 us (18%)
  between operations  15.7 us (7%)
  local copies, waits for them, and re-layouts  6.75 us (3%)
  other arithmetic  6.12 us (3%)
    all_to_all x1, blocking collectives, shards(): lax.all_to_all(outgoing.reshape(lines, GROUPS * slots, width), LINE, 0, 0...  46.2 us
    all_to_all x1, waiting for transfers between devices, shards(): lax.all_to_all(jnp.where((row_members == 1)[:, None, None, None], column_...  26.4 us
    ppermute x7, starting transfers between devices, shards(): lax.ppermute(row_grad[d], 'y', [(i, (i + d) % size_y) for i in range(size...  24.6 us
    ppermute x3, starting transfers between devices, shards(): lax.ppermute(group_index, x_axes, [(i, (i + d) % size_x) for i in range(s...  20.1 us
    pallas_call x1, Pallas kernels, expert_apply(): pl.pallas_call(functools.partial(expert_kernel, slots, sources), grid=(un...  13.6 us
    pallas_call x1, Pallas kernels, mixer_base(): pl.pallas_call(functools.partial(mixer_kernel, head_size), grid_spec=pltp...  11.6 us
    all_to_all x1, starting transfers between devices, shards(): lax.all_to_all(produced.reshape(lines, GROUPS * slots, width), LINE, 0, 0...  9.14 us
    all_to_all x1, starting transfers between devices, shards(): lax.all_to_all(jnp.broadcast_to(held[None], (size_y,) + held.shape), 'y',...  8.62 us
  transfers between devices with their start and end apart: 16, of which 5 were waited for; matrix products, arithmetic and copies ran while one was open for 4% of the time, Pallas kernels for 17%

profile of v8, /device:TPU:56, one launch (start us, length us, event | category | flops | bytes accessed | tf_op | source)
XLA Modules:
  0.0 226.1 jit_solution(16387163126110960786)
XLA Ops:
  7.2 0.0 all-gather.2.cloned.1.call-start
  7.2 1.2 pad_maximum_fusion
  8.4 0.7 collective-permute-start.3
  9.1 0.0 collective-permute-done.3
  9.1 0.8 copy-done.3
  10.0 0.0 all-gather.2.cloned.1.call-update
  10.0 0.1 reshape.175
  10.1 0.1 reshape.184
  10.2 0.1 pad.7.clone
  10.3 0.1 maximum_maximum_fusion
  10.4 0.9 broadcast_in_dim.71
  11.2 8.6 %all-to-all-start = ((bf16[8,2,144,128]{3,2,1,0:T(8,128)(2,1)}), bf16[8,2,144,128]{3,2,1,0:T(8,128)(2,1)S(1)}, u32[]{:S(2)}, u32[]{:S(2)}) async-start(bf16[8,2,144,128]{3,2,1,0:T(8,128)(2,1)} %broadcast_in_dim.71), calls=%async_computation | async-start | bytes 1179648 | tf_op jit(solution)/shard_map/all_to_all | solution.py:458
  19.9 1.9 collective-permute-start
  21.8 16.1 %collective-permute-start.1 = (s32[1]{0:T(128)}, s32[1]{0:T(128)}, u32[]{:S(2)}, u32[]{:S(2)}) collective-permute-start(s32[1]{0:T(128)} %param.26), channel_id=1, source_target_pairs={{0,32},{16,48},{32,0},{48,16},{1,33},{17,49},{33,1},{49,17},{2,34}... | collective-permute-start | bytes 20 | tf_op jit(solution)/shard_map/ppermute | solution.py:462
  37.9 2.1 collective-permute-start.2
  40.7 0.0 collective-permute-done
  40.7 0.0 collective-permute-done.1
  40.7 2.8 %collective-permute-done.2 = s32[1]{0:T(128)} collective-permute-done((s32[1]{0:T(128)}, s32[1]{0:T(128)}, u32[]{:S(2)}, u32[]{:S(2)}) %collective-permute-start.2) | collective-permute-done | bytes 36 | tf_op jit(solution)/shard_map/ppermute | solution.py:462
  43.5 1.9 pad_add_fusion
  45.4 0.2 select_reduce_fusion.members_ref
  45.6 0.0 all-to-all-done
  45.7 1.2 broadcast_select_fusion
  46.9 3.7 %all-to-all-start.1 = ((bf16[4,8,144,128]{3,2,1,0:T(8,128)(2,1)}), bf16[4,8,144,128]{3,2,1,0:T(8,128)(2,1)S(1)}, u32[]{:S(2)}, u32[]{:S(2)}) async-start(bf16[4,8,144,128]{3,2,1,0:T(8,128)(2,1)} %broadcast_select_fusion), calls=%async_computation.1 | async-start | bytes 2359296 | tf_op jit(solution)/shard_map/all_to_all | solution.py:469
  51.2 0.1 copy.104
  51.3 0.1 broadcast_in_dim.76
  51.4 0.7 broadcast_in_dim_reshape.3.skip_ref
  52.1 0.1 convert_reduce_fusion
  52.2 0.7 compare_select_fusion.step_ref
  52.9 26.4 %all-to-all-done.1.state_ref = bf16[4,8,144,128]{3,2,1,0:T(8,128)(2,1)S(1)} async-done(((bf16[4,8,144,128]{3,2,1,0:T(8,128)(2,1)}), bf16[4,8,144,128]{3,2,1,0:T(8,128)(2,1)S(1)}, u32[]{:S(2)}, u32[]{:S(2)}) %all-to-all-start.1) | async-done | bytes 1179680 | tf_op jit(solution)/shard_map/all_to_all | solution.py:469
  79.3 0.7 pad_convert_fusion.prior_ref
  80.0 11.6 %shard_map.184 = (f32[128,4096]{1,0:T(8,128)}, bf16[4,8,144,128]{3,2,1,0:T(8,128)(2,1)}, f32[128,64]{1,0:T(8,128)}) custom-call(s32[1]{0:T(128)S(6)} %copy.117.length_ref, s32[1]{0:T(128)} %bitcast.2.row_ref, bf16[128,4096]{1,0:T(8,128)(2,1)} %x_ref.1, f32[8,4096]{1,0:T(8,128)} %pad_convert_fusion.prior_ref, f32[4,4096]{1,0:T(4,128)} %conv_ref.1, ...), custom_call_target="tpu_custom_call" | custom-call | flops 1342177280 | bytes 5242880 | tf_op jit(solution)/shard_map/pallas_call | solution.py:125
  91.7 1.7 copy-done
  93.4 0.8 copy-done.1
  94.2 5.7 %shard_map.185 = bf16[768,1024]{1,0:T(8,128)(2,1)S(1)} custom-call(s32[1]{0:T(128)S(6)} %copy.117.length_ref, f32[128,4096]{1,0:T(8,128)S(1)} %copy-done, bf16[4,8,144,128]{3,2,1,0:T(8,128)(2,1)S(1)} %all-to-all-done.1.state_ref, bf16[128,128]{1,0:T(8,128)(2,1)S(1)} %copy-done.2, f32[128,64]{1,0:T(8,128)S(1)} %copy-done.1, s32[1,128]{1,0:T(1,128)S(1)} %bitcast_add_fusion.spot_ref), custom_call_target="tpu_custom_call" | custom-call | flops 939524096 | bytes 4718592 | tf_op jit(solution)/shard_map/pallas_call | solution.py:208
  99.9 46.2 %all_to_all.25 = bf16[16,48,1024]{2,1,0:T(8,128)(2,1)} all-to-all(bf16[16,48,1024]{2,1,0:T(8,128)(2,1)S(1)} %bitcast.53), channel_id=1, replica_groups={{0,2,4,6,8,10,12,14,48,50,52,54,56,58,60,62},{16,18,20,22,24,26,28,30,3..., dimensions={0} | all-to-all | bytes 3145728 | tf_op jit(solution)/shard_map/all_to_all | solution.py:509
  146.0 3.5 %all-to-all-start.3 = ((bf16[4,8,144,128]{3,2,1,0:T(8,128)(2,1)}), bf16[4,8,144,128]{3,2,1,0:T(8,128)(2,1)S(1)}, u32[]{:S(2)}, u32[]{:S(2)}) async-start(bf16[4,8,144,128]{3,2,1,0:T(8,128)(2,1)} %get-tuple-element.16), calls=%async_computation.3 | async-start | bytes 2359296 | tf_op jit(solution)/shard_map/all_to_all | solution.py:518
  149.6 4.5 %shard_map.186.rows_ref = bf16[192,4096]{1,0:T(8,128)(2,1)} custom-call(bf16[768,1024]{1,0:T(8,128)(2,1)} %bitcast.56), custom_call_target="tpu_custom_call" | custom-call | flops 1207959552 | bytes 3145728 | tf_op jit(solution)/shard_map/pallas_call | solution.py:249
  154.1 13.6 %shard_map.187 = bf16[768,1024]{1,0:T(8,128)(2,1)} custom-call(bf16[192,4096]{1,0:T(8,128)(2,1)} %shard_map.186.rows_ref, bf16[3,768,4096]{2,1,0:T(8,128)(2,1)} %all-gather.2.cloned.1.call-done.weight_ref), custom_call_target="tpu_custom_call" | custom-call | flops 3623878656 | bytes 22020096 | tf_op jit(solution)/shard_map/pallas_call | solution.py:299
  167.7 0.0 all-to-all-done.3.column_ref
  167.7 9.1 %all-to-all-start.4 = ((bf16[16,48,1024]{2,1,0:T(8,128)(2,1)}), bf16[16,48,1024]{2,1,0:T(8,128)(2,1)S(1)}, u32[]{:S(2)}, u32[]{:S(2)}) async-start(bf16[16,48,1024]{2,1,0:T(8,128)(2,1)} %bitcast.55), calls=%async_computation.4 | async-start | bytes 3145728 | tf_op jit(solution)/shard_map/all_to_all | solution.py:523
  176.9 1.2 shard_map.189
  178.1 0.0 copy-start.9
  178.1 1.9 collective-permute-start.10
  180.1 5.1 %collective-permute-start.4 = (bf16[2,144,128]{2,1,0:T(8,128)(2,1)S(1)}, bf16[2,144,128]{2,1,0:T(8,128)(2,1)S(1)}, u32[]{:S(2)}, u32[]{:S(2)}) collective-permute-start(bf16[2,144,128]{2,1,0:T(8,128)(2,1)S(1)} %get-tuple-element.27), channel_id=1, source_target_pairs={{0,64},{64,128},{128,192},{192,256},{256,320},{320,384},{384,448},... | collective-permute-start | bytes 221192 | tf_op jit(solution)/shard_map/ppermute | solution.py:532
  185.2 0.1 copy.93
  185.3 0.1 copy.100
  185.5 0.1 copy.96
  185.6 1.9 collective-permute-start.5
  187.5 1.9 collective-permute-start.6
  189.4 7.8 %collective-permute-start.7 = (bf16[2,144,128]{2,1,0:T(8,128)(2,1)S(1)}, bf16[2,144,128]{2,1,0:T(8,128)(2,1)S(1)}, u32[]{:S(2)}, u32[]{:S(2)}) collective-permute-start(bf16[2,144,128]{2,1,0:T(8,128)(2,1)S(1)} %get-tuple-element.24), channel_id=1, source_target_pairs={{0,256},{64,320},{128,384},{192,448},{256,0},{320,64},{384,128},{4... | collective-permute-start | bytes 221192 | tf_op jit(solution)/shard_map/ppermute | solution.py:532
  197.3 0.0 collective-permute-done.10.refs_7_
  197.3 1.9 collective-permute-start.8
  199.2 3.9 %collective-permute-start.9 = (bf16[2,144,128]{2,1,0:T(8,128)(2,1)S(1)}, bf16[2,144,128]{2,1,0:T(8,128)(2,1)S(1)}, u32[]{:S(2)}, u32[]{:S(2)}) collective-permute-start(bf16[2,144,128]{2,1,0:T(8,128)(2,1)S(1)} %get-tuple-element.22), channel_id=1, source_target_pairs={{0,384},{64,448},{128,0},{192,64},{256,128},{320,192},{384,256},{4... | collective-permute-start | bytes 221192 | tf_op jit(solution)/shard_map/ppermute | solution.py:532
  203.2 0.1 fusion.3.spot_ref
  203.3 0.1 copy.109.gain_ref
  203.4 0.0 collective-permute-done.5.refs_2_
  203.4 0.0 collective-permute-done.7.refs_4_
  203.4 6.2 %collective-permute-done.8.refs_5_ = bf16[2,144,128]{2,1,0:T(8,128)(2,1)S(1)} collective-permute-done((bf16[2,144,128]{2,1,0:T(8,128)(2,1)S(1)}, bf16[2,144,128]{2,1,0:T(8,128)(2,1)S(1)}, u32[]{:S(2)}, u32[]{:S(2)}) %collective-permute-start.8) | collective-permute-done | bytes 73760 | tf_op jit(solution)/shard_map/ppermute | solution.py:532
  209.6 1.4 collective-permute-done.9.refs_6_
  211.0 0.7 shard_map.190
  211.8 0.1 reshape.182
  211.9 0.7 reshape.183
  212.6 3.9 %all-to-all-done.4 = bf16[16,48,1024]{2,1,0:T(8,128)(2,1)S(1)} async-done(((bf16[16,48,1024]{2,1,0:T(8,128)(2,1)}), bf16[16,48,1024]{2,1,0:T(8,128)(2,1)S(1)}, u32[]{:S(2)}, u32[]{:S(2)}) %all-to-all-start.4) | async-done | bytes 1572896 | tf_op jit(solution)/shard_map/all_to_all | solution.py:523
  216.5 2.8 %shard_map.188 = bf16[128,4096]{1,0:T(8,128)(2,1)} custom-call(s32[128,1]{1,0:T(8,128)S(1)} %fusion.3.spot_ref, f32[128,1]{1,0:T(8,128)S(1)} %copy.109.gain_ref, bf16[768,1024]{1,0:T(8,128)(2,1)S(1)} %bitcast.54), custom_call_target="tpu_custom_call" | custom-call | flops 805306368 | bytes 2621440 | tf_op jit(solution)/shard_map/pallas_call | solution.py:330
  (33 shorter events, 0.2 us)
Async XLA Ops:
  7.2 2.8 %copy-start.6 = (bf16[2,2,192]{2,1,0:T(2,128)(2,1)S(1)}, bf16[2,2,192]{2,1,0:T(2,128)(2,1)}, u32[]{:S(2)}) copy-start(bf16[2,2,192]{2,1,0:T(2,128)(2,1)} %param.25) | copy-start | bytes 4612
  7.2 3.1 %copy-start.4 = (bf16[2,2,64,128]{3,2,1,0:T(8,128)(2,1)S(1)}, bf16[2,2,64,128]{3,2,1,0:T(8,128)(2,1)}, u32[]{:S(2)}) copy-start(bf16[2,2,64,128]{3,2,1,0:T(8,128)(2,1)} %param.24) | copy-start | bytes 196612
  7.2 146.9 %all-gather.2.cloned.1.call-start = ((), (), s32[]{:S(2)}) async-start(), calls=%async_computation.5 | async-start | bytes 19464192 | tf_op jit(solution)/shard_map/all_gather | solution.py:440
  8.4 0.7 collective-permute-start.3
  9.1 0.8 copy-start.3
  11.2 34.4 %all-to-all-start = ((bf16[8,2,144,128]{3,2,1,0:T(8,128)(2,1)}), bf16[8,2,144,128]{3,2,1,0:T(8,128)(2,1)S(1)}, u32[]{:S(2)}, u32[]{:S(2)}) async-start(bf16[8,2,144,128]{3,2,1,0:T(8,128)(2,1)} %broadcast_in_dim.71), calls=%async_computation | async-start | bytes 1179648 | tf_op jit(solution)/shard_map/all_to_all | solution.py:458
  19.9 20.8 %collective-permute-start = (s32[1]{0:T(128)}, s32[1]{0:T(128)}, u32[]{:S(2)}, u32[]{:S(2)}) collective-permute-start(s32[1]{0:T(128)} %param.26), channel_id=1, source_target_pairs={{0,16},{16,32},{32,48},{48,0},{1,17},{17,33},{33,49},{49,1},{2,18}... | collective-permute-start | bytes 20 | tf_op jit(solution)/shard_map/ppermute | solution.py:462
  21.8 18.9 %collective-permute-start.1 = (s32[1]{0:T(128)}, s32[1]{0:T(128)}, u32[]{:S(2)}, u32[]{:S(2)}) collective-permute-start(s32[1]{0:T(128)} %param.26), channel_id=1, source_target_pairs={{0,32},{16,48},{32,0},{48,16},{1,33},{17,49},{33,1},{49,17},{2,34}... | collective-permute-start | bytes 20 | tf_op jit(solution)/shard_map/ppermute | solution.py:462
  37.9 5.7 %collective-permute-start.2 = (s32[1]{0:T(128)}, s32[1]{0:T(128)}, u32[]{:S(2)}, u32[]{:S(2)}) collective-permute-start(s32[1]{0:T(128)} %param.26), channel_id=1, source_target_pairs={{0,48},{16,0},{32,16},{48,32},{1,49},{17,1},{33,17},{49,33},{2,50}... | collective-permute-start | bytes 20 | tf_op jit(solution)/shard_map/ppermute | solution.py:462
  46.9 4.3 %copy-start.5 = (f32[128,64]{0,1:T(8,128)S(1)}, f32[128,64]{0,1:T(8,128)}, u32[]{:S(2)}) copy-start(f32[128,64]{0,1:T(8,128)} %param.20) | copy-start | bytes 98308
  46.9 4.4 %copy-start.7 = (f32[64]{0:T(128)S(1)}, f32[64]{0:T(128)}, u32[]{:S(2)}) copy-start(f32[64]{0:T(128)} %param.22) | copy-start | bytes 772
  46.9 5.2 %copy-start.8 = (s32[128,1]{0,1:T(1,128)S(1)}, s32[128,1]{0,1:T(1,128)}, u32[]{:S(2)}) copy-start(s32[128,1]{0,1:T(1,128)} %param.29) | copy-start | bytes 1540
  46.9 32.4 %all-to-all-start.1 = ((bf16[4,8,144,128]{3,2,1,0:T(8,128)(2,1)}), bf16[4,8,144,128]{3,2,1,0:T(8,128)(2,1)S(1)}, u32[]{:S(2)}, u32[]{:S(2)}) async-start(bf16[4,8,144,128]{3,2,1,0:T(8,128)(2,1)} %broadcast_select_fusion), calls=%async_computation.1 | async-start | bytes 2359296 | tf_op jit(solution)/shard_map/all_to_all | solution.py:469
  80.0 11.7 %copy-start.2 = (bf16[128,128]{1,0:T(8,128)(2,1)S(1)}, bf16[128,128]{1,0:T(8,128)(2,1)}, u32[]{:S(2)}) copy-start(bf16[128,128]{1,0:T(8,128)(2,1)} %c_ref.3) | copy-start | bytes 98308
  91.7 1.7 copy-start
  93.4 0.8 copy-start.1
  146.0 21.7 %all-to-all-start.3 = ((bf16[4,8,144,128]{3,2,1,0:T(8,128)(2,1)}), bf16[4,8,144,128]{3,2,1,0:T(8,128)(2,1)S(1)}, u32[]{:S(2)}, u32[]{:S(2)}) async-start(bf16[4,8,144,128]{3,2,1,0:T(8,128)(2,1)} %get-tuple-element.16), calls=%async_computation.3 | async-start | bytes 2359296 | tf_op jit(solution)/shard_map/all_to_all | solution.py:518
  167.7 48.8 %all-to-all-start.4 = ((bf16[16,48,1024]{2,1,0:T(8,128)(2,1)}), bf16[16,48,1024]{2,1,0:T(8,128)(2,1)S(1)}, u32[]{:S(2)}, u32[]{:S(2)}) async-start(bf16[16,48,1024]{2,1,0:T(8,128)(2,1)} %bitcast.55), calls=%async_computation.4 | async-start | bytes 3145728 | tf_op jit(solution)/shard_map/all_to_all | solution.py:523
  178.1 25.2 %copy-start.9 = (f32[128,1]{0,1:T(1,128)S(1)}, f32[128,1]{0,1:T(1,128)}, u32[]{:S(2)}) copy-start(f32[128,1]{0,1:T(1,128)} %param.30) | copy-start | bytes 1540
  178.1 19.1 %collective-permute-start.10 = (bf16[2,144,128]{2,1,0:T(8,128)(2,1)S(1)}, bf16[2,144,128]{2,1,0:T(8,128)(2,1)S(1)}, u32[]{:S(2)}, u32[]{:S(2)}) collective-permute-start(bf16[2,144,128]{2,1,0:T(8,128)(2,1)S(1)} %get-tuple-element.21), channel_id=1, source_target_pairs={{0,448},{64,0},{128,64},{192,128},{256,192},{320,256},{384,320},{4... | collective-permute-start | bytes 221192 | tf_op jit(solution)/shard_map/ppermute | solution.py:532
  180.1 19.1 %collective-permute-start.4 = (bf16[2,144,128]{2,1,0:T(8,128)(2,1)S(1)}, bf16[2,144,128]{2,1,0:T(8,128)(2,1)S(1)}, u32[]{:S(2)}, u32[]{:S(2)}) collective-permute-start(bf16[2,144,128]{2,1,0:T(8,128)(2,1)S(1)} %get-tuple-element.27), channel_id=1, source_target_pairs={{0,64},{64,128},{128,192},{192,256},{256,320},{320,384},{384,448},... | collective-permute-start | bytes 221192 | tf_op jit(solution)/shard_map/ppermute | solution.py:532
  185.6 17.8 %collective-permute-start.5 = (bf16[2,144,128]{2,1,0:T(8,128)(2,1)S(1)}, bf16[2,144,128]{2,1,0:T(8,128)(2,1)S(1)}, u32[]{:S(2)}, u32[]{:S(2)}) collective-permute-start(bf16[2,144,128]{2,1,0:T(8,128)(2,1)S(1)} %get-tuple-element.26), channel_id=1, source_target_pairs={{0,128},{64,192},{128,256},{192,320},{256,384},{320,448},{384,0},{... | collective-permute-start | bytes 221192 | tf_op jit(solution)/shard_map/ppermute | solution.py:532
  187.5 15.9 %collective-permute-start.6 = (bf16[2,144,128]{2,1,0:T(8,128)(2,1)S(1)}, bf16[2,144,128]{2,1,0:T(8,128)(2,1)S(1)}, u32[]{:S(2)}, u32[]{:S(2)}) collective-permute-start(bf16[2,144,128]{2,1,0:T(8,128)(2,1)S(1)} %get-tuple-element.25), channel_id=1, source_target_pairs={{0,192},{64,256},{128,320},{192,384},{256,448},{320,0},{384,64},{4... | collective-permute-start | bytes 221192 | tf_op jit(solution)/shard_map/ppermute | solution.py:532
  189.4 13.9 %collective-permute-start.7 = (bf16[2,144,128]{2,1,0:T(8,128)(2,1)S(1)}, bf16[2,144,128]{2,1,0:T(8,128)(2,1)S(1)}, u32[]{:S(2)}, u32[]{:S(2)}) collective-permute-start(bf16[2,144,128]{2,1,0:T(8,128)(2,1)S(1)} %get-tuple-element.24), channel_id=1, source_target_pairs={{0,256},{64,320},{128,384},{192,448},{256,0},{320,64},{384,128},{4... | collective-permute-start | bytes 221192 | tf_op jit(solution)/shard_map/ppermute | solution.py:532
  197.3 12.3 %collective-permute-start.8 = (bf16[2,144,128]{2,1,0:T(8,128)(2,1)S(1)}, bf16[2,144,128]{2,1,0:T(8,128)(2,1)S(1)}, u32[]{:S(2)}, u32[]{:S(2)}) collective-permute-start(bf16[2,144,128]{2,1,0:T(8,128)(2,1)S(1)} %get-tuple-element.23), channel_id=1, source_target_pairs={{0,320},{64,384},{128,448},{192,0},{256,64},{320,128},{384,192},{4... | collective-permute-start | bytes 221192 | tf_op jit(solution)/shard_map/ppermute | solution.py:532
  199.2 11.8 %collective-permute-start.9 = (bf16[2,144,128]{2,1,0:T(8,128)(2,1)S(1)}, bf16[2,144,128]{2,1,0:T(8,128)(2,1)S(1)}, u32[]{:S(2)}, u32[]{:S(2)}) collective-permute-start(bf16[2,144,128]{2,1,0:T(8,128)(2,1)S(1)} %get-tuple-element.22), channel_id=1, source_target_pairs={{0,384},{64,448},{128,0},{192,64},{256,128},{320,192},{384,256},{4... | collective-permute-start | bytes 221192 | tf_op jit(solution)/shard_map/ppermute | solution.py:532
Sparse Core Ops, SparseCore 0:
  10.1 143.2 all-gather.1
